TPU v7x, 256 devices: a whole 4x4x8 slice. The times are simulated.
256 devices in a mesh: dp: 8 (over x, core), vocab: 32 (over y, z).
Axes of the slice: x: 4, y: 4, z: 8, core: 2. Of those that a mesh axis runs over, the one named last changes fastest.
Arguments:
- hidden_states: bfloat16 [1024, 5120], P('dp'), may hold values from -70 to 70, as said below
- head: bfloat16 [5120, 77824], P('dp', 'vocab'), may hold values from -2 to 2
- token_ids: int32 [1024], P('dp'), may hold values from 0 to 77823
- valid: int32 [1024], P('dp'), may hold values 0 or 1
- advantage: float32 [1024], P('dp'), may hold values from -6 to 6
Outputs:
- hidden_grad: float32 [1024, 5120], P('vocab', 'dp')
- head_grad: float32 [5120, 77824], P('dp', 'vocab')
Inputs may be any that keep to these rules, and one draw needn't show every extreme that they name: `hidden_states`: hidden states of order one, some tokens larger than others.
All inputs are finite; a program needn't handle non-finite values. No bound on the sum of `valid` on one device may be relied on, other than what follows from the above.
Results may differ from a plain program's by a relative error of at most 0.0034.
Values may be sent and summed in bfloat16 or wider, within the bound.
No kernel may reach another device: no remote copies, remote signals or barrier semaphores. Data moves between devices by JAX's collectives and lax.ppermute only.
A program may use at most 128 MiB of HBM per device.

v0:
```python
import jax
import jax.numpy as jnp
from jax import lax
from jax.sharding import PartitionSpec as P

ROUNDS = 24


ramp_width = 0.5


def shards(hidden_states, head, token_ids, valid, advantage):
    voc_cols = head.shape[1]
    columns = lax.all_to_all(hidden_states, "dp", split_axis=1, concat_axis=0, tiled=True)
    logits = lax.psum_scatter(
        jnp.dot(columns, head, preferred_element_type=jnp.float32),
        "dp",
        scatter_dimension=0,
        tiled=True,
    )
    offset = lax.axis_index("vocab") * voc_cols
    hit = jnp.arange(voc_cols, dtype=jnp.int32)[None, :] + offset == token_ids[:, None]
    picked_part = jnp.sum(jnp.where(hit, logits, 0.0), axis=1)
    local_high = jnp.max(logits, axis=1)
    highest = lax.pmax(local_high, "vocab")
    shifted = jnp.exp(logits - highest[:, None])
    total, moment, picked = lax.psum(
        (jnp.sum(shifted, axis=1), jnp.sum(shifted * logits, axis=1), picked_part), "vocab"
    )
    normal = highest + jnp.log(total)
    entropy = normal - moment / total
    validf = valid.astype(jnp.float32)
    start_high = jnp.log(jnp.float32(voc_cols * lax.axis_size("vocab"))) + 1.0
    counted = lax.psum(jnp.sum(validf), "dp")
    quota = jnp.floor(counted / 5.0)

    def round_step(step, bounds):
        low, high = bounds
        middle = (low + high) * 0.5
        above = lax.psum(jnp.sum(jnp.where(entropy > middle, validf, 0.0)), "dp")
        more = above > quota
        return (jnp.where(more, middle, low), jnp.where(more, high, middle))

    low, threshold = lax.fori_loop(0, ROUNDS, round_step, (jnp.float32(0.0), start_high))
    gate = validf * jnp.clip((entropy - threshold) / ramp_width + 0.5, 0.0, 1.0)
    coef = -(gate * advantage)
    probs = jnp.exp(logits - normal[:, None])
    slopes = (coef[:, None] * (hit.astype(jnp.float32) - probs)).astype(jnp.bfloat16)
    piece = lax.all_gather(slopes, "dp", axis=0, tiled=True)
    grad_w = lax.dot_general(
        columns, piece, (((0,), (0,)), ((), ())), preferred_element_type=jnp.float32
    )
    product = lax.dot_general(
        piece, head, (((1,), (1,)), ((), ())), preferred_element_type=jnp.float32
    )
    partial_h = product
    head_grad, partial_h = (grad_w, partial_h)
    hidden_grad = lax.psum_scatter(partial_h, "vocab", scatter_dimension=0, tiled=True)
    return (hidden_grad, head_grad)


def solution(mesh):
    placed = (P("dp", None), P("dp", "vocab"), P("dp"), P("dp"), P("dp"))
    return jax.shard_map(
        shards,
        mesh=mesh,
        in_specs=placed,
        out_specs=(P("vocab", "dp"), P("dp", "vocab")),
        check_vma=False,
    )
```

profile of v0, /device:TPU:32, one launch (start us, length us, event | category | flops | bytes accessed | tf_op | source)
XLA Modules:
  0.0 869.0 jit_solution(13171633182702304960)
XLA Ops:
  9.8 23.4 %all_to_all.19 = bf16[128,8,640]{0,2,1:T(8,128)(2,1)} all-to-all(bf16[128,8,640]{0,2,1:T(8,128)(2,1)} %bitcast.12), channel_id=1, replica_groups=mesh['dp'=8,'vocab'=32] {'dp'}, dimensions={1} | all-to-all | bytes 2621440 | tf_op jit(solution)/shard_map/all_to_all | solution.py:14
  44.8 13.3 %psum.30 = f32[]{:T(128)} all-reduce(f32[]{:T(128)} %convert_reduce_fusion), channel_id=1, replica_groups=mesh['dp'=8,'vocab'=32] {'dp'}, use_global_device_ids=true, to_apply=%region_8.0 | all-reduce | flops 1 | bytes 8 | tf_op jit(solution)/shard_map/psum | solution.py:34
  58.7 48.3 %reduce-scatter.3.cloned.1.call-done = f32[128,2432]{1,0:T(8,128)} async-done(((f32[1024,2432]{1,0:T(8,128)}), f32[128,2432]{1,0:T(8,128)}) %reduce-scatter.3.cloned.1.call-update) | async-done | bytes 1245200 | tf_op jit(solution)/shard_map/reduce_scatter | solution.py:15
  108.4 71.6 %pmax.7 = f32[128]{0:T(128)S(1)} all-reduce(f32[128]{0:T(128)S(1)} %reduce_max.9), channel_id=1, replica_groups=mesh['dp'=8,'vocab'=32] {'vocab'}, use_global_device_ids=true, to_apply=%region_2.0 | all-reduce | flops 128 | bytes 1024 | tf_op jit(solution)/shard_map/pmax | solution.py:25
  181.7 73.6 %all-reduce = (f32[128]{0:T(128)S(1)}, f32[128]{0:T(128)S(1)}) all-reduce(f32[128]{0:T(128)S(1)} %get-tuple-element.42, f32[128]{0:T(128)S(1)} %get-tuple-element.41), channel_id=1, replica_groups=mesh['dp'=8,'vocab'=32] {'vocab'}, use_global_device_ids=true, to_apply=%region_4.0 | all-reduce | flops 256 | bytes 2048 | tf_op jit(solution)/shard_map/psum | solution.py:27
  255.3 348.4 %while.12 = (s32[]{:T(128)}, f32[]{:T(128)}, f32[]{:T(128)}, f32[128]{0:T(128)S(1)}, f32[128]{0:T(128)S(1)}, /*index=5*/f32[]{:T(128)}, s32[]{:T(128)}, f32[]{:T(128)}) while((s32[]{:T(128)}, f32[]{:T(128)}, f32[]{:T(128)}, f32[128]{0:T(128)S(1)}, f32[128]{0:T(128)S(1)}, /*index=5*/f32[]{:T(128)}, s32[]{:T(128)}, f32[]{:T(128)}) %tuple.27), condition=%wide.region_12.13_spmd, body=%wide.region_9.12_spmd.sunk | while | flops 391 | bytes 1184 | solution.py:44
  256.0 13.1 %psum.32 = f32[]{:T(128)} all-reduce(f32[]{:T(128)} %fusion.11), channel_id=1, replica_groups=mesh['dp'=8,'vocab'=32] {'dp'}, use_global_device_ids=true, to_apply=%region_11.11 | all-reduce | flops 1 | bytes 8 | tf_op jit(solution)/shard_map/while/body/eval_jaxpr/psum | solution.py:40
  270.5 13.1 %psum.32 = f32[]{:T(128)} all-reduce(f32[]{:T(128)} %fusion.11), channel_id=1, replica_groups=mesh['dp'=8,'vocab'=32] {'dp'}, use_global_device_ids=true, to_apply=%region_11.11 | all-reduce | flops 1 | bytes 8 | tf_op jit(solution)/shard_map/while/body/eval_jaxpr/psum | solution.py:40
  285.0 13.1 %psum.32 = f32[]{:T(128)} all-reduce(f32[]{:T(128)} %fusion.11), channel_id=1, replica_groups=mesh['dp'=8,'vocab'=32] {'dp'}, use_global_device_ids=true, to_apply=%region_11.11 | all-reduce | flops 1 | bytes 8 | tf_op jit(solution)/shard_map/while/body/eval_jaxpr/psum | solution.py:40
  299.6 13.1 %psum.32 = f32[]{:T(128)} all-reduce(f32[]{:T(128)} %fusion.11), channel_id=1, replica_groups=mesh['dp'=8,'vocab'=32] {'dp'}, use_global_device_ids=true, to_apply=%region_11.11 | all-reduce | flops 1 | bytes 8 | tf_op jit(solution)/shard_map/while/body/eval_jaxpr/psum | solution.py:40
  314.1 13.1 %psum.32 = f32[]{:T(128)} all-reduce(f32[]{:T(128)} %fusion.11), channel_id=1, replica_groups=mesh['dp'=8,'vocab'=32] {'dp'}, use_global_device_ids=true, to_apply=%region_11.11 | all-reduce | flops 1 | bytes 8 | tf_op jit(solution)/shard_map/while/body/eval_jaxpr/psum | solution.py:40
  328.6 13.1 %psum.32 = f32[]{:T(128)} all-reduce(f32[]{:T(128)} %fusion.11), channel_id=1, replica_groups=mesh['dp'=8,'vocab'=32] {'dp'}, use_global_device_ids=true, to_apply=%region_11.11 | all-reduce | flops 1 | bytes 8 | tf_op jit(solution)/shard_map/while/body/eval_jaxpr/psum | solution.py:40
  343.1 13.1 %psum.32 = f32[]{:T(128)} all-reduce(f32[]{:T(128)} %fusion.11), channel_id=1, replica_groups=mesh['dp'=8,'vocab'=32] {'dp'}, use_global_device_ids=true, to_apply=%region_11.11 | all-reduce | flops 1 | bytes 8 | tf_op jit(solution)/shard_map/while/body/eval_jaxpr/psum | solution.py:40
  357.6 13.1 %psum.32 = f32[]{:T(128)} all-reduce(f32[]{:T(128)} %fusion.11), channel_id=1, replica_groups=mesh['dp'=8,'vocab'=32] {'dp'}, use_global_device_ids=true, to_apply=%region_11.11 | all-reduce | flops 1 | bytes 8 | tf_op jit(solution)/shard_map/while/body/eval_jaxpr/psum | solution.py:40
  372.1 13.1 %psum.32 = f32[]{:T(128)} all-reduce(f32[]{:T(128)} %fusion.11), channel_id=1, replica_groups=mesh['dp'=8,'vocab'=32] {'dp'}, use_global_device_ids=true, to_apply=%region_11.11 | all-reduce | flops 1 | bytes 8 | tf_op jit(solution)/shard_map/while/body/eval_jaxpr/psum | solution.py:40
  386.7 13.1 %psum.32 = f32[]{:T(128)} all-reduce(f32[]{:T(128)} %fusion.11), channel_id=1, replica_groups=mesh['dp'=8,'vocab'=32] {'dp'}, use_global_device_ids=true, to_apply=%region_11.11 | all-reduce | flops 1 | bytes 8 | tf_op jit(solution)/shard_map/while/body/eval_jaxpr/psum | solution.py:40
  401.2 13.1 %psum.32 = f32[]{:T(128)} all-reduce(f32[]{:T(128)} %fusion.11), channel_id=1, replica_groups=mesh['dp'=8,'vocab'=32] {'dp'}, use_global_device_ids=true, to_apply=%region_11.11 | all-reduce | flops 1 | bytes 8 | tf_op jit(solution)/shard_map/while/body/eval_jaxpr/psum | solution.py:40
  531.8 13.1 %psum.32 = f32[]{:T(128)} all-reduce(f32[]{:T(128)} %fusion.11), channel_id=1, replica_groups=mesh['dp'=8,'vocab'=32] {'dp'}, use_global_device_ids=true, to_apply=%region_11.11 | all-reduce | flops 1 | bytes 8 | tf_op jit(solution)/shard_map/while/body/eval_jaxpr/psum | solution.py:40
  546.4 13.1 %psum.32 = f32[]{:T(128)} all-reduce(f32[]{:T(128)} %fusion.11), channel_id=1, replica_groups=mesh['dp'=8,'vocab'=32] {'dp'}, use_global_device_ids=true, to_apply=%region_11.11 | all-reduce | flops 1 | bytes 8 | tf_op jit(solution)/shard_map/while/body/eval_jaxpr/psum | solution.py:40
  560.9 13.1 %psum.32 = f32[]{:T(128)} all-reduce(f32[]{:T(128)} %fusion.11), channel_id=1, replica_groups=mesh['dp'=8,'vocab'=32] {'dp'}, use_global_device_ids=true, to_apply=%region_11.11 | all-reduce | flops 1 | bytes 8 | tf_op jit(solution)/shard_map/while/body/eval_jaxpr/psum | solution.py:40
  575.4 13.1 %psum.32 = f32[]{:T(128)} all-reduce(f32[]{:T(128)} %fusion.11), channel_id=1, replica_groups=mesh['dp'=8,'vocab'=32] {'dp'}, use_global_device_ids=true, to_apply=%region_11.11 | all-reduce | flops 1 | bytes 8 | tf_op jit(solution)/shard_map/while/body/eval_jaxpr/psum | solution.py:40
  589.9 13.1 %psum.32 = f32[]{:T(128)} all-reduce(f32[]{:T(128)} %fusion.11), channel_id=1, replica_groups=mesh['dp'=8,'vocab'=32] {'dp'}, use_global_device_ids=true, to_apply=%region_11.11 | all-reduce | flops 1 | bytes 8 | tf_op jit(solution)/shard_map/while/body/eval_jaxpr/psum | solution.py:40
  606.4 30.3 %all-gather.2.cloned.1.call-done = bf16[1024,2432]{1,0:T(8,128)(2,1)} async-done(((bf16[128,2432]{1,0:T(8,128)(2,1)}), bf16[1024,2432]{1,0:T(8,128)(2,1)}) %all-gather.2.cloned.1.call-update) | async-done | bytes 4980752 | tf_op jit(solution)/shard_map/all_gather | solution.py:49
  662.4 200.1 %reduce-scatter.5.cloned.1.call-done = f32[32,640]{1,0:T(8,128)} async-done(((f32[1024,640]{1,0:T(8,128)}), f32[32,640]{1,0:T(8,128)}) %reduce-scatter.5.cloned.1.call-update) | async-done | bytes 81936 | tf_op jit(solution)/shard_map/reduce_scatter | solution.py:58
  (60 shorter events, 167.0 us)
Async XLA Ops:
  7.2 28.4 %copy-start = (bf16[640,2432]{1,0:T(8,128)(2,1)S(1)}, bf16[640,2432]{1,0:T(8,128)(2,1)}, u32[]{:S(2)}) copy-start(bf16[640,2432]{1,0:T(8,128)(2,1)} %param.8) | copy-start | bytes 9338884
  7.2 99.8 %reduce-scatter.3.cloned.1.call-start = ((), (), s32[]{:S(2)}) async-start(), calls=%async_computation.3 | async-start | bytes 11206656 | tf_op jit(solution)/shard_map/reduce_scatter | solution.py:15
  43.6 0.7 copy-start.2
  43.6 593.1 %all-gather.2.cloned.1.call-start = ((), (), s32[]{:S(2)}) async-start(), calls=%async_computation.4 | async-start | bytes 5603328 | tf_op jit(solution)/shard_map/all_gather | solution.py:49
  58.7 545.1 %copy-start.1 = (f32[128]{0:T(128)S(1)}, f32[128]{0:T(128)}, u32[]{:S(2)}) copy-start(f32[128]{0:T(128)} %param.11) | copy-start | bytes 1540
  58.7 545.1 %copy-start.3 = (s32[128]{0:T(128)S(1)}, s32[128]{0:T(128)}, u32[]{:S(2)}) copy-start(s32[128]{0:T(128)} %param.9) | copy-start | bytes 1540
  606.4 256.1 %reduce-scatter.5.cloned.1.call-start = ((), (), s32[]{:S(2)}) async-start(), calls=%async_computation.5 | async-start | bytes 2703360 | tf_op jit(solution)/shard_map/reduce_scatter | solution.py:58
Sparse Core Ops, SparseCore 0:
  43.7 63.1 reduce-scatter.2
  606.5 30.1 all-gather.1
  645.1 217.3 reduce-scatter.4
where the time goes:
time: 872 us; the launch traced here: 869 us
  blocking collectives  497 us (57%)
  waiting for transfers between devices  279 us (32%)
  matrix products  25.7 us (3%)
  other arithmetic  22.7 us (3%)
  loops' own time  17.4 us (2%)
  between operations  14.4 us (2%)
  local copies, waits for them, and re-layouts  13.5 us (2%)
    psum x24, blocking collectives, round_step(): above = lax.psum(jnp.sum(jnp.where(entropy > middle, validf, 0.0)), 'dp')  315 us
    reduce_scatter x1, waiting for transfers between devices, shards(): lax.psum_scatter(partial_h, 'vocab', scatter_dimension=0, tiled=True)  200 us
    psum x1, blocking collectives, shards(): lax.psum((jnp.sum(shifted, axis=1), jnp.sum(shifted * logits, axis=1), pi...  73.6 us
    pmax x1, blocking collectives, shards(): highest = lax.pmax(local_high, 'vocab')  71.6 us
    reduce_scatter x1, waiting for transfers between devices, shards(): lax.psum_scatter(jnp.dot(columns, head, preferred_element_type=jnp.float3...  48.3 us
    all_gather x1, waiting for transfers between devices, shards(): piece = lax.all_gather(slopes, 'dp', axis=0, tiled=True)  30.3 us
    all_to_all x1, blocking collectives, shards(): lax.all_to_all(hidden_states, 'dp', split_axis=1, concat_axis=0, tiled=True)  23.4 us
  transfers between devices with their start and end apart: 3, of which 3 were waited for; matrix products, arithmetic and copies ran while one was open for 2% of the time, Pallas kernels for 0%

commit v1 on v0

v1 whole, which is shorter than its diff:
```python
import functools

import jax
import jax.numpy as jnp
import numpy as np
from jax import lax
from jax.experimental import pallas as pl
from jax.experimental.pallas import tpu as pltpu
from jax.sharding import Mesh, PartitionSpec as P

ROUNDS = 24
LEVELS = 6
CAP = 16
CAP_OWNER = 48

ramp_width = 0.5
DP = ("x", "c")
VOC = ("y", "z")
f32 = jnp.float32
bf16 = jnp.bfloat16


def ring(n, shift):
    return [(i, (i + shift) % n) for i in range(n)]


SWAP = [(0, 1), (1, 0)]


def dense(hidden_states, head, token_ids, valid, advantage):
    voc_cols = head.shape[1]
    columns = lax.all_to_all(hidden_states, DP, split_axis=1, concat_axis=0, tiled=True)
    logits = lax.psum_scatter(
        jnp.dot(columns, head, preferred_element_type=f32), DP, scatter_dimension=0, tiled=True
    )
    offset = lax.axis_index(VOC) * voc_cols
    hit = jnp.arange(voc_cols, dtype=jnp.int32)[None, :] + offset == token_ids[:, None]
    highest = lax.pmax(jnp.max(logits, axis=1), VOC)
    shifted = jnp.exp(logits - highest[:, None])
    total, moment = lax.psum((jnp.sum(shifted, axis=1), jnp.sum(shifted * logits, axis=1)), VOC)
    normal = highest + jnp.log(total)
    entropy = normal - moment / total
    validf = valid.astype(f32)
    start_high = jnp.log(f32(voc_cols * lax.axis_size(VOC))) + 1.0
    counted = lax.psum(jnp.sum(validf), DP)
    quota = jnp.floor((counted + 0.5) * 0.2)

    def round_step(step, bounds):
        low, high = bounds
        middle = (low + high) * 0.5
        above = lax.psum(jnp.sum(jnp.where(entropy > middle, validf, 0.0)), DP)
        more = above > quota
        return (jnp.where(more, middle, low), jnp.where(more, high, middle))

    _, threshold = lax.fori_loop(0, ROUNDS, round_step, (f32(0.0), start_high))
    gate = validf * jnp.clip((entropy - threshold) / ramp_width + 0.5, 0.0, 1.0)
    coef = -(gate * advantage)
    probs = jnp.exp(logits - normal[:, None])
    slopes = (coef[:, None] * (hit.astype(f32) - probs)).astype(bf16)
    piece = lax.all_gather(slopes, DP, axis=0, tiled=True)
    head_grad = lax.dot_general(columns, piece, (((0,), (0,)), ((), ())), preferred_element_type=f32)
    product = lax.dot_general(piece, head, (((1,), (1,)), ((), ())), preferred_element_type=f32)
    return lax.psum_scatter(product, VOC, scatter_dimension=0, tiled=True), head_grad


def bisect(entropy, counted, start_high):
    columns = jnp.transpose(entropy)
    quota = jnp.floor((counted + 0.5) * 0.2)
    lane = lax.broadcasted_iota(jnp.int32, (1, 128), 1)
    leaves = 1 << LEVELS
    low = jnp.zeros((1, 128), f32)
    high = jnp.full((1, 128), start_high, f32)
    for _ in range(ROUNDS // LEVELS):
        for level in range(LEVELS):
            middle = (low + high) * 0.5
            bit = ((lane >> (LEVELS - 1 - level)) & 1) == 1
            low, high = jnp.where(bit, middle, low), jnp.where(bit, high, middle)
        above = jnp.zeros((128, 128), f32)
        for i in range(8):
            above = above + jnp.where(columns[:, i : i + 1] > low, 1.0, 0.0)
        above = jnp.sum(above, axis=0, keepdims=True)
        more = jnp.where(((above > quota) | (lane == 0)) & (lane < leaves), 1.0, 0.0)
        here = lane == jnp.sum(more, axis=1, keepdims=True).astype(jnp.int32) - 1
        low, high = (
            jnp.broadcast_to(jnp.sum(jnp.where(here, v, 0.0), axis=1, keepdims=True), (1, 128))
            for v in (low, high)
        )
    return high[:, :1]


def call(kernel, out, args, scratch=(), vmem=16, smem=0, **kw):
    specs = [pl.BlockSpec(memory_space=pltpu.SMEM)] * smem
    specs += [pl.BlockSpec(memory_space=pltpu.VMEM)] * (len(args) - smem)
    return pl.pallas_call(
        kernel,
        in_specs=specs,
        out_shape=out,
        scratch_shapes=list(scratch),
        compiler_params=pltpu.CompilerParams(vmem_limit_bytes=vmem << 20),
        **kw,
    )(*args)


def struct(shape, dtype):
    return jax.ShapeDtypeStruct(shape, dtype)


LN2_64 = float(np.log(2.0) / 64.0)


def partial_kernel(at, b0, b1, b2, b3, head, other, own, q1, q2, q3, mine, theirs, part):
    tokens = b0.shape[0]
    rows, cols = head.shape
    here = pl.ds(pl.multiple_of(at[1] * rows, 128), rows)
    there = pl.ds(pl.multiple_of((1 - at[1]) * rows, 128), rows)
    for s, block in enumerate((b0, b1, b2, b3)):
        mine[s * tokens : (s + 1) * tokens, :] = block[:, here]
        theirs[s * tokens : (s + 1) * tokens, :] = block[:, there]

    def tile(at_col, size):
        span = pl.ds(at_col, size)
        part[:, span] = jnp.dot(mine[...], head[:, span], preferred_element_type=f32) + jnp.dot(
            theirs[...], other[:, span], preferred_element_type=f32
        )

    wide = cols // 256

    @pl.loop(0, wide)
    def _(i):
        tile(pl.multiple_of(i * 256, 256), 256)

    if cols > wide * 256:
        tile(wide * 256, cols - wide * 256)
    own[...] = part[0:tokens, :]
    step = 32
    for s, out in ((1, q1), (2, q2), (3, q3)):

        @pl.loop(0, tokens // step)
        def _(i, s=s, out=out):
            to = pl.ds(pl.multiple_of(i * step, step), step)
            block = part[pl.ds(pl.multiple_of(s * tokens + i * step, step), step), :]
            top = jnp.maximum(jnp.max(jnp.abs(block), axis=1, keepdims=True), 1e-30)
            power = jnp.ceil(jnp.log(top) * (1.0 / LN2_64)) + 1.0
            fixed = jnp.round(block * (jnp.exp(power * -LN2_64) * 32766.0))
            out[to, 0:cols] = fixed.astype(jnp.int32).astype(jnp.int16)
            wide_power = jnp.broadcast_to(power.astype(jnp.int32), (step, 128))
            out[to, cols : cols + 128] = wide_power.astype(jnp.int16)


def total_kernel(own, q1, q2, q3, logits, sent, stats):
    tokens, cols = own.shape
    step = 16
    lane = lax.broadcasted_iota(jnp.int32, (step, 128), 1)

    @pl.loop(0, tokens // step)
    def _(i):
        at = pl.ds(pl.multiple_of(i * step, step), step)
        value = own[at, :]
        for q in (q1, q2, q3):
            power = q[at, cols : cols + 128].astype(jnp.int32).astype(f32)[:, :1]
            scale = jnp.exp(power * LN2_64) * (1.0 / 32766.0)
            value = value + q[at, 0:cols].astype(jnp.int32).astype(f32) * scale
        logits[at, :] = value
        high = jnp.max(value, axis=1, keepdims=True)
        shifted = jnp.exp(value - high)
        total = jnp.sum(shifted, axis=1, keepdims=True)
        moment = jnp.sum(shifted * value, axis=1, keepdims=True)
        stats[at, :] = jnp.where(lane == 0, high, jnp.where(lane == 1, total, moment))

    rows = jnp.transpose(stats[...])[0:8, :]
    for i in range(sent.shape[0]):
        sent[i] = rows


def merge_kernel(parts, valid, advantage, sent):
    high = parts[0, 0:1, :]
    for i in range(1, parts.shape[0]):
        high = jnp.maximum(high, parts[i, 0:1, :])
    sums = jnp.zeros((8, 128), f32)
    for i in range(parts.shape[0]):
        sums = sums + jnp.exp(parts[i, 0:1, :] - high) * parts[i]
    row = lax.broadcasted_iota(jnp.int32, (8, 128), 0)
    out = jnp.where(row == 0, high, sums)
    out = jnp.where(row == 3, valid[...].astype(f32), jnp.where(row == 4, advantage[...], out))
    for i in range(sent.shape[0]):
        sent[i] = out


def plan_kernel(start_high, cap_owner, parts, coef_out, normal_out, packed_out, slot_out, flag, rows):
    owners = 8
    ny = parts.shape[0] // owners
    for o in range(owners):
        high = parts[o * ny, 0:1, :]
        for y in range(1, ny):
            high = jnp.maximum(high, parts[o * ny + y, 0:1, :])
        sums = jnp.zeros((8, 128), f32)
        for y in range(ny):
            sums = sums + jnp.exp(parts[o * ny + y, 0:1, :] - high) * parts[o * ny + y]
        row = lax.broadcasted_iota(jnp.int32, (8, 128), 0)
        normal = high + jnp.log(sums[1:2, :])
        entropy = normal - sums[2:3, :] / sums[1:2, :]
        rows[o] = jnp.where(row == 0, normal, jnp.where(row == 1, entropy, parts[o * ny]))
    normal, entropy, valid, advantage = (
        jnp.concatenate([rows[o, k : k + 1, :] for o in range(owners)], axis=0) for k in (0, 1, 3, 4)
    )
    counted = jnp.sum(jnp.sum(valid, axis=1, keepdims=True), axis=0, keepdims=True)
    threshold = bisect(jnp.where(valid > 0.0, entropy, -jnp.inf), counted, start_high)
    gate = valid * jnp.clip((entropy - threshold) / ramp_width + 0.5, 0.0, 1.0)
    coef = -(gate * advantage)
    active = coef != 0.0
    activef = active.astype(f32)
    i = lax.broadcasted_iota(jnp.int32, (128, 128), 0)
    j = lax.broadcasted_iota(jnp.int32, (128, 128), 1)
    ahead = (i < j).astype(f32)
    group = 128 // (32 // owners)
    same = (i // group == j // group).astype(f32)
    rank_owner = jnp.dot(activef, ahead, preferred_element_type=f32)
    rank_group = jnp.dot(activef, ahead * same, preferred_element_type=f32)
    start = (lax.broadcasted_iota(jnp.int32, (8, 128), 1) // group * CAP).astype(f32)
    coef_out[...] = coef
    normal_out[...] = normal
    packed_out[...] = jnp.where(active, rank_owner, -1.0)
    slot_out[...] = jnp.where(active, rank_group + start, -1.0)
    over = jnp.where(active & ((rank_owner >= cap_owner) | (rank_group >= CAP)), 1.0, 0.0)
    flag[0, 0] = jnp.max(over).astype(jnp.int32)


def as_columns(rows):
    row = lax.broadcasted_iota(jnp.int32, (8, 128), 0)
    out = jnp.zeros((8, 128), f32)
    for k, value in enumerate(rows):
        out = jnp.where(row == k, value, out)
    return jnp.transpose(out)


def one_hot(count, slots):
    row = lax.broadcasted_iota(jnp.int32, (count, 128), 0).astype(f32)
    return (row == slots).astype(f32).astype(bf16)


def slopes_kernel(at, logits, coef_all, normal_all, packed_all, ids, out):
    me = pl.ds(at[2], 1)
    count = out.shape[0]
    columns = as_columns([coef_all[me, :], normal_all[me, :], ids[...].astype(f32)])
    coef, normal, token = columns[:, 0:1], columns[:, 1:2], columns[:, 2:3].astype(jnp.int32) - at[3]
    choose = one_hot(count, packed_all[me, :])
    lane = lax.broadcasted_iota(jnp.int32, (128, 128), 1)
    for k in range(logits.shape[1] // 128):
        span = slice(k * 128, (k + 1) * 128)
        hit = (lane + k * 128 == token).astype(f32)
        slopes = (coef * (hit - jnp.exp(logits[:, span] - normal))).astype(bf16)
        out[:, span] = jnp.dot(choose, slopes, preferred_element_type=f32).astype(bf16)


def product_kernel(nx, at, mine, theirs, head, packed_all, slot_all, out, held):
    half = mine.shape[0]
    count = half // nx
    for k, rows in enumerate((mine, theirs)):
        held[k * half : (k + 1) * half, :] = lax.dot_general(
            rows[...], head[...], (((1,), (1,)), ((), ())), preferred_element_type=f32
        ).astype(bf16)
    size = out.shape[0] // (2 * nx)
    for owner in range(2 * nx):
        to, core = owner // 2, owner % 2
        source = lax.rem(at[0] - to + nx, nx) * count + lax.rem(at[1] + core, 2) * half
        block = held[pl.ds(pl.multiple_of(source, 16), count), :]
        spread = lax.dot_general(
            one_hot(size, slot_all[owner : owner + 1, :]),
            one_hot(count, packed_all[owner : owner + 1, :]),
            (((1,), (1,)), ((), ())),
            preferred_element_type=f32,
        ).astype(bf16)
        out[owner * size : (owner + 1) * size, :] = jnp.dot(
            spread, block, preferred_element_type=f32
        ).astype(bf16)


def outer_kernel(nx, at, packed_all, hid_mine, hid_theirs, mine, theirs, out, held):
    half = mine.shape[0]
    count = half // nx
    for k, hidden in enumerate((hid_mine, hid_theirs)):
        for s in range(nx):
            owner = lax.rem(at[0] - s + nx, nx) * 2 + lax.rem(at[1] + k, 2)
            choose = one_hot(count, packed_all[pl.ds(owner, 1), :])
            to = k * half + s * count
            held[to : to + count, :] = jnp.dot(
                choose, hidden[s * 128 : (s + 1) * 128, :], preferred_element_type=f32
            ).astype(bf16)
    total = jnp.zeros(out.shape, f32)
    for k, rows in enumerate((mine, theirs)):
        total = total + lax.dot_general(
            held[k * half : (k + 1) * half, :],
            rows[...],
            (((0,), (0,)), ((), ())),
            preferred_element_type=f32,
        )
    out[...] = total


def sum_kernel(at, parts, slot_all, out, ranks):
    n_voc = parts.shape[0] // CAP
    total = parts[0:CAP, :].astype(f32)
    for i in range(1, n_voc):
        total = total + parts[i * CAP : (i + 1) * CAP, :].astype(f32)
    group = out.shape[0]
    per_owner = 128 // group
    owner, place = at[4] // per_owner, lax.rem(at[4], per_owner)
    ranks[...] = as_columns([slot_all[pl.ds(owner, 1), :]])
    rank = ranks[pl.ds(pl.multiple_of(place * group, group), group), :][:, 0:1]
    rank = rank - (place * CAP).astype(f32)
    rows = jnp.zeros(out.shape, f32)
    for r in range(CAP):
        rows = rows + jnp.where(rank == float(r), total[r : r + 1, :], 0.0)
    out[...] = rows


def shards(hidden_states, head, token_ids, valid, advantage):
    tokens, width = hidden_states.shape
    rows, voc_cols = head.shape
    nx, n_voc, n_dp = lax.axis_size("x"), lax.axis_size(VOC), lax.axis_size(DP)
    x, c, block = lax.axis_index("x"), lax.axis_index("c"), lax.axis_index(VOC)
    at = jnp.stack([x, c, x * 2 + c, block * voc_cols, block]).astype(jnp.int32)
    chip_rows = width // nx

    head_other = lax.ppermute(head, "c", SWAP)

    def block_for(to):
        return lax.dynamic_slice(hidden_states, (0, to * chip_rows), (tokens, chip_rows))

    came = {s: lax.ppermute(block_for((x + s) % nx), "x", ring(nx, s)) for s in (2, 1, 3)}
    packed = struct((tokens, voc_cols + 128), jnp.int16)
    own, q1, q2, q3, hid_mine, hid_send = call(
        partial_kernel,
        [struct((tokens, voc_cols), f32), packed, packed, packed]
        + [struct((nx * tokens, rows), bf16)] * 2,
        [at, block_for(x), came[1], came[2], came[3], head, head_other],
        [pltpu.VMEM((nx * tokens, voc_cols), f32)],
        vmem=32,
        smem=1,
    )
    sent = {s: lax.ppermute(q, "x", ring(nx, -s)) for s, q in ((2, q2), (1, q1), (3, q3))}
    hid_theirs = lax.ppermute(hid_send, "c", SWAP)
    logits, stats = call(
        total_kernel,
        [struct((tokens, voc_cols), f32), struct((lax.axis_size("z"), 8, 128), f32)],
        [own, sent[1], sent[2], sent[3]],
        [pltpu.VMEM((tokens, 128), f32)],
    )

    stats = lax.all_to_all(stats, "z", 0, 0, tiled=True)
    everyone = DP + ("y",)
    stats = call(
        merge_kernel,
        struct((lax.axis_size(everyone), 8, 128), f32),
        [stats, valid.reshape(1, tokens), advantage.reshape(1, tokens)],
    )
    stats = lax.all_to_all(stats, everyone, 0, 0, tiled=True)
    start_high = float(np.float32(np.log(np.float32(voc_cols * n_voc))) + np.float32(1.0))
    table = struct((n_dp, tokens), f32)
    coef_all, normal_all, packed_all, slot_all, flag = call(
        functools.partial(plan_kernel, start_high, CAP_OWNER),
        [table] * 4 + [struct((1, 1), jnp.int32)],
        [stats],
        [pltpu.VMEM((n_dp, 8, 128), f32)],
        out_specs=[pl.BlockSpec(memory_space=pltpu.VMEM)] * 4 + [pl.BlockSpec(memory_space=pltpu.SMEM)],
    )

    def sparse(_):
        piece = call(
            slopes_kernel,
            struct((CAP_OWNER, voc_cols), bf16),
            [at, logits, coef_all, normal_all, packed_all, token_ids.reshape(1, tokens)],
            smem=1,
        )
        pieces = {s: lax.ppermute(piece, "x", ring(nx, s)) for s in (2, 1, 3)}
        mine = jnp.concatenate([piece, pieces[1], pieces[2], pieces[3]], axis=0)
        theirs = lax.ppermute(mine, "c", SWAP)
        product = call(
            functools.partial(product_kernel, nx),
            struct((n_voc * CAP, rows), bf16),
            [at, mine, theirs, head, packed_all, slot_all],
            [pltpu.VMEM((2 * nx * CAP_OWNER, rows), bf16)],
            smem=1,
        )
        parts = lax.all_to_all(product, VOC, 0, 0, tiled=True)
        tile = 128
        head_grad = pl.pallas_call(
            functools.partial(outer_kernel, nx),
            grid=(rows // tile,),
            in_specs=[
                pl.BlockSpec(memory_space=pltpu.SMEM),
                pl.BlockSpec((n_dp, tokens), lambda i: (0, 0)),
                pl.BlockSpec((nx * tokens, tile), lambda i: (0, i)),
                pl.BlockSpec((nx * tokens, tile), lambda i: (0, i)),
                pl.BlockSpec((nx * CAP_OWNER, voc_cols), lambda i: (0, 0)),
                pl.BlockSpec((nx * CAP_OWNER, voc_cols), lambda i: (0, 0)),
            ],
            out_specs=pl.BlockSpec((tile, voc_cols), lambda i: (i, 0)),
            out_shape=struct((rows, voc_cols), f32),
            scratch_shapes=[pltpu.VMEM((2 * nx * CAP_OWNER, tile), bf16)],
            compiler_params=pltpu.CompilerParams(vmem_limit_bytes=24 << 20),
            cost_estimate=pl.CostEstimate(
                flops=4 * nx * CAP_OWNER * rows * voc_cols,
                bytes_accessed=4 * rows * voc_cols,
                transcendentals=0,
            ),
        )(at, packed_all, hid_mine, hid_theirs, mine, theirs)
        hidden_grad = call(
            sum_kernel,
            struct((tokens * n_dp // n_voc, rows), f32),
            [at, parts, slot_all],
            [pltpu.VMEM((tokens, 8), f32)],
            smem=1,
        )
        return hidden_grad, head_grad

    def whole(_):
        return dense(hidden_states, head, token_ids, valid, advantage)

    return lax.cond(flag[0, 0] != 0, whole, sparse, 0)


def solution(mesh):
    chips = Mesh(mesh.devices.reshape(4, 2, 4, 8), DP + VOC)
    placed = (P(DP, None), P(DP, VOC), P(DP), P(DP), P(DP))
    return jax.shard_map(
        shards,
        mesh=chips,
        in_specs=placed,
        out_specs=(P(VOC, DP), P(DP, VOC)),
        check_vma=False,
    )
```

time: 872 us -> 166 us (0.19)
  blocking collectives: 497 us -> 15 us
  waiting for transfers between devices: 279 us -> 81.1 us
  Pallas kernels: 0 us -> 29.7 us
  matrix products: 25.7 us -> 0 us
  starting transfers between devices: 0.12 us -> 22.9 us
  other arithmetic: 22.7 us -> 0.08 us
  loops' own time: 17.4 us -> 0.05 us
  local copies, waits for them, and re-layouts: 13.5 us -> 2.36 us
    psum x26 -> x0, blocking collectives: 402 us -> none  [the longest x24 315 us: round_step(): above = lax.psum(jnp.sum(jnp.where(entropy > middle, validf, 0.0)), 'dp')]
    reduce_scatter x2 -> x0, waiting for transfers between devices: 248 us -> none  [the longest x1 200 us: shards(): lax.psum_scatter(partial_h, 'vocab', scatter_dimension=0, tiled=True)]
    pmax x1 -> x0, blocking collectives: 71.6 us -> none  [shards(): highest = lax.pmax(local_high, 'vocab')]
    ppermute x0 -> x12, waiting for transfers between devices: none -> 58.7 us  [the longest x3 30 us: shards(): lax.ppermute(q, 'x', ring(nx, -s))]
    all_gather x1 -> x0, waiting for transfers between devices: 30.3 us -> none  [shards(): piece = lax.all_gather(slopes, 'dp', axis=0, tiled=True)]
    pallas_call x0 -> x8, Pallas kernels: none -> 29.7 us  [the longest x7 23.2 us: call(): pl.pallas_call(kernel, in_specs=specs, out_shape=out, scratch_shapes=list...]
    dot_general x3 -> x0, matrix products: 25.7 us -> none  [the longest x1 9.53 us: shards(): lax.dot_general(columns, piece, (((0,), (0,)), ((), ())), preferred_eleme...]
    all_to_all x0 -> x2, waiting for transfers between devices: none -> 22.4 us  [the longest x1 14.6 us: sparse(): parts = lax.all_to_all(product, VOC, 0, 0, tiled=True)]
  transfers between devices with their start and end apart: 3 -> 14, of which waited for: 3 -> 10; matrix products, arithmetic and copies ran while one was open for 2% -> 1% of each run, Pallas kernels for 0% -> 7%
where the time goes in v1:
time: 166 us
  waiting for transfers between devices  81.1 us (49%)
  Pallas kernels  29.7 us (18%)
  starting transfers between devices  22.9 us (14%)
  blocking collectives  15 us (9%)
  between operations  14.8 us (9%)
  local copies, waits for them, and re-layouts  2.36 us (1%)
    ppermute x3, waiting for transfers between devices, shards(): lax.ppermute(q, 'x', ring(nx, -s))  30 us
    pallas_call x7, Pallas kernels, call(): pl.pallas_call(kernel, in_specs=specs, out_shape=out, scratch_shapes=list...  23.2 us
    all_to_all x1, blocking collectives, shards(): stats = lax.all_to_all(stats, 'z', 0, 0, tiled=True)  15 us
    all_to_all x1, waiting for transfers between devices, sparse(): parts = lax.all_to_all(product, VOC, 0, 0, tiled=True)  14.6 us
    ppermute x3, waiting for transfers between devices, shards(): lax.ppermute(block_for((x + s) % nx), 'x', ring(nx, s))  13.8 us
    ppermute x3, waiting for transfers between devices, sparse(): pieces = {s: lax.ppermute(piece, 'x', ring(nx, s)) for s in (2, 1, 3)}  12.4 us
    all_to_all x1, waiting for transfers between devices, shards(): stats = lax.all_to_all(stats, everyone, 0, 0, tiled=True)  7.83 us
    pallas_call x1, Pallas kernels, sparse(): pl.pallas_call(functools.partial(outer_kernel, nx), grid=(rows // tile,),...  6.5 us
  transfers between devices with their start and end apart: 14, of which 10 were waited for; matrix products, arithmetic and copies ran while one was open for 1% of the time, Pallas kernels for 7%

profile of v1, /device:TPU:32, one launch (start us, length us, event | category | flops | bytes accessed | tf_op | source)
XLA Modules:
  0.0 165.9 jit_solution(5970826862156818929)
XLA Ops:
  7.3 2.2 %constant_dynamic-slice_fusion = (bf16[128,1280]{1,0:T(8,128)(2,1)}, bf16[128,1280]{1,0:T(8,128)(2,1)}, bf16[128,1280]{1,0:T(8,128)(2,1)}, bf16[128,1280]{1,0:T(8,128)(2,1)S(1)}) fusion(bf16[128,5120]{1,0:T(8,128)(2,1)} %param.9, s32[]{:T(128)S(6)} %select_n.44, s32[]{:T(128)S(6)} %select_n.42, s32[]{:T(128)S(6)} %select_n.40, s32[]{:T(128)S(6)} %select_n.38), kind=kLoop, calls=%fused_computation.13 | loop fusion | bytes 2621456 | tf_op jit(solution)/shard_map/dynamic_slice | solution.py:328
  9.6 1.5 collective-permute-start.4
  11.1 2.7 %collective-permute-start.5 = (bf16[128,1280]{1,0:T(8,128)(2,1)}, bf16[128,1280]{1,0:T(8,128)(2,1)}, u32[]{:S(2)}, u32[]{:S(2)}) collective-permute-start(bf16[128,1280]{1,0:T(8,128)(2,1)} %get-tuple-element.144), channel_id=1, source_target_pairs={{0,128},{64,192},{128,0},{192,64},{1,129},{65,193},{129,1},{193,65... | collective-permute-start | bytes 983048 | tf_op jit(solution)/shard_map/ppermute | solution.py:330
  15.3 5.8 %collective-permute-done.4.b1 = bf16[128,1280]{1,0:T(8,128)(2,1)} collective-permute-done((bf16[128,1280]{1,0:T(8,128)(2,1)}, bf16[128,1280]{1,0:T(8,128)(2,1)}, u32[]{:S(2)}, u32[]{:S(2)}) %collective-permute-start.4) | collective-permute-done | bytes 327712 | tf_op jit(solution)/shard_map/ppermute | solution.py:330
  21.1 8.0 %collective-permute-done.5.b2 = bf16[128,1280]{1,0:T(8,128)(2,1)} collective-permute-done((bf16[128,1280]{1,0:T(8,128)(2,1)}, bf16[128,1280]{1,0:T(8,128)(2,1)}, u32[]{:S(2)}, u32[]{:S(2)}) %collective-permute-start.5) | collective-permute-done | bytes 327712 | tf_op jit(solution)/shard_map/ppermute | solution.py:330
  29.2 10.5 %shard_map.72 = (f32[128,2432]{1,0:T(8,128)S(1)}, s16[128,2560]{1,0:T(8,128)(2,1)S(1)}, s16[128,2560]{1,0:T(8,128)(2,1)S(1)}, s16[128,2560]{1,0:T(8,128)(2,1)S(1...) custom-call(s32[5]{0:T(128)S(1)} %stack.23.at, bf16[128,1280]{1,0:T(8,128)(2,1)S(1)} %get-tuple-element.146.b0, ...), custom_call_target="tpu_custom_call" | custom-call | tf_op jit(solution)/shard_map/pallas_call | solution.py:94
  39.7 2.3 %collective-permute-start.8 = (s16[128,2560]{1,0:T(8,128)(2,1)S(1)}, s16[128,2560]{1,0:T(8,128)(2,1)S(1)}, u32[]{:S(2)}, u32[]{:S(2)}) collective-permute-start(s16[128,2560]{1,0:T(8,128)(2,1)S(1)} %get-tuple-element.93), channel_id=1, source_target_pairs={{0,192},{64,0},{128,64},{192,128},{1,193},{65,1},{129,65},{193,129... | collective-permute-start | bytes 1966088 | tf_op jit(solution)/shard_map/ppermute | solution.py:341
  43.8 26.4 %collective-permute-done.8.q1 = s16[128,2560]{1,0:T(8,128)(2,1)S(1)} collective-permute-done((s16[128,2560]{1,0:T(8,128)(2,1)S(1)}, s16[128,2560]{1,0:T(8,128)(2,1)S(1)}, u32[]{:S(2)}, u32[]{:S(2)}) %collective-permute-start.8) | collective-permute-done | bytes 655392 | tf_op jit(solution)/shard_map/ppermute | solution.py:341
  70.2 3.5 %collective-permute-done.10.q3 = s16[128,2560]{1,0:T(8,128)(2,1)S(1)} collective-permute-done((s16[128,2560]{1,0:T(8,128)(2,1)S(1)}, s16[128,2560]{1,0:T(8,128)(2,1)S(1)}, u32[]{:S(2)}, u32[]{:S(2)}) %collective-permute-start.10) | collective-permute-done | bytes 655392 | tf_op jit(solution)/shard_map/ppermute | solution.py:341
  73.7 2.5 %shard_map.73 = (f32[128,2432]{1,0:T(8,128)S(1)}, f32[8,8,128]{2,1,0:T(8,128)S(1)}) custom-call(f32[128,2432]{1,0:T(8,128)S(1)} %get-tuple-element.92.own, s16[128,2560]{1,0:T(8,128)(2,1)S(1)} %collective-permute-done.8.q1, s16[128,2560]{1,0:T(8,128)(2,1)S(1)} %collective-permute-done.9.q2, s16[128,2560]{1,0:T(8,128)(2,1)S(1)} %collective-permute-done.10.q3), custom_call_target="tpu_custom_call" | custom-call | tf_op jit(solution)/shard_map/pallas_call | solution.py:94
  76.2 15.0 %all_to_all.34.parts = f32[8,8,128]{2,1,0:T(8,128)S(1)} all-to-all(f32[8,8,128]{2,1,0:T(8,128)S(1)} %get-tuple-element.96), channel_id=1, replica_groups=mesh['x'=4,'c'=2,'y'=4,'z'=8] {'z'}, dimensions={0} | all-to-all | bytes 65536 | tf_op jit(solution)/shard_map/all_to_all | solution.py:350
  91.9 5.0 %all-to-all-start.3 = ((f32[32,8,128]{2,1,0:T(8,128)}), f32[32,8,128]{2,1,0:T(8,128)S(1)}, u32[]{:S(2)}, u32[]{:S(2)}) async-start(f32[32,8,128]{2,1,0:T(8,128)} %shard_map.74), calls=%async_computation.5 | async-start | bytes 262144 | tf_op jit(solution)/shard_map/all_to_all | solution.py:357
  96.9 7.8 %all-to-all-done.3.parts = f32[32,8,128]{2,1,0:T(8,128)S(1)} async-done(((f32[32,8,128]{2,1,0:T(8,128)}), f32[32,8,128]{2,1,0:T(8,128)S(1)}, u32[]{:S(2)}, u32[]{:S(2)}) %all-to-all-start.3) | async-done | bytes 131104 | tf_op jit(solution)/shard_map/all_to_all | solution.py:357
  104.7 2.1 %shard_map.75 = (f32[8,128]{1,0:T(8,128)S(1)}, f32[8,128]{1,0:T(8,128)S(1)}, f32[8,128]{1,0:T(8,128)S(1)}, f32[8,128]{1,0:T(8,128)S(1)}, s32[1,1]{1,0:T(1,128)}) custom-call(f32[32,8,128]{2,1,0:T(8,128)S(1)} %all-to-all-done.3.parts), custom_call_target="tpu_custom_call" | custom-call | tf_op jit(solution)/shard_map/pallas_call | solution.py:94
  107.5 51.6 %conditional.1 = (f32[32,640]{1,0:T(8,128)}, f32[640,2432]{1,0:T(8,128)}) conditional(s32[]{:T(128)} %bitcast.14, (s32[128]{0:T(128)S(1)}, s32[5]{0:T(128)S(1)}, f32[128,2432]{1,0:T(8,128)S(1)}, f32[8,128]{1,0:T(8,128)S(1)}, f32[8,128]{1,0:T(8,128)S(1)}, /*index=5*/f32[8,128]{1,0:T(8,128)S(1)}, bf16[640,2432]{1,0:T(8,128)(2,1)}, ...), branch_computations={%region_0.1_spmd, %region_1.16_spmd} | conditional | flops 9566442496 | bytes 138560592 | solution.py:420
  109.9 1.5 collective-permute-start.1
  111.5 5.9 %collective-permute-done.2 = bf16[48,2432]{1,0:T(8,128)(2,1)S(1)} collective-permute-done((bf16[48,2432]{1,0:T(8,128)(2,1)S(1)}, bf16[48,2432]{1,0:T(8,128)(2,1)S(1)}, u32[]{:S(2)}, u32[]{:S(2)}) %collective-permute-start.2) | collective-permute-done | bytes 233504 | tf_op jit(solution)/shard_map/cond/branch_0_fun/ppermute | solution.py:375
  117.4 2.7 %collective-permute-done.1 = bf16[48,2432]{1,0:T(8,128)(2,1)S(1)} collective-permute-done((bf16[48,2432]{1,0:T(8,128)(2,1)S(1)}, bf16[48,2432]{1,0:T(8,128)(2,1)S(1)}, u32[]{:S(2)}, u32[]{:S(2)}) %collective-permute-start.1) | collective-permute-done | bytes 233504 | tf_op jit(solution)/shard_map/cond/branch_0_fun/ppermute | solution.py:375
  120.1 3.8 %collective-permute-done = bf16[48,2432]{1,0:T(8,128)(2,1)S(1)} collective-permute-done((bf16[48,2432]{1,0:T(8,128)(2,1)S(1)}, bf16[48,2432]{1,0:T(8,128)(2,1)S(1)}, u32[]{:S(2)}, u32[]{:S(2)}) %collective-permute-start) | collective-permute-done | bytes 233504 | tf_op jit(solution)/shard_map/cond/branch_0_fun/ppermute | solution.py:375
  124.2 2.5 %collective-permute-done.3.theirs = bf16[192,2432]{1,0:T(8,128)(2,1)S(1)} collective-permute-done((bf16[192,2432]{1,0:T(8,128)(2,1)S(1)}, bf16[192,2432]{1,0:T(8,128)(2,1)S(1)}, u32[]{:S(2)}, u32[]{:S(2)}) %collective-permute-start.3) | collective-permute-done | bytes 933920 | tf_op jit(solution)/shard_map/cond/branch_0_fun/ppermute | solution.py:377
  126.7 4.8 %branch_0_fun.5 = bf16[512,640]{1,0:T(8,128)(2,1)} custom-call(s32[5]{0:T(128)S(1)} %get-tuple-element.54.at, bf16[192,2432]{1,0:T(8,128)(2,1)S(1)} %pad_maximum_fusion.mine, bf16[192,2432]{1,0:T(8,128)(2,1)S(1)} %collective-permute-done.3.theirs, bf16[640,2432]{1,0:T(8,128)(2,1)S(1)} %copy-done, f32[8,128]{1,0:T(8,128)S(1)} %get-tuple-element.58.packed_all, ...), custom_call_target="tpu_custom_call" | custom-call | tf_op jit(solution)/shard_map/cond/branch_0_fun/pallas_call | solution.py:94
  131.5 5.0 %all-to-all-start = ((bf16[32,16,640]{2,1,0:T(8,128)(2,1)}), bf16[32,16,640]{2,1,0:T(8,128)(2,1)S(1)}, u32[]{:S(2)}, u32[]{:S(2)}) async-start(bf16[32,16,640]{2,1,0:T(8,128)(2,1)} %bitcast.1), calls=%async_computation | async-start | bytes 1310720 | tf_op jit(solution)/shard_map/cond/branch_0_fun/all_to_all | solution.py:385
  136.5 6.5 %branch_0_fun.7 = f32[640,2432]{1,0:T(8,128)} custom-call(s32[5]{0:T(128)S(1)} %get-tuple-element.54.at, f32[8,128]{1,0:T(8,128)S(1)} %get-tuple-element.58.packed_all, bf16[512,640]{1,0:T(8,128)(2,1)S(1)} %get-tuple-element.62.hid_mine, bf16[512,640]{1,0:T(8,128)(2,1)} %copy-done.4, bf16[192,2432]{1,0:T(8,128)(2,1)S(1)} %pad_maximum_fusion.mine, ...), custom_call_target="tpu_custom_call" | custom-call | flops 1195376640 | bytes 6225920 | tf_op jit(solution)/shard_map/cond/branch_0_fun/pallas_call | solution.py:387
  143.0 14.6 %all-to-all-done = bf16[32,16,640]{2,1,0:T(8,128)(2,1)S(1)} async-done(((bf16[32,16,640]{2,1,0:T(8,128)(2,1)}), bf16[32,16,640]{2,1,0:T(8,128)(2,1)S(1)}, u32[]{:S(2)}, u32[]{:S(2)}) %all-to-all-start) | async-done | bytes 655392 | tf_op jit(solution)/shard_map/cond/branch_0_fun/all_to_all | solution.py:385
  (29 shorter events, 8.4 us)
Async XLA Ops:
  7.2 22.0 %collective-permute-start.7 = (bf16[640,2432]{1,0:T(8,128)(2,1)}, bf16[640,2432]{1,0:T(8,128)(2,1)S(1)}, u32[]{:S(2)}, u32[]{:S(2)}) collective-permute-start(bf16[640,2432]{1,0:T(8,128)(2,1)} %head.1), channel_id=1, source_target_pairs={{0,32},{32,0},{1,33},{33,1},{2,34},{34,2},{3,35},{35,3},{4,36},{36... | collective-permute-start | bytes 9338888 | tf_op jit(solution)/shard_map/ppermute | solution.py:325
  9.6 11.6 %collective-permute-start.4 = (bf16[128,1280]{1,0:T(8,128)(2,1)}, bf16[128,1280]{1,0:T(8,128)(2,1)}, u32[]{:S(2)}, u32[]{:S(2)}) collective-permute-start(bf16[128,1280]{1,0:T(8,128)(2,1)} %get-tuple-element.145), channel_id=1, source_target_pairs={{0,64},{64,128},{128,192},{192,0},{1,65},{65,129},{129,193},{193,1... | collective-permute-start | bytes 983048 | tf_op jit(solution)/shard_map/ppermute | solution.py:330
  11.1 18.1 %collective-permute-start.5 = (bf16[128,1280]{1,0:T(8,128)(2,1)}, bf16[128,1280]{1,0:T(8,128)(2,1)}, u32[]{:S(2)}, u32[]{:S(2)}) collective-permute-start(bf16[128,1280]{1,0:T(8,128)(2,1)} %get-tuple-element.144), channel_id=1, source_target_pairs={{0,128},{64,192},{128,0},{192,64},{1,129},{65,193},{129,1},{193,65... | collective-permute-start | bytes 983048 | tf_op jit(solution)/shard_map/ppermute | solution.py:330
  13.8 15.4 %collective-permute-start.6 = (bf16[128,1280]{1,0:T(8,128)(2,1)}, bf16[128,1280]{1,0:T(8,128)(2,1)}, u32[]{:S(2)}, u32[]{:S(2)}) collective-permute-start(bf16[128,1280]{1,0:T(8,128)(2,1)} %get-tuple-element.143), channel_id=1, source_target_pairs={{0,192},{64,0},{128,64},{192,128},{1,193},{65,1},{129,65},{193,129... | collective-permute-start | bytes 983048 | tf_op jit(solution)/shard_map/ppermute | solution.py:330
  39.7 51.5 %copy-start.5 = (s32[128]{0:T(128)S(1)}, s32[128]{0:T(128)}, u32[]{:S(2)}) copy-start(s32[128]{0:T(128)} %param.12) | copy-start | bytes 1540
  39.7 51.5 %copy-start.6 = (f32[128]{0:T(128)S(1)}, f32[128]{0:T(128)}, u32[]{:S(2)}) copy-start(f32[128]{0:T(128)} %param.13) | copy-start | bytes 1540
  39.7 30.5 %collective-permute-start.8 = (s16[128,2560]{1,0:T(8,128)(2,1)S(1)}, s16[128,2560]{1,0:T(8,128)(2,1)S(1)}, u32[]{:S(2)}, u32[]{:S(2)}) collective-permute-start(s16[128,2560]{1,0:T(8,128)(2,1)S(1)} %get-tuple-element.93), channel_id=1, source_target_pairs={{0,192},{64,0},{128,64},{192,128},{1,193},{65,1},{129,65},{193,129... | collective-permute-start | bytes 1966088 | tf_op jit(solution)/shard_map/ppermute | solution.py:341
  41.9 28.3 %collective-permute-start.9 = (s16[128,2560]{1,0:T(8,128)(2,1)S(1)}, s16[128,2560]{1,0:T(8,128)(2,1)S(1)}, u32[]{:S(2)}, u32[]{:S(2)}) collective-permute-start(s16[128,2560]{1,0:T(8,128)(2,1)S(1)} %get-tuple-element.94), channel_id=1, source_target_pairs={{0,128},{64,192},{128,0},{192,64},{1,129},{65,193},{129,1},{193,65... | collective-permute-start | bytes 1966088 | tf_op jit(solution)/shard_map/ppermute | solution.py:341
  43.1 30.7 %collective-permute-start.10 = (s16[128,2560]{1,0:T(8,128)(2,1)S(1)}, s16[128,2560]{1,0:T(8,128)(2,1)S(1)}, u32[]{:S(2)}, u32[]{:S(2)}) collective-permute-start(s16[128,2560]{1,0:T(8,128)(2,1)S(1)} %get-tuple-element.95), channel_id=1, source_target_pairs={{0,64},{64,128},{128,192},{192,0},{1,65},{65,129},{129,193},{193,1... | collective-permute-start | bytes 1966088 | tf_op jit(solution)/shard_map/ppermute | solution.py:341
  43.7 63.7 %collective-permute-start.11 = (bf16[512,640]{1,0:T(8,128)(2,1)}, bf16[512,640]{1,0:T(8,128)(2,1)S(1)}, u32[]{:S(2)}, u32[]{:S(2)}) collective-permute-start(bf16[512,640]{1,0:T(8,128)(2,1)} %get-tuple-element.104), channel_id=1, source_target_pairs={{0,32},{32,0},{1,33},{33,1},{2,34},{34,2},{3,35},{35,3},{4,36},{36... | collective-permute-start | bytes 1966088 | tf_op jit(solution)/shard_map/ppermute | solution.py:342
  73.7 33.7 %copy-start.3 = (bf16[512,640]{1,0:T(8,128)(2,1)S(1)}, bf16[512,640]{1,0:T(8,128)(2,1)}, u32[]{:S(2)}) copy-start(bf16[512,640]{1,0:T(8,128)(2,1)} %get-tuple-element.103) | copy-start | bytes 1966084
  73.7 33.8 %copy-start.7 = (s32[128]{0:T(128)S(1)}, s32[128]{0:T(128)}, u32[]{:S(2)}) copy-start(s32[128]{0:T(128)} %param.11) | copy-start | bytes 1540
  91.9 12.9 %all-to-all-start.3 = ((f32[32,8,128]{2,1,0:T(8,128)}), f32[32,8,128]{2,1,0:T(8,128)S(1)}, u32[]{:S(2)}, u32[]{:S(2)}) async-start(f32[32,8,128]{2,1,0:T(8,128)} %shard_map.74), calls=%async_computation.5 | async-start | bytes 262144 | tf_op jit(solution)/shard_map/all_to_all | solution.py:357
  107.5 16.4 %copy-start.4 = (bf16[512,640]{1,0:T(8,128)(2,1)}, bf16[512,640]{1,0:T(8,128)(2,1)S(1)}, u32[]{:S(2)}) copy-start(bf16[512,640]{1,0:T(8,128)(2,1)S(1)} %get-tuple-element.63.hid_theirs) | copy-start | bytes 1966084 | tf_op jit(solution)/shard_map/cond
  107.5 19.2 %copy-start = (bf16[640,2432]{1,0:T(8,128)(2,1)S(1)}, bf16[640,2432]{1,0:T(8,128)(2,1)}, u32[]{:S(2)}) copy-start(bf16[640,2432]{1,0:T(8,128)(2,1)} %get-tuple-element.60.head) | copy-start | bytes 9338884 | tf_op jit(solution)/shard_map/cond
  108.7 8.6 %collective-permute-start.2 = (bf16[48,2432]{1,0:T(8,128)(2,1)S(1)}, bf16[48,2432]{1,0:T(8,128)(2,1)S(1)}, u32[]{:S(2)}, u32[]{:S(2)}) collective-permute-start(bf16[48,2432]{1,0:T(8,128)(2,1)S(1)} %branch_0_fun.4), channel_id=1, source_target_pairs={{0,192},{64,0},{128,64},{192,128},{1,193},{65,1},{129,65},{193,129... | collective-permute-start | bytes 700424 | tf_op jit(solution)/shard_map/cond/branch_0_fun/ppermute | solution.py:375
  109.9 10.1 %collective-permute-start.1 = (bf16[48,2432]{1,0:T(8,128)(2,1)S(1)}, bf16[48,2432]{1,0:T(8,128)(2,1)S(1)}, u32[]{:S(2)}, u32[]{:S(2)}) collective-permute-start(bf16[48,2432]{1,0:T(8,128)(2,1)S(1)} %branch_0_fun.4), channel_id=1, source_target_pairs={{0,128},{64,192},{128,0},{192,64},{1,129},{65,193},{129,1},{193,65... | collective-permute-start | bytes 700424 | tf_op jit(solution)/shard_map/cond/branch_0_fun/ppermute | solution.py:375
  111.5 12.4 %collective-permute-start = (bf16[48,2432]{1,0:T(8,128)(2,1)S(1)}, bf16[48,2432]{1,0:T(8,128)(2,1)S(1)}, u32[]{:S(2)}, u32[]{:S(2)}) collective-permute-start(bf16[48,2432]{1,0:T(8,128)(2,1)S(1)} %branch_0_fun.4), channel_id=1, source_target_pairs={{0,64},{64,128},{128,192},{192,0},{1,65},{65,129},{129,193},{193,1... | collective-permute-start | bytes 700424 | tf_op jit(solution)/shard_map/cond/branch_0_fun/ppermute | solution.py:375
  123.9 2.8 %collective-permute-start.3 = (bf16[192,2432]{1,0:T(8,128)(2,1)S(1)}, bf16[192,2432]{1,0:T(8,128)(2,1)S(1)}, u32[]{:S(2)}, u32[]{:S(2)}) collective-permute-start(bf16[192,2432]{1,0:T(8,128)(2,1)S(1)} %pad_maximum_fusion.mine), channel_id=1, source_target_pairs={{0,32},{32,0},{1,33},{33,1},{2,34},{34,2},{3,35},{35,3},{4,36},{36... | collective-permute-start | bytes 2801672 | tf_op jit(solution)/shard_map/cond/branch_0_fun/ppermute | solution.py:377
  131.5 26.1 %all-to-all-start = ((bf16[32,16,640]{2,1,0:T(8,128)(2,1)}), bf16[32,16,640]{2,1,0:T(8,128)(2,1)S(1)}, u32[]{:S(2)}, u32[]{:S(2)}) async-start(bf16[32,16,640]{2,1,0:T(8,128)(2,1)} %bitcast.1), calls=%async_computation | async-start | bytes 1310720 | tf_op jit(solution)/shard_map/cond/branch_0_fun/all_to_all | solution.py:385

commit v2 on v1

--- a/solution.py
+++ b/solution.py
@@ -12,6 +12,7 @@
 LEVELS = 6
 CAP = 16
 CAP_OWNER = 48
+ORDER = (0, 1, 3, 2)
 
 ramp_width = 0.5
 DP = ("x", "c")
@@ -105,24 +106,45 @@
     return jax.ShapeDtypeStruct(shape, dtype)
 
 
+def estimate(m, k, n):
+    return pl.CostEstimate(flops=2 * m * k * n, bytes_accessed=2 * k * n, transcendentals=0)
+
+
 LN2_64 = float(np.log(2.0) / 64.0)
 
 
-def partial_kernel(at, b0, b1, b2, b3, head, other, own, q1, q2, q3, mine, theirs, part):
-    tokens = b0.shape[0]
-    rows, cols = head.shape
-    here = pl.ds(pl.multiple_of(at[1] * rows, 128), rows)
-    there = pl.ds(pl.multiple_of((1 - at[1]) * rows, 128), rows)
-    for s, block in enumerate((b0, b1, b2, b3)):
-        mine[s * tokens : (s + 1) * tokens, :] = block[:, here]
-        theirs[s * tokens : (s + 1) * tokens, :] = block[:, there]
-
-    def tile(at_col, size):
-        span = pl.ds(at_col, size)
-        part[:, span] = jnp.dot(mine[...], head[:, span], preferred_element_type=f32) + jnp.dot(
-            theirs[...], other[:, span], preferred_element_type=f32
-        )
-
+def split_kernel(at, hidden, b0, b1, b2, b3):
+    chip_rows = b0.shape[1]
+    nx = hidden.shape[1] // chip_rows
+    for s, out in enumerate((b0, b1, b2, b3)):
+        to = lax.rem(at[0] + s, nx) * chip_rows
+        out[...] = hidden[:, pl.ds(pl.multiple_of(to, 128), chip_rows)]
+
+
+def turn_kernel(head, kept, turned):
+    kept[...] = head[...]
+    for k in range(head.shape[1] // 128):
+        span = slice(k * 128, (k + 1) * 128)
+        turned[span, :] = jnp.transpose(head[:, span])
+
+
+def pack(block, out, to):
+    step, cols = block.shape
+    top = jnp.maximum(jnp.max(jnp.abs(block), axis=1, keepdims=True), 1e-30)
+    power = jnp.ceil(jnp.log(top) * (1.0 / LN2_64)) + 1.0
+    fixed = jnp.round(block * (jnp.exp(power * -LN2_64) * 32766.0))
+    out[to, 0:cols] = fixed.astype(jnp.int32).astype(jnp.int16)
+    wide_power = jnp.broadcast_to(power.astype(jnp.int32), (step, 128))
+    out[to, cols : cols + 128] = wide_power.astype(jnp.int16)
+
+
+def unpack(ref, at):
+    cols = ref.shape[1] - 128
+    power = ref[at, cols : cols + 128].astype(jnp.int32).astype(f32)[:, :1]
+    return ref[at, 0:cols].astype(jnp.int32).astype(f32) * (jnp.exp(power * LN2_64) * (1.0 / 32766.0))
+
+
+def over_columns(cols, tile):
     wide = cols // 256
 
     @pl.loop(0, wide)
@@ -131,24 +153,73 @@
 
     if cols > wide * 256:
         tile(wide * 256, cols - wide * 256)
-    own[...] = part[0:tokens, :]
+
+
+def halves(at, rows):
+    return (
+        pl.ds(pl.multiple_of(at[1] * rows, 128), rows),
+        pl.ds(pl.multiple_of((1 - at[1]) * rows, 128), rows),
+    )
+
+
+def far_kernel(at, block, head, other, low, high, tick, part):
+    tokens = block.shape[0]
+    rows, cols = head.shape
+    here, there = halves(at, rows)
+
+    def tile(start, size):
+        span = pl.ds(start, size)
+        part[:, span] = jnp.dot(block[:, here], head[:, span], preferred_element_type=f32) + jnp.dot(
+            block[:, there], other[:, span], preferred_element_type=f32
+        )
+
+    over_columns(cols, tile)
+    tick[...] = jnp.zeros(tick.shape, f32)
     step = 32
-    for s, out in ((1, q1), (2, q2), (3, q3)):
-
-        @pl.loop(0, tokens // step)
-        def _(i, s=s, out=out):
-            to = pl.ds(pl.multiple_of(i * step, step), step)
-            block = part[pl.ds(pl.multiple_of(s * tokens + i * step, step), step), :]
-            top = jnp.maximum(jnp.max(jnp.abs(block), axis=1, keepdims=True), 1e-30)
-            power = jnp.ceil(jnp.log(top) * (1.0 / LN2_64)) + 1.0
-            fixed = jnp.round(block * (jnp.exp(power * -LN2_64) * 32766.0))
-            out[to, 0:cols] = fixed.astype(jnp.int32).astype(jnp.int16)
-            wide_power = jnp.broadcast_to(power.astype(jnp.int32), (step, 128))
-            out[to, cols : cols + 128] = wide_power.astype(jnp.int16)
-
-
-def total_kernel(own, q1, q2, q3, logits, sent, stats):
-    tokens, cols = own.shape
+    for k, out in enumerate((low, high)):
+
+        @pl.loop(0, tokens // 2 // step)
+        def _(i, k=k, out=out):
+            source = pl.multiple_of(k * (tokens // 2) + i * step, step)
+            pack(part[pl.ds(source, step), :], out, pl.ds(pl.multiple_of(i * step, step), step))
+
+
+def near_kernel(at, tick, b0, b1, b2, b3, head, other, own, p1, p3, mine, theirs):
+    tokens = b0.shape[0]
+    rows, cols = head.shape
+    here, there = halves(at, rows)
+    for k, block in enumerate((b0, b1, b3, b2)):
+        mine[k * tokens : (k + 1) * tokens, :] = block[:, here]
+        theirs[k * tokens : (k + 1) * tokens, :] = block[:, there]
+
+    def tile(start, size):
+        span = pl.ds(start, size)
+        part = jnp.dot(mine[0 : 3 * tokens, :], head[:, span], preferred_element_type=f32) + jnp.dot(
+            theirs[0 : 3 * tokens, :], other[:, span], preferred_element_type=f32
+        )
+        own[:, span] = part[0:tokens, :]
+        p1[:, span] = part[tokens : 2 * tokens, :]
+        p3[:, span] = part[2 * tokens :, :]
+
+    over_columns(cols, tile)
+
+
+def relay_kernel(p1, p3, low, high, q1, q3):
+    tokens = p1.shape[0]
+    half, step = tokens // 2, 32
+
+    @pl.loop(0, half // step)
+    def _(i):
+        near = pl.ds(pl.multiple_of(i * step, step), step)
+        far = pl.ds(pl.multiple_of(half + i * step, step), step)
+        pack(p1[near, :] + unpack(low, near), q1, near)
+        pack(p1[far, :], q1, far)
+        pack(p3[near, :], q3, near)
+        pack(p3[far, :] + unpack(high, near), q3, far)
+
+
+def total_kernel(own, q1, q3, logits, sent, stats):
+    tokens = own.shape[0]
     step = 16
     lane = lax.broadcasted_iota(jnp.int32, (step, 128), 1)
 
@@ -156,10 +227,7 @@
     def _(i):
         at = pl.ds(pl.multiple_of(i * step, step), step)
         value = own[at, :]
-        for q in (q1, q2, q3):
-            power = q[at, cols : cols + 128].astype(jnp.int32).astype(f32)[:, :1]
-            scale = jnp.exp(power * LN2_64) * (1.0 / 32766.0)
-            value = value + q[at, 0:cols].astype(jnp.int32).astype(f32) * scale
+        value = value + unpack(q1, at) + unpack(q3, at)
         logits[at, :] = value
         high = jnp.max(value, axis=1, keepdims=True)
         shifted = jnp.exp(value - high)
@@ -252,12 +320,12 @@
         out[:, span] = jnp.dot(choose, slopes, preferred_element_type=f32).astype(bf16)
 
 
-def product_kernel(nx, at, mine, theirs, head, packed_all, slot_all, out, held):
+def product_kernel(nx, at, mine, theirs, turned, packed_all, slot_all, out, held):
     half = mine.shape[0]
     count = half // nx
     for k, rows in enumerate((mine, theirs)):
         held[k * half : (k + 1) * half, :] = lax.dot_general(
-            rows[...], head[...], (((1,), (1,)), ((), ())), preferred_element_type=f32
+            rows[...], turned[...], (((1,), (0,)), ((), ())), preferred_element_type=f32
         ).astype(bf16)
     size = out.shape[0] // (2 * nx)
     for owner in range(2 * nx):
@@ -284,7 +352,7 @@
             choose = one_hot(count, packed_all[pl.ds(owner, 1), :])
             to = k * half + s * count
             held[to : to + count, :] = jnp.dot(
-                choose, hidden[s * 128 : (s + 1) * 128, :], preferred_element_type=f32
+                choose, hidden[ORDER[s] * 128 : (ORDER[s] + 1) * 128, :], preferred_element_type=f32
             ).astype(bf16)
     total = jnp.zeros(out.shape, f32)
     for k, rows in enumerate((mine, theirs)):
@@ -324,26 +392,39 @@
 
     head_other = lax.ppermute(head, "c", SWAP)
 
-    def block_for(to):
-        return lax.dynamic_slice(hidden_states, (0, to * chip_rows), (tokens, chip_rows))
-
-    came = {s: lax.ppermute(block_for((x + s) % nx), "x", ring(nx, s)) for s in (2, 1, 3)}
+    block_shape = struct((tokens, chip_rows), bf16)
+    b0, *leave = call(split_kernel, [block_shape] * 4, [at, hidden_states], smem=1)
+    came = {s: lax.ppermute(leave[s - 1], "x", ring(nx, s)) for s in (2, 1, 3)}
+    kept, turned = call(
+        turn_kernel, [struct((rows, voc_cols), bf16), struct((voc_cols, rows), bf16)], [head]
+    )
+    half = struct((tokens // 2, voc_cols + 128), jnp.int16)
+    low, high, tick = call(
+        far_kernel,
+        [half, half, struct((8, 128), f32)],
+        [at, came[2], kept, head_other],
+        [pltpu.VMEM((tokens, voc_cols), f32)],
+        smem=1,
+        cost_estimate=estimate(tokens, chip_rows, voc_cols),
+    )
+    low, high = lax.ppermute(low, "x", ring(nx, -1)), lax.ppermute(high, "x", ring(nx, 1))
+    partial = struct((tokens, voc_cols), f32)
+    own, p1, p3, hid_mine, hid_send = call(
+        near_kernel,
+        [partial] * 3 + [struct((nx * tokens, rows), bf16)] * 2,
+        [at, tick, b0, came[1], came[2], came[3], kept, head_other],
+        vmem=24,
+        smem=1,
+        cost_estimate=estimate(3 * tokens, chip_rows, voc_cols),
+    )
     packed = struct((tokens, voc_cols + 128), jnp.int16)
-    own, q1, q2, q3, hid_mine, hid_send = call(
-        partial_kernel,
-        [struct((tokens, voc_cols), f32), packed, packed, packed]
-        + [struct((nx * tokens, rows), bf16)] * 2,
-        [at, block_for(x), came[1], came[2], came[3], head, head_other],
-        [pltpu.VMEM((nx * tokens, voc_cols), f32)],
-        vmem=32,
-        smem=1,
-    )
-    sent = {s: lax.ppermute(q, "x", ring(nx, -s)) for s, q in ((2, q2), (1, q1), (3, q3))}
+    q1, q3 = call(relay_kernel, [packed] * 2, [p1, p3, low, high])
+    q1, q3 = lax.ppermute(q1, "x", ring(nx, -1)), lax.ppermute(q3, "x", ring(nx, 1))
     hid_theirs = lax.ppermute(hid_send, "c", SWAP)
     logits, stats = call(
         total_kernel,
-        [struct((tokens, voc_cols), f32), struct((lax.axis_size("z"), 8, 128), f32)],
-        [own, sent[1], sent[2], sent[3]],
+        [partial, struct((lax.axis_size("z"), 8, 128), f32)],
+        [own, q1, q3],
         [pltpu.VMEM((tokens, 128), f32)],
     )
 
@@ -378,7 +459,7 @@
         product = call(
             functools.partial(product_kernel, nx),
             struct((n_voc * CAP, rows), bf16),
-            [at, mine, theirs, head, packed_all, slot_all],
+            [at, mine, theirs, turned, packed_all, slot_all],
             [pltpu.VMEM((2 * nx * CAP_OWNER, rows), bf16)],
             smem=1,
         )

time: 166 us -> 146 us (0.88)
  waiting for transfers between devices: 81.1 us -> 56.7 us
  Pallas kernels: 29.7 us -> 35 us
  local copies, waits for them, and re-layouts: 2.36 us -> 0.12 us
    ppermute x6 -> x7, waiting for transfers between devices: 43.8 us -> 19.4 us  [the longest x1 12.7 us: shards(): lax.ppermute(q1, 'x', ring(nx, -1))]
    pallas_call x7 -> x11, Pallas kernels: 23.2 us -> 28.5 us  [call(): pl.pallas_call(kernel, in_specs=specs, out_shape=out, scratch_shapes=list...]
    dynamic_slice x1 -> x0, local copies, waits for them, and re-layouts: 2.25 us -> none  [block_for(): lax.dynamic_slice(hidden_states, (0, to * chip_rows), (tokens, chip_rows))]
    ppermute x6 -> x7, starting transfers between devices: 9.73 us -> 11.3 us  [the longest x3 6.35 us: shards(): came = {s: lax.ppermute(leave[s - 1], 'x', ring(nx, s)) for s in (2, 1, 3)}]
  transfers between devices with their start and end apart: 14 -> 15, of which waited for: 10 -> 12; matrix products, arithmetic and copies ran while one was open for 1% -> 0% of each run, Pallas kernels for 7% -> 19%
where the time goes in v2:
time: 146 us
  waiting for transfers between devices  56.7 us (39%)
  Pallas kernels  35 us (24%)
  starting transfers between devices  24.1 us (17%)
  blocking collectives  15 us (10%)
  between operations  14.8 us (10%)
    pallas_call x11, Pallas kernels, call(): pl.pallas_call(kernel, in_specs=specs, out_shape=out, scratch_shapes=list...  28.5 us
    all_to_all x1, blocking collectives, shards(): stats = lax.all_to_all(stats, 'z', 0, 0, tiled=True)  15 us
    all_to_all x1, waiting for transfers between devices, sparse(): parts = lax.all_to_all(product, VOC, 0, 0, tiled=True)  14.5 us
    ppermute x1, waiting for transfers between devices, shards(): lax.ppermute(q1, 'x', ring(nx, -1))  12.7 us
    ppermute x3, waiting for transfers between devices, sparse(): pieces = {s: lax.ppermute(piece, 'x', ring(nx, s)) for s in (2, 1, 3)}  12.4 us
    all_to_all x1, waiting for transfers between devices, shards(): stats = lax.all_to_all(stats, everyone, 0, 0, tiled=True)  7.83 us
    pallas_call x1, Pallas kernels, sparse(): pl.pallas_call(functools.partial(outer_kernel, nx), grid=(rows // tile,),...  6.51 us
    ppermute x3, starting transfers between devices, shards(): came = {s: lax.ppermute(leave[s - 1], 'x', ring(nx, s)) for s in (2, 1, 3)}  6.35 us
  transfers between devices with their start and end apart: 15, of which 12 were waited for; matrix products, arithmetic and copies ran while one was open for 0% of the time, Pallas kernels for 19%

profile of v2, /device:TPU:32, one launch (start us, length us, event | category | flops | bytes accessed | tf_op | source)
XLA Modules:
  0.0 145.8 jit_solution(8296359134419597604)
XLA Ops:
  8.8 3.1 %collective-permute-start.4 = (bf16[128,1280]{1,0:T(8,128)(2,1)S(1)}, bf16[128,1280]{1,0:T(8,128)(2,1)S(1)}, u32[]{:S(2)}, u32[]{:S(2)}) collective-permute-start(bf16[128,1280]{1,0:T(8,128)(2,1)S(1)} %get-tuple-element.102), channel_id=1, source_target_pairs={{0,128},{64,192},{128,0},{192,64},{1,129},{65,193},{129,1},{193,65... | collective-permute-start | bytes 983048 | tf_op jit(solution)/shard_map/ppermute | solution.py:397
  12.5 2.6 %collective-permute-start.7 = (bf16[128,1280]{1,0:T(8,128)(2,1)S(1)}, bf16[128,1280]{1,0:T(8,128)(2,1)S(1)}, u32[]{:S(2)}, u32[]{:S(2)}) collective-permute-start(bf16[128,1280]{1,0:T(8,128)(2,1)S(1)} %get-tuple-element.107), channel_id=1, source_target_pairs={{0,192},{64,0},{128,64},{192,128},{1,193},{65,1},{129,65},{193,129... | collective-permute-start | bytes 983048 | tf_op jit(solution)/shard_map/ppermute | solution.py:397
  15.1 4.7 %shard_map.73 = (bf16[640,2432]{1,0:T(8,128)(2,1)S(1)}, bf16[2432,640]{1,0:T(8,128)(2,1)}) custom-call(bf16[640,2432]{1,0:T(8,128)(2,1)} %head.1), custom_call_target="tpu_custom_call" | custom-call | tf_op jit(solution)/shard_map/pallas_call | solution.py:95
  20.9 3.7 %shard_map.74 = (s16[64,2560]{1,0:T(8,128)(2,1)S(1)}, s16[64,2560]{1,0:T(8,128)(2,1)S(1)}, f32[8,128]{1,0:T(8,128)S(1)}) custom-call(s32[5]{0:T(128)S(1)} %stack.23.at, bf16[128,1280]{1,0:T(8,128)(2,1)S(1)} %collective-permute-done.4.block.b2, bf16[640,2432]{1,0:T(8,128)(2,1)S(1)} %get-tuple-element.103.head, bf16[640,2432]{1,0:T(8,128)(2,1)S(1)} %collective-permute-done.5.other), custom_call_target="tpu_custom_call" | custom-call | flops 796917760 | bytes 6225920 | tf_op jit(solution)/shard_map/pallas_call | solution.py:95
  24.6 2.8 %collective-permute-start.8 = (s16[64,2560]{1,0:T(8,128)(2,1)S(1)}, s16[64,2560]{1,0:T(8,128)(2,1)S(1)}, u32[]{:S(2)}, u32[]{:S(2)}) collective-permute-start(s16[64,2560]{1,0:T(8,128)(2,1)S(1)} %get-tuple-element.111), channel_id=1, source_target_pairs={{0,192},{64,0},{128,64},{192,128},{1,193},{65,1},{129,65},{193,129... | collective-permute-start | bytes 983048 | tf_op jit(solution)/shard_map/ppermute | solution.py:410
  28.0 5.9 %shard_map.75 = (f32[128,2432]{1,0:T(8,128)S(1)}, f32[128,2432]{1,0:T(8,128)S(1)}, f32[128,2432]{1,0:T(8,128)S(1)}, bf16[512,640]{1,0:T(8,128)(2,1)}, bf16[512,640]{1,0:T(8,128)(2,1)}) custom-call(s32[5]{0:T(128)S(1)} %stack.23.at, f32[8,128]{1,0:T(8,128)S(1)} %get-tuple-element.104.tick, bf16[128,1280]{1,0:T(8,128)(2,1)S(1)} %get-tuple-element.105.b0, ...), custom_call_target="tpu_custom_call" | custom-call | flops 2390753280 | bytes 6225920 | tf_op jit(solution)/shard_map/pallas_call | solution.py:95
  34.7 2.7 %collective-permute-done.9.high = s16[64,2560]{1,0:T(8,128)(2,1)S(1)} collective-permute-done((s16[64,2560]{1,0:T(8,128)(2,1)S(1)}, s16[64,2560]{1,0:T(8,128)(2,1)S(1)}, u32[]{:S(2)}, u32[]{:S(2)}) %collective-permute-start.9) | collective-permute-done | bytes 327712 | tf_op jit(solution)/shard_map/ppermute | solution.py:410
  38.4 1.7 %collective-permute-start.11 = (s16[128,2560]{1,0:T(8,128)(2,1)S(1)}, s16[128,2560]{1,0:T(8,128)(2,1)S(1)}, u32[]{:S(2)}, u32[]{:S(2)}) collective-permute-start(s16[128,2560]{1,0:T(8,128)(2,1)S(1)} %get-tuple-element.114), channel_id=1, source_target_pairs={{0,64},{64,128},{128,192},{192,0},{1,65},{65,129},{129,193},{193,1... | collective-permute-start | bytes 1966088 | tf_op jit(solution)/shard_map/ppermute | solution.py:422
  40.2 12.7 %collective-permute-done.10.q1 = s16[128,2560]{1,0:T(8,128)(2,1)S(1)} collective-permute-done((s16[128,2560]{1,0:T(8,128)(2,1)S(1)}, s16[128,2560]{1,0:T(8,128)(2,1)S(1)}, u32[]{:S(2)}, u32[]{:S(2)}) %collective-permute-start.10) | collective-permute-done | bytes 655392 | tf_op jit(solution)/shard_map/ppermute | solution.py:422
  52.9 1.7 %collective-permute-done.11.q3 = s16[128,2560]{1,0:T(8,128)(2,1)S(1)} collective-permute-done((s16[128,2560]{1,0:T(8,128)(2,1)S(1)}, s16[128,2560]{1,0:T(8,128)(2,1)S(1)}, u32[]{:S(2)}, u32[]{:S(2)}) %collective-permute-start.11) | collective-permute-done | bytes 655392 | tf_op jit(solution)/shard_map/ppermute | solution.py:422
  54.6 2.4 %shard_map.77 = (f32[128,2432]{1,0:T(8,128)S(1)}, f32[8,8,128]{2,1,0:T(8,128)S(1)}) custom-call(f32[128,2432]{1,0:T(8,128)S(1)} %get-tuple-element.108.own, s16[128,2560]{1,0:T(8,128)(2,1)S(1)} %collective-permute-done.10.q1, s16[128,2560]{1,0:T(8,128)(2,1)S(1)} %collective-permute-done.11.q3), custom_call_target="tpu_custom_call" | custom-call | tf_op jit(solution)/shard_map/pallas_call | solution.py:95
  57.0 15.0 %all_to_all.34.parts = f32[8,8,128]{2,1,0:T(8,128)S(1)} all-to-all(f32[8,8,128]{2,1,0:T(8,128)S(1)} %get-tuple-element.115), channel_id=1, replica_groups=mesh['x'=4,'c'=2,'y'=4,'z'=8] {'z'}, dimensions={0} | all-to-all | bytes 65536 | tf_op jit(solution)/shard_map/all_to_all | solution.py:431
  72.6 4.9 %all-to-all-start.3 = ((f32[32,8,128]{2,1,0:T(8,128)}), f32[32,8,128]{2,1,0:T(8,128)S(1)}, u32[]{:S(2)}, u32[]{:S(2)}) async-start(f32[32,8,128]{2,1,0:T(8,128)} %shard_map.78), calls=%async_computation.5 | async-start | bytes 262144 | tf_op jit(solution)/shard_map/all_to_all | solution.py:438
  77.5 7.8 %all-to-all-done.3.parts = f32[32,8,128]{2,1,0:T(8,128)S(1)} async-done(((f32[32,8,128]{2,1,0:T(8,128)}), f32[32,8,128]{2,1,0:T(8,128)S(1)}, u32[]{:S(2)}, u32[]{:S(2)}) %all-to-all-start.3) | async-done | bytes 131104 | tf_op jit(solution)/shard_map/all_to_all | solution.py:438
  85.3 2.1 %shard_map.79 = (f32[8,128]{1,0:T(8,128)S(1)}, f32[8,128]{1,0:T(8,128)S(1)}, f32[8,128]{1,0:T(8,128)S(1)}, f32[8,128]{1,0:T(8,128)S(1)}, s32[1,1]{1,0:T(1,128)}) custom-call(f32[32,8,128]{2,1,0:T(8,128)S(1)} %all-to-all-done.3.parts), custom_call_target="tpu_custom_call" | custom-call | tf_op jit(solution)/shard_map/pallas_call | solution.py:95
  88.1 50.8 %conditional.1 = (f32[32,640]{1,0:T(8,128)}, f32[640,2432]{1,0:T(8,128)}) conditional(s32[]{:T(128)} %bitcast.14, (s32[128]{0:T(128)S(1)}, s32[5]{0:T(128)S(1)}, f32[128,2432]{1,0:T(8,128)S(1)}, f32[8,128]{1,0:T(8,128)S(1)}, f32[8,128]{1,0:T(8,128)S(1)}, /*index=5*/f32[8,128]{1,0:T(8,128)S(1)}, bf16[2432,640]{1,0:T(8,128)(2,1)}, ...), branch_computations={%region_0.0_spmd, %region_1.16_spmd} | conditional | flops 9566442496 | bytes 125846592 | solution.py:501
  92.1 5.9 %collective-permute-done.2 = bf16[48,2432]{1,0:T(8,128)(2,1)S(1)} collective-permute-done((bf16[48,2432]{1,0:T(8,128)(2,1)S(1)}, bf16[48,2432]{1,0:T(8,128)(2,1)S(1)}, u32[]{:S(2)}, u32[]{:S(2)}) %collective-permute-start.2) | collective-permute-done | bytes 233504 | tf_op jit(solution)/shard_map/cond/branch_0_fun/ppermute | solution.py:456
  98.0 2.7 %collective-permute-done.1 = bf16[48,2432]{1,0:T(8,128)(2,1)S(1)} collective-permute-done((bf16[48,2432]{1,0:T(8,128)(2,1)S(1)}, bf16[48,2432]{1,0:T(8,128)(2,1)S(1)}, u32[]{:S(2)}, u32[]{:S(2)}) %collective-permute-start.1) | collective-permute-done | bytes 233504 | tf_op jit(solution)/shard_map/cond/branch_0_fun/ppermute | solution.py:456
  100.7 3.8 %collective-permute-done = bf16[48,2432]{1,0:T(8,128)(2,1)S(1)} collective-permute-done((bf16[48,2432]{1,0:T(8,128)(2,1)S(1)}, bf16[48,2432]{1,0:T(8,128)(2,1)S(1)}, u32[]{:S(2)}, u32[]{:S(2)}) %collective-permute-start) | collective-permute-done | bytes 233504 | tf_op jit(solution)/shard_map/cond/branch_0_fun/ppermute | solution.py:456
  104.6 2.5 %collective-permute-done.3.theirs = bf16[192,2432]{1,0:T(8,128)(2,1)S(1)} collective-permute-done((bf16[192,2432]{1,0:T(8,128)(2,1)S(1)}, bf16[192,2432]{1,0:T(8,128)(2,1)S(1)}, u32[]{:S(2)}, u32[]{:S(2)}) %collective-permute-start.3) | collective-permute-done | bytes 933920 | tf_op jit(solution)/shard_map/cond/branch_0_fun/ppermute | solution.py:458
  107.1 4.2 %branch_0_fun.5 = bf16[512,640]{1,0:T(8,128)(2,1)} custom-call(s32[5]{0:T(128)S(1)} %get-tuple-element.54.at, bf16[192,2432]{1,0:T(8,128)(2,1)S(1)} %pad_maximum_fusion.mine, bf16[192,2432]{1,0:T(8,128)(2,1)S(1)} %collective-permute-done.3.theirs, bf16[2432,640]{1,0:T(8,128)(2,1)S(1)} %copy-done.1, f32[8,128]{1,0:T(8,128)S(1)} %get-tuple-element.58.packed_all, ...), custom_call_target="tpu_custom_call" | custom-call | tf_op jit(solution)/shard_map/cond/branch_0_fun/pallas_call | solution.py:95
  111.4 5.0 %all-to-all-start = ((bf16[32,16,640]{2,1,0:T(8,128)(2,1)}), bf16[32,16,640]{2,1,0:T(8,128)(2,1)S(1)}, u32[]{:S(2)}, u32[]{:S(2)}) async-start(bf16[32,16,640]{2,1,0:T(8,128)(2,1)} %bitcast.1), calls=%async_computation | async-start | bytes 1310720 | tf_op jit(solution)/shard_map/cond/branch_0_fun/all_to_all | solution.py:466
  116.4 6.5 %branch_0_fun.7 = f32[640,2432]{1,0:T(8,128)} custom-call(s32[5]{0:T(128)S(1)} %get-tuple-element.54.at, f32[8,128]{1,0:T(8,128)S(1)} %get-tuple-element.58.packed_all, bf16[512,640]{1,0:T(8,128)(2,1)S(1)} %get-tuple-element.62.hid_mine, bf16[512,640]{1,0:T(8,128)(2,1)} %copy-done.3, bf16[192,2432]{1,0:T(8,128)(2,1)S(1)} %pad_maximum_fusion.mine, ...), custom_call_target="tpu_custom_call" | custom-call | flops 1195376640 | bytes 6225920 | tf_op jit(solution)/shard_map/cond/branch_0_fun/pallas_call | solution.py:468
  122.9 14.5 %all-to-all-done = bf16[32,16,640]{2,1,0:T(8,128)(2,1)S(1)} async-done(((bf16[32,16,640]{2,1,0:T(8,128)(2,1)}), bf16[32,16,640]{2,1,0:T(8,128)(2,1)S(1)}, u32[]{:S(2)}, u32[]{:S(2)}) %all-to-all-start) | async-done | bytes 655392 | tf_op jit(solution)/shard_map/cond/branch_0_fun/all_to_all | solution.py:466
  (34 shorter events, 12.0 us)
Async XLA Ops:
  7.2 13.8 %collective-permute-start.5 = (bf16[640,2432]{1,0:T(8,128)(2,1)}, bf16[640,2432]{1,0:T(8,128)(2,1)S(1)}, u32[]{:S(2)}, u32[]{:S(2)}) collective-permute-start(bf16[640,2432]{1,0:T(8,128)(2,1)} %head.1), channel_id=1, source_target_pairs={{0,32},{32,0},{1,33},{33,1},{2,34},{34,2},{3,35},{35,3},{4,36},{36... | collective-permute-start | bytes 9338888 | tf_op jit(solution)/shard_map/ppermute | solution.py:393
  8.8 12.1 %collective-permute-start.4 = (bf16[128,1280]{1,0:T(8,128)(2,1)S(1)}, bf16[128,1280]{1,0:T(8,128)(2,1)S(1)}, u32[]{:S(2)}, u32[]{:S(2)}) collective-permute-start(bf16[128,1280]{1,0:T(8,128)(2,1)S(1)} %get-tuple-element.102), channel_id=1, source_target_pairs={{0,128},{64,192},{128,0},{192,64},{1,129},{65,193},{129,1},{193,65... | collective-permute-start | bytes 983048 | tf_op jit(solution)/shard_map/ppermute | solution.py:397
  11.9 15.6 %collective-permute-start.6 = (bf16[128,1280]{1,0:T(8,128)(2,1)S(1)}, bf16[128,1280]{1,0:T(8,128)(2,1)S(1)}, u32[]{:S(2)}, u32[]{:S(2)}) collective-permute-start(bf16[128,1280]{1,0:T(8,128)(2,1)S(1)} %get-tuple-element.106), channel_id=1, source_target_pairs={{0,64},{64,128},{128,192},{192,0},{1,65},{65,129},{129,193},{193,1... | collective-permute-start | bytes 983048 | tf_op jit(solution)/shard_map/ppermute | solution.py:397
  12.5 15.5 %collective-permute-start.7 = (bf16[128,1280]{1,0:T(8,128)(2,1)S(1)}, bf16[128,1280]{1,0:T(8,128)(2,1)S(1)}, u32[]{:S(2)}, u32[]{:S(2)}) collective-permute-start(bf16[128,1280]{1,0:T(8,128)(2,1)S(1)} %get-tuple-element.107), channel_id=1, source_target_pairs={{0,192},{64,0},{128,64},{192,128},{1,193},{65,1},{129,65},{193,129... | collective-permute-start | bytes 983048 | tf_op jit(solution)/shard_map/ppermute | solution.py:397
  24.6 10.0 %collective-permute-start.8 = (s16[64,2560]{1,0:T(8,128)(2,1)S(1)}, s16[64,2560]{1,0:T(8,128)(2,1)S(1)}, u32[]{:S(2)}, u32[]{:S(2)}) collective-permute-start(s16[64,2560]{1,0:T(8,128)(2,1)S(1)} %get-tuple-element.111), channel_id=1, source_target_pairs={{0,192},{64,0},{128,64},{192,128},{1,193},{65,1},{129,65},{193,129... | collective-permute-start | bytes 983048 | tf_op jit(solution)/shard_map/ppermute | solution.py:410
  27.5 9.8 %collective-permute-start.9 = (s16[64,2560]{1,0:T(8,128)(2,1)S(1)}, s16[64,2560]{1,0:T(8,128)(2,1)S(1)}, u32[]{:S(2)}, u32[]{:S(2)}) collective-permute-start(s16[64,2560]{1,0:T(8,128)(2,1)S(1)} %get-tuple-element.112), channel_id=1, source_target_pairs={{0,64},{64,128},{128,192},{192,0},{1,65},{65,129},{129,193},{193,1... | collective-permute-start | bytes 983048 | tf_op jit(solution)/shard_map/ppermute | solution.py:410
  38.0 33.9 %copy-start.4 = (s32[128]{0:T(128)S(1)}, s32[128]{0:T(128)}, u32[]{:S(2)}) copy-start(s32[128]{0:T(128)} %param.12) | copy-start | bytes 1540
  38.1 33.9 %copy-start.5 = (f32[128]{0:T(128)S(1)}, f32[128]{0:T(128)}, u32[]{:S(2)}) copy-start(f32[128]{0:T(128)} %param.13) | copy-start | bytes 1540
  38.1 50.0 %copy-start.2 = (bf16[512,640]{1,0:T(8,128)(2,1)S(1)}, bf16[512,640]{1,0:T(8,128)(2,1)}, u32[]{:S(2)}) copy-start(bf16[512,640]{1,0:T(8,128)(2,1)} %get-tuple-element.123) | copy-start | bytes 1966084
  38.1 50.0 %copy-start.6 = (s32[128]{0:T(128)S(1)}, s32[128]{0:T(128)}, u32[]{:S(2)}) copy-start(s32[128]{0:T(128)} %param.11) | copy-start | bytes 1540
  38.1 14.8 %collective-permute-start.10 = (s16[128,2560]{1,0:T(8,128)(2,1)S(1)}, s16[128,2560]{1,0:T(8,128)(2,1)S(1)}, u32[]{:S(2)}, u32[]{:S(2)}) collective-permute-start(s16[128,2560]{1,0:T(8,128)(2,1)S(1)} %get-tuple-element.113), channel_id=1, source_target_pairs={{0,192},{64,0},{128,64},{192,128},{1,193},{65,1},{129,65},{193,129... | collective-permute-start | bytes 1966088 | tf_op jit(solution)/shard_map/ppermute | solution.py:422
  38.4 16.1 %collective-permute-start.11 = (s16[128,2560]{1,0:T(8,128)(2,1)S(1)}, s16[128,2560]{1,0:T(8,128)(2,1)S(1)}, u32[]{:S(2)}, u32[]{:S(2)}) collective-permute-start(s16[128,2560]{1,0:T(8,128)(2,1)S(1)} %get-tuple-element.114), channel_id=1, source_target_pairs={{0,64},{64,128},{128,192},{192,0},{1,65},{65,129},{129,193},{193,1... | collective-permute-start | bytes 1966088 | tf_op jit(solution)/shard_map/ppermute | solution.py:422
  40.2 47.9 %collective-permute-start.12 = (bf16[512,640]{1,0:T(8,128)(2,1)}, bf16[512,640]{1,0:T(8,128)(2,1)S(1)}, u32[]{:S(2)}, u32[]{:S(2)}) collective-permute-start(bf16[512,640]{1,0:T(8,128)(2,1)} %get-tuple-element.124), channel_id=1, source_target_pairs={{0,32},{32,0},{1,33},{33,1},{2,34},{34,2},{3,35},{35,3},{4,36},{36... | collective-permute-start | bytes 1966088 | tf_op jit(solution)/shard_map/ppermute | solution.py:423
  72.6 12.7 %all-to-all-start.3 = ((f32[32,8,128]{2,1,0:T(8,128)}), f32[32,8,128]{2,1,0:T(8,128)S(1)}, u32[]{:S(2)}, u32[]{:S(2)}) async-start(f32[32,8,128]{2,1,0:T(8,128)} %shard_map.78), calls=%async_computation.5 | async-start | bytes 262144 | tf_op jit(solution)/shard_map/all_to_all | solution.py:438
  88.1 16.4 %copy-start.3 = (bf16[512,640]{1,0:T(8,128)(2,1)}, bf16[512,640]{1,0:T(8,128)(2,1)S(1)}, u32[]{:S(2)}) copy-start(bf16[512,640]{1,0:T(8,128)(2,1)S(1)} %get-tuple-element.63.hid_theirs) | copy-start | bytes 1966084 | tf_op jit(solution)/shard_map/cond
  88.1 19.0 %copy-start.1 = (bf16[2432,640]{1,0:T(8,128)(2,1)S(1)}, bf16[2432,640]{1,0:T(8,128)(2,1)}, u32[]{:S(2)}) copy-start(bf16[2432,640]{1,0:T(8,128)(2,1)} %get-tuple-element.60.turned) | copy-start | bytes 9338884 | tf_op jit(solution)/shard_map/cond
  89.3 8.6 %collective-permute-start.2 = (bf16[48,2432]{1,0:T(8,128)(2,1)S(1)}, bf16[48,2432]{1,0:T(8,128)(2,1)S(1)}, u32[]{:S(2)}, u32[]{:S(2)}) collective-permute-start(bf16[48,2432]{1,0:T(8,128)(2,1)S(1)} %branch_0_fun.4), channel_id=1, source_target_pairs={{0,192},{64,0},{128,64},{192,128},{1,193},{65,1},{129,65},{193,129... | collective-permute-start | bytes 700424 | tf_op jit(solution)/shard_map/cond/branch_0_fun/ppermute | solution.py:456
  90.5 10.1 %collective-permute-start.1 = (bf16[48,2432]{1,0:T(8,128)(2,1)S(1)}, bf16[48,2432]{1,0:T(8,128)(2,1)S(1)}, u32[]{:S(2)}, u32[]{:S(2)}) collective-permute-start(bf16[48,2432]{1,0:T(8,128)(2,1)S(1)} %branch_0_fun.4), channel_id=1, source_target_pairs={{0,128},{64,192},{128,0},{192,64},{1,129},{65,193},{129,1},{193,65... | collective-permute-start | bytes 700424 | tf_op jit(solution)/shard_map/cond/branch_0_fun/ppermute | solution.py:456
  92.1 12.4 %collective-permute-start = (bf16[48,2432]{1,0:T(8,128)(2,1)S(1)}, bf16[48,2432]{1,0:T(8,128)(2,1)S(1)}, u32[]{:S(2)}, u32[]{:S(2)}) collective-permute-start(bf16[48,2432]{1,0:T(8,128)(2,1)S(1)} %branch_0_fun.4), channel_id=1, source_target_pairs={{0,64},{64,128},{128,192},{192,0},{1,65},{65,129},{129,193},{193,1... | collective-permute-start | bytes 700424 | tf_op jit(solution)/shard_map/cond/branch_0_fun/ppermute | solution.py:456
  104.5 2.6 %collective-permute-start.3 = (bf16[192,2432]{1,0:T(8,128)(2,1)S(1)}, bf16[192,2432]{1,0:T(8,128)(2,1)S(1)}, u32[]{:S(2)}, u32[]{:S(2)}) collective-permute-start(bf16[192,2432]{1,0:T(8,128)(2,1)S(1)} %pad_maximum_fusion.mine), channel_id=1, source_target_pairs={{0,32},{32,0},{1,33},{33,1},{2,34},{34,2},{3,35},{35,3},{4,36},{36... | collective-permute-start | bytes 2801672 | tf_op jit(solution)/shard_map/cond/branch_0_fun/ppermute | solution.py:458
  111.4 26.1 %all-to-all-start = ((bf16[32,16,640]{2,1,0:T(8,128)(2,1)}), bf16[32,16,640]{2,1,0:T(8,128)(2,1)S(1)}, u32[]{:S(2)}, u32[]{:S(2)}) async-start(bf16[32,16,640]{2,1,0:T(8,128)(2,1)} %bitcast.1), calls=%async_computation | async-start | bytes 1310720 | tf_op jit(solution)/shard_map/cond/branch_0_fun/all_to_all | solution.py:466

commit v3 on v2

--- a/solution.py
+++ b/solution.py
@@ -11,8 +11,9 @@
 ROUNDS = 24
 LEVELS = 6
 CAP = 16
-CAP_OWNER = 48
+CAP_PAIR = 64
 ORDER = (0, 1, 3, 2)
+NX = 4
 
 ramp_width = 0.5
 DP = ("x", "c")
@@ -218,7 +219,7 @@
         pack(p3[far, :] + unpack(high, near), q3, far)
 
 
-def total_kernel(own, q1, q3, logits, sent, stats):
+def total_kernel(own, q1, q3, packed, sent, stats):
     tokens = own.shape[0]
     step = 16
     lane = lax.broadcasted_iota(jnp.int32, (step, 128), 1)
@@ -228,7 +229,7 @@
         at = pl.ds(pl.multiple_of(i * step, step), step)
         value = own[at, :]
         value = value + unpack(q1, at) + unpack(q3, at)
-        logits[at, :] = value
+        pack(value, packed, at)
         high = jnp.max(value, axis=1, keepdims=True)
         shifted = jnp.exp(value - high)
         total = jnp.sum(shifted, axis=1, keepdims=True)
@@ -240,7 +241,7 @@
         sent[i] = rows
 
 
-def merge_kernel(parts, valid, advantage, sent):
+def merge_kernel(parts, valid, advantage, ids, sent):
     high = parts[0, 0:1, :]
     for i in range(1, parts.shape[0]):
         high = jnp.maximum(high, parts[i, 0:1, :])
@@ -250,11 +251,12 @@
     row = lax.broadcasted_iota(jnp.int32, (8, 128), 0)
     out = jnp.where(row == 0, high, sums)
     out = jnp.where(row == 3, valid[...].astype(f32), jnp.where(row == 4, advantage[...], out))
+    out = jnp.where(row == 5, ids[...].astype(f32), out)
     for i in range(sent.shape[0]):
         sent[i] = out
 
 
-def plan_kernel(start_high, cap_owner, parts, coef_out, normal_out, packed_out, slot_out, flag, rows):
+def plan_kernel(start_high, parts, coef_out, normal_out, id_out, packed_out, slot_out, flag, rows):
     owners = 8
     ny = parts.shape[0] // owners
     for o in range(owners):
@@ -268,8 +270,8 @@
         normal = high + jnp.log(sums[1:2, :])
         entropy = normal - sums[2:3, :] / sums[1:2, :]
         rows[o] = jnp.where(row == 0, normal, jnp.where(row == 1, entropy, parts[o * ny]))
-    normal, entropy, valid, advantage = (
-        jnp.concatenate([rows[o, k : k + 1, :] for o in range(owners)], axis=0) for k in (0, 1, 3, 4)
+    normal, entropy, valid, advantage, ids = (
+        jnp.concatenate([rows[o, k : k + 1, :] for o in range(owners)], axis=0) for k in (0, 1, 3, 4, 5)
     )
     counted = jnp.sum(jnp.sum(valid, axis=1, keepdims=True), axis=0, keepdims=True)
     threshold = bisect(jnp.where(valid > 0.0, entropy, -jnp.inf), counted, start_high)
@@ -282,14 +284,20 @@
     ahead = (i < j).astype(f32)
     group = 128 // (32 // owners)
     same = (i // group == j // group).astype(f32)
-    rank_owner = jnp.dot(activef, ahead, preferred_element_type=f32)
+    rank_pair = jnp.dot(activef, ahead, preferred_element_type=f32)
+    i = lax.broadcasted_iota(jnp.int32, (8, 8), 0)
+    j = lax.broadcasted_iota(jnp.int32, (8, 8), 1)
+    first = ((j == i - 1) & (i % 2 == 1)).astype(f32)
+    counts = jnp.broadcast_to(jnp.sum(activef, axis=1, keepdims=True), (8, 128))
+    rank_pair = rank_pair + jnp.dot(first, counts, preferred_element_type=f32)
     rank_group = jnp.dot(activef, ahead * same, preferred_element_type=f32)
     start = (lax.broadcasted_iota(jnp.int32, (8, 128), 1) // group * CAP).astype(f32)
     coef_out[...] = coef
     normal_out[...] = normal
-    packed_out[...] = jnp.where(active, rank_owner, -1.0)
+    id_out[...] = ids
+    packed_out[...] = jnp.where(active, rank_pair, -1.0)
     slot_out[...] = jnp.where(active, rank_group + start, -1.0)
-    over = jnp.where(active & ((rank_owner >= cap_owner) | (rank_group >= CAP)), 1.0, 0.0)
+    over = jnp.where(active & ((rank_pair >= CAP_PAIR) | (rank_group >= CAP)), 1.0, 0.0)
     flag[0, 0] = jnp.max(over).astype(jnp.int32)
 
 
@@ -306,70 +314,79 @@
     return (row == slots).astype(f32).astype(bf16)
 
 
-def slopes_kernel(at, logits, coef_all, normal_all, packed_all, ids, out):
-    me = pl.ds(at[2], 1)
-    count = out.shape[0]
-    columns = as_columns([coef_all[me, :], normal_all[me, :], ids[...].astype(f32)])
-    coef, normal, token = columns[:, 0:1], columns[:, 1:2], columns[:, 2:3].astype(jnp.int32) - at[3]
-    choose = one_hot(count, packed_all[me, :])
-    lane = lax.broadcasted_iota(jnp.int32, (128, 128), 1)
-    for k in range(logits.shape[1] // 128):
-        span = slice(k * 128, (k + 1) * 128)
-        hit = (lane + k * 128 == token).astype(f32)
-        slopes = (coef * (hit - jnp.exp(logits[:, span] - normal))).astype(bf16)
-        out[:, span] = jnp.dot(choose, slopes, preferred_element_type=f32).astype(bf16)
-
-
-def product_kernel(nx, at, mine, theirs, turned, packed_all, slot_all, out, held):
-    half = mine.shape[0]
-    count = half // nx
-    for k, rows in enumerate((mine, theirs)):
-        held[k * half : (k + 1) * half, :] = lax.dot_general(
-            rows[...], turned[...], (((1,), (0,)), ((), ())), preferred_element_type=f32
-        ).astype(bf16)
-    size = out.shape[0] // (2 * nx)
-    for owner in range(2 * nx):
-        to, core = owner // 2, owner % 2
-        source = lax.rem(at[0] - to + nx, nx) * count + lax.rem(at[1] + core, 2) * half
-        block = held[pl.ds(pl.multiple_of(source, 16), count), :]
-        spread = lax.dot_general(
-            one_hot(size, slot_all[owner : owner + 1, :]),
-            one_hot(count, packed_all[owner : owner + 1, :]),
+def owner_of(at, s, k):
+    return lax.rem(at[0] - s + NX, NX) * 2 + lax.rem(at[1] + k, 2)
+
+
+def slopes_kernel(at, coef_all, normal_all, id_all, packed_all, m0, m1, m2, m3, out):
+    cols = out.shape[1]
+    for s, ref in enumerate((m0, m1, m2, m3)):
+        me = pl.ds(owner_of(at, s, 0), 1)
+        column = as_columns([coef_all[me, :], normal_all[me, :], id_all[me, :]])
+        power = ref[:, cols : cols + 128].astype(jnp.int32).astype(f32)[:, :1]
+        scale = jnp.exp(power * LN2_64) * (1.0 / 32766.0)
+        choose = one_hot(CAP_PAIR, packed_all[me, :])
+
+        def tile(start, size, s=s, ref=ref, column=column, scale=scale, choose=choose):
+            span = pl.ds(start, size)
+            lane = lax.broadcasted_iota(jnp.int32, (128, size), 1)
+            token = column[:, 2:3].astype(jnp.int32) - (at[3] + start)
+            logits = ref[:, span].astype(jnp.int32).astype(f32) * scale
+            hit = jnp.where(lane == token, 1.0, 0.0)
+            slopes = (column[:, 0:1] * (hit - jnp.exp(logits - column[:, 1:2]))).astype(bf16)
+            out[s * CAP_PAIR : (s + 1) * CAP_PAIR, span] = jnp.dot(
+                choose, slopes, preferred_element_type=f32
+            ).astype(bf16)
+
+        over_columns(cols, tile)
+
+
+def product_kernel(at, mine, theirs, turned, slopes, o0, o1, o2, o3, held):
+    slopes[...] = (mine[...].astype(f32) + theirs[...].astype(f32)).astype(bf16)
+    held[...] = jnp.dot(slopes[...], turned[...], preferred_element_type=f32).astype(bf16)
+    for k, out in enumerate((o0, o1, o2, o3)):
+        source = lax.rem(at[0] - at[5] - k + 2 * NX, NX) * CAP_PAIR
+        out[...] = held[pl.ds(pl.multiple_of(source, CAP_PAIR), CAP_PAIR), :]
+
+
+def outer_kernel(at, packed_all, hid_mine, hid_theirs, slopes, out, held):
+    for s in range(NX):
+        rows = jnp.zeros((CAP_PAIR, out.shape[0]), f32)
+        for k, hidden in enumerate((hid_mine, hid_theirs)):
+            choose = one_hot(CAP_PAIR, packed_all[pl.ds(owner_of(at, s, k), 1), :])
+            rows = rows + jnp.dot(
+                choose, hidden[ORDER[s] * 128 : (ORDER[s] + 1) * 128, :], preferred_element_type=f32
+            )
+        held[s * CAP_PAIR : (s + 1) * CAP_PAIR, :] = rows.astype(bf16)
+    out[...] = lax.dot_general(
+        held[...], slopes[...], (((0,), (0,)), ((), ())), preferred_element_type=f32
+    )
+
+
+def spread_kernel(at, r0, r1, r2, r3, packed_all, slot_all, out):
+    size = out.shape[0]
+    spread = jnp.zeros((size, CAP_PAIR), f32)
+    for k in range(2):
+        me = pl.ds(at[5] * 2 + k, 1)
+        slot = slot_all[me, :]
+        slot = jnp.where(slot >= 0.0, slot + float(k * size // 2), -1.0)
+        spread = spread + lax.dot_general(
+            one_hot(size, slot),
+            one_hot(CAP_PAIR, packed_all[me, :]),
             (((1,), (1,)), ((), ())),
             preferred_element_type=f32,
-        ).astype(bf16)
-        out[owner * size : (owner + 1) * size, :] = jnp.dot(
-            spread, block, preferred_element_type=f32
-        ).astype(bf16)
-
-
-def outer_kernel(nx, at, packed_all, hid_mine, hid_theirs, mine, theirs, out, held):
-    half = mine.shape[0]
-    count = half // nx
-    for k, hidden in enumerate((hid_mine, hid_theirs)):
-        for s in range(nx):
-            owner = lax.rem(at[0] - s + nx, nx) * 2 + lax.rem(at[1] + k, 2)
-            choose = one_hot(count, packed_all[pl.ds(owner, 1), :])
-            to = k * half + s * count
-            held[to : to + count, :] = jnp.dot(
-                choose, hidden[ORDER[s] * 128 : (ORDER[s] + 1) * 128, :], preferred_element_type=f32
-            ).astype(bf16)
+        )
+    spread = spread.astype(bf16)
     total = jnp.zeros(out.shape, f32)
-    for k, rows in enumerate((mine, theirs)):
-        total = total + lax.dot_general(
-            held[k * half : (k + 1) * half, :],
-            rows[...],
-            (((0,), (0,)), ((), ())),
-            preferred_element_type=f32,
-        )
+    for r in (r0, r1, r2, r3):
+        total = total + jnp.dot(spread, r[...], preferred_element_type=f32)
     out[...] = total
 
 
 def sum_kernel(at, parts, slot_all, out, ranks):
-    n_voc = parts.shape[0] // CAP
-    total = parts[0:CAP, :].astype(f32)
-    for i in range(1, n_voc):
-        total = total + parts[i * CAP : (i + 1) * CAP, :].astype(f32)
+    total = parts[0:CAP, :]
+    for i in range(1, parts.shape[0] // CAP):
+        total = total + parts[i * CAP : (i + 1) * CAP, :]
     group = out.shape[0]
     per_owner = 128 // group
     owner, place = at[4] // per_owner, lax.rem(at[4], per_owner)
@@ -387,7 +404,7 @@
     rows, voc_cols = head.shape
     nx, n_voc, n_dp = lax.axis_size("x"), lax.axis_size(VOC), lax.axis_size(DP)
     x, c, block = lax.axis_index("x"), lax.axis_index("c"), lax.axis_index(VOC)
-    at = jnp.stack([x, c, x * 2 + c, block * voc_cols, block]).astype(jnp.int32)
+    at = jnp.stack([x, c, x * 2 + c, block * voc_cols, block, lax.axis_index("y")]).astype(jnp.int32)
     chip_rows = width // nx
 
     head_other = lax.ppermute(head, "c", SWAP)
@@ -423,73 +440,75 @@
     hid_theirs = lax.ppermute(hid_send, "c", SWAP)
     logits, stats = call(
         total_kernel,
-        [partial, struct((lax.axis_size("z"), 8, 128), f32)],
+        [packed, struct((lax.axis_size("z"), 8, 128), f32)],
         [own, q1, q3],
         [pltpu.VMEM((tokens, 128), f32)],
     )
+    mine = {s: lax.ppermute(logits, "x", ring(nx, s)) for s in (2, 1, 3)}
+    mine[0] = logits
 
     stats = lax.all_to_all(stats, "z", 0, 0, tiled=True)
     everyone = DP + ("y",)
     stats = call(
         merge_kernel,
         struct((lax.axis_size(everyone), 8, 128), f32),
-        [stats, valid.reshape(1, tokens), advantage.reshape(1, tokens)],
+        [stats] + [v.reshape(1, tokens) for v in (valid, advantage, token_ids)],
     )
     stats = lax.all_to_all(stats, everyone, 0, 0, tiled=True)
     start_high = float(np.float32(np.log(np.float32(voc_cols * n_voc))) + np.float32(1.0))
     table = struct((n_dp, tokens), f32)
-    coef_all, normal_all, packed_all, slot_all, flag = call(
-        functools.partial(plan_kernel, start_high, CAP_OWNER),
-        [table] * 4 + [struct((1, 1), jnp.int32)],
+    coef_all, normal_all, id_all, packed_all, slot_all, flag = call(
+        functools.partial(plan_kernel, start_high),
+        [table] * 5 + [struct((1, 1), jnp.int32)],
         [stats],
         [pltpu.VMEM((n_dp, 8, 128), f32)],
-        out_specs=[pl.BlockSpec(memory_space=pltpu.VMEM)] * 4 + [pl.BlockSpec(memory_space=pltpu.SMEM)],
+        out_specs=[pl.BlockSpec(memory_space=pltpu.VMEM)] * 5 + [pl.BlockSpec(memory_space=pltpu.SMEM)],
     )
 
     def sparse(_):
-        piece = call(
+        slopes = struct((nx * CAP_PAIR, voc_cols), bf16)
+        kept_rows = call(
             slopes_kernel,
-            struct((CAP_OWNER, voc_cols), bf16),
-            [at, logits, coef_all, normal_all, packed_all, token_ids.reshape(1, tokens)],
+            slopes,
+            [at, coef_all, normal_all, id_all, packed_all] + [mine[s] for s in range(nx)],
             smem=1,
         )
-        pieces = {s: lax.ppermute(piece, "x", ring(nx, s)) for s in (2, 1, 3)}
-        mine = jnp.concatenate([piece, pieces[1], pieces[2], pieces[3]], axis=0)
-        theirs = lax.ppermute(mine, "c", SWAP)
-        product = call(
-            functools.partial(product_kernel, nx),
-            struct((n_voc * CAP, rows), bf16),
-            [at, mine, theirs, turned, packed_all, slot_all],
-            [pltpu.VMEM((2 * nx * CAP_OWNER, rows), bf16)],
+        slopes, *parts = call(
+            product_kernel,
+            [slopes] + [struct((CAP_PAIR, rows), bf16)] * nx,
+            [at, kept_rows, lax.ppermute(kept_rows, "c", SWAP), turned],
+            [pltpu.VMEM((nx * CAP_PAIR, rows), bf16)],
             smem=1,
         )
-        parts = lax.all_to_all(product, VOC, 0, 0, tiled=True)
+        parts = [parts[0]] + [lax.ppermute(parts[k], "y", ring(nx, k)) for k in range(1, nx)]
         tile = 128
         head_grad = pl.pallas_call(
-            functools.partial(outer_kernel, nx),
+            outer_kernel,
             grid=(rows // tile,),
             in_specs=[
                 pl.BlockSpec(memory_space=pltpu.SMEM),
                 pl.BlockSpec((n_dp, tokens), lambda i: (0, 0)),
                 pl.BlockSpec((nx * tokens, tile), lambda i: (0, i)),
                 pl.BlockSpec((nx * tokens, tile), lambda i: (0, i)),
-                pl.BlockSpec((nx * CAP_OWNER, voc_cols), lambda i: (0, 0)),
-                pl.BlockSpec((nx * CAP_OWNER, voc_cols), lambda i: (0, 0)),
+                pl.BlockSpec((nx * CAP_PAIR, voc_cols), lambda i: (0, 0)),
             ],
             out_specs=pl.BlockSpec((tile, voc_cols), lambda i: (i, 0)),
             out_shape=struct((rows, voc_cols), f32),
-            scratch_shapes=[pltpu.VMEM((2 * nx * CAP_OWNER, tile), bf16)],
+            scratch_shapes=[pltpu.VMEM((nx * CAP_PAIR, tile), bf16)],
             compiler_params=pltpu.CompilerParams(vmem_limit_bytes=24 << 20),
-            cost_estimate=pl.CostEstimate(
-                flops=4 * nx * CAP_OWNER * rows * voc_cols,
-                bytes_accessed=4 * rows * voc_cols,
-                transcendentals=0,
-            ),
-        )(at, packed_all, hid_mine, hid_theirs, mine, theirs)
+            cost_estimate=estimate(rows, nx * CAP_PAIR, voc_cols),
+        )(at, packed_all, hid_mine, hid_theirs, slopes)
+        spread = call(
+            spread_kernel,
+            struct((n_voc * CAP // nx, rows), f32),
+            [at, *parts, packed_all, slot_all],
+            smem=1,
+        )
+        spread = lax.all_to_all(spread, "z", 0, 0, tiled=True)
         hidden_grad = call(
             sum_kernel,
             struct((tokens * n_dp // n_voc, rows), f32),
-            [at, parts, slot_all],
+            [at, spread, slot_all],
             [pltpu.VMEM((tokens, 8), f32)],
             smem=1,
         )

time: 146 us -> 152 us (1.041)
  waiting for transfers between devices: 56.7 us -> 39.6 us
  Pallas kernels: 35 us -> 46.4 us
  starting transfers between devices: 24.1 us -> 34.6 us
    pallas_call x11 -> x12, Pallas kernels: 28.5 us -> 40.9 us  [call(): pl.pallas_call(kernel, in_specs=specs, out_shape=out, scratch_shapes=list...]
    all_to_all x1, waiting for transfers between devices: 14.5 us -> 5.49 us  [sparse(): spread = lax.all_to_all(spread, 'z', 0, 0, tiled=True)]
    ppermute x4 -> x7, waiting for transfers between devices: 14.8 us -> 6.95 us  [the longest x3 4.11 us: sparse(): lax.ppermute(parts[k], 'y', ring(nx, k))]
    ppermute x4 -> x7, starting transfers between devices: 2.86 us -> 7.35 us  [the longest x3 3.99 us: sparse(): lax.ppermute(parts[k], 'y', ring(nx, k))]
    all_to_all x1, starting transfers between devices: 5.01 us -> 8.51 us  [sparse(): spread = lax.all_to_all(spread, 'z', 0, 0, tiled=True)]
    all_to_all x1, starting transfers between devices: 4.87 us -> 7.4 us  [shards(): stats = lax.all_to_all(stats, everyone, 0, 0, tiled=True)]
  transfers between devices with their start and end apart: 15 -> 18, of which waited for: 12 -> 11; matrix products, arithmetic and copies ran while one was open for 0% -> 0% of each run, Pallas kernels for 19% -> 18%
where the time goes in v3:
time: 152 us; the launch traced here: 150 us
  Pallas kernels  46.4 us (31%)
  waiting for transfers between devices  39.6 us (26%)
  starting transfers between devices  34.6 us (23%)
  blocking collectives  14.9 us (10%)
  between operations  14.8 us (10%)
    pallas_call x12, Pallas kernels, call(): pl.pallas_call(kernel, in_specs=specs, out_shape=out, scratch_shapes=list...  40.9 us
    all_to_all x1, blocking collectives, shards(): stats = lax.all_to_all(stats, 'z', 0, 0, tiled=True)  14.9 us
    ppermute x1, waiting for transfers between devices, shards(): lax.ppermute(q1, 'x', ring(nx, -1))  12.7 us
    all_to_all x1, starting transfers between devices, sparse(): spread = lax.all_to_all(spread, 'z', 0, 0, tiled=True)  8.51 us
    all_to_all x1, waiting for transfers between devices, shards(): stats = lax.all_to_all(stats, everyone, 0, 0, tiled=True)  7.66 us
    all_to_all x1, starting transfers between devices, shards(): stats = lax.all_to_all(stats, everyone, 0, 0, tiled=True)  7.4 us
    ppermute x3, starting transfers between devices, shards(): came = {s: lax.ppermute(leave[s - 1], 'x', ring(nx, s)) for s in (2, 1, 3)}  6.35 us
    pallas_call x1, Pallas kernels, sparse(): pl.pallas_call(outer_kernel, grid=(rows // tile,), in_specs=[pl.BlockSpec...  5.49 us
  transfers between devices with their start and end apart: 18, of which 11 were waited for; matrix products, arithmetic and copies ran while one was open for 0% of the time, Pallas kernels for 18%

profile of v3, /device:TPU:32, one launch (start us, length us, event | category | flops | bytes accessed | tf_op | source)
XLA Modules:
  0.0 150.4 jit_solution(12929018685767668774)
XLA Ops:
  8.8 3.1 %collective-permute-start.4 = (bf16[128,1280]{1,0:T(8,128)(2,1)S(1)}, bf16[128,1280]{1,0:T(8,128)(2,1)S(1)}, u32[]{:S(2)}, u32[]{:S(2)}) collective-permute-start(bf16[128,1280]{1,0:T(8,128)(2,1)S(1)} %get-tuple-element.117), channel_id=1, source_target_pairs={{0,128},{64,192},{128,0},{192,64},{1,129},{65,193},{129,1},{193,65... | collective-permute-start | bytes 983048 | tf_op jit(solution)/shard_map/ppermute | solution.py:414
  12.5 2.6 %collective-permute-start.7 = (bf16[128,1280]{1,0:T(8,128)(2,1)S(1)}, bf16[128,1280]{1,0:T(8,128)(2,1)S(1)}, u32[]{:S(2)}, u32[]{:S(2)}) collective-permute-start(bf16[128,1280]{1,0:T(8,128)(2,1)S(1)} %get-tuple-element.122), channel_id=1, source_target_pairs={{0,192},{64,0},{128,64},{192,128},{1,193},{65,1},{129,65},{193,129... | collective-permute-start | bytes 983048 | tf_op jit(solution)/shard_map/ppermute | solution.py:414
  15.1 4.7 %shard_map.73 = (bf16[640,2432]{1,0:T(8,128)(2,1)S(1)}, bf16[2432,640]{1,0:T(8,128)(2,1)}) custom-call(bf16[640,2432]{1,0:T(8,128)(2,1)} %head.1), custom_call_target="tpu_custom_call" | custom-call | tf_op jit(solution)/shard_map/pallas_call | solution.py:96
  20.9 3.7 %shard_map.74 = (s16[64,2560]{1,0:T(8,128)(2,1)S(1)}, s16[64,2560]{1,0:T(8,128)(2,1)S(1)}, f32[8,128]{1,0:T(8,128)S(1)}) custom-call(s32[6]{0:T(128)S(1)} %stack.27.at, bf16[128,1280]{1,0:T(8,128)(2,1)S(1)} %collective-permute-done.4.block.b2, bf16[640,2432]{1,0:T(8,128)(2,1)S(1)} %get-tuple-element.118.head, bf16[640,2432]{1,0:T(8,128)(2,1)S(1)} %collective-permute-done.5.other), custom_call_target="tpu_custom_call" | custom-call | flops 796917760 | bytes 6225920 | tf_op jit(solution)/shard_map/pallas_call | solution.py:96
  24.6 2.8 %collective-permute-start.8 = (s16[64,2560]{1,0:T(8,128)(2,1)S(1)}, s16[64,2560]{1,0:T(8,128)(2,1)S(1)}, u32[]{:S(2)}, u32[]{:S(2)}) collective-permute-start(s16[64,2560]{1,0:T(8,128)(2,1)S(1)} %get-tuple-element.126), channel_id=1, source_target_pairs={{0,192},{64,0},{128,64},{192,128},{1,193},{65,1},{129,65},{193,129... | collective-permute-start | bytes 983048 | tf_op jit(solution)/shard_map/ppermute | solution.py:427
  28.0 5.9 %shard_map.75 = (f32[128,2432]{1,0:T(8,128)S(1)}, f32[128,2432]{1,0:T(8,128)S(1)}, f32[128,2432]{1,0:T(8,128)S(1)}, bf16[512,640]{1,0:T(8,128)(2,1)}, bf16[512,640]{1,0:T(8,128)(2,1)}) custom-call(s32[6]{0:T(128)S(1)} %stack.27.at, f32[8,128]{1,0:T(8,128)S(1)} %get-tuple-element.119.tick, bf16[128,1280]{1,0:T(8,128)(2,1)S(1)} %get-tuple-element.120.b0, ...), custom_call_target="tpu_custom_call" | custom-call | flops 2390753280 | bytes 6225920 | tf_op jit(solution)/shard_map/pallas_call | solution.py:96
  34.7 2.7 %collective-permute-done.9.high = s16[64,2560]{1,0:T(8,128)(2,1)S(1)} collective-permute-done((s16[64,2560]{1,0:T(8,128)(2,1)S(1)}, s16[64,2560]{1,0:T(8,128)(2,1)S(1)}, u32[]{:S(2)}, u32[]{:S(2)}) %collective-permute-start.9) | collective-permute-done | bytes 327712 | tf_op jit(solution)/shard_map/ppermute | solution.py:427
  38.4 1.7 %collective-permute-start.11 = (s16[128,2560]{1,0:T(8,128)(2,1)S(1)}, s16[128,2560]{1,0:T(8,128)(2,1)S(1)}, u32[]{:S(2)}, u32[]{:S(2)}) collective-permute-start(s16[128,2560]{1,0:T(8,128)(2,1)S(1)} %get-tuple-element.129), channel_id=1, source_target_pairs={{0,64},{64,128},{128,192},{192,0},{1,65},{65,129},{129,193},{193,1... | collective-permute-start | bytes 1966088 | tf_op jit(solution)/shard_map/ppermute | solution.py:439
  40.1 12.7 %collective-permute-done.10.q1 = s16[128,2560]{1,0:T(8,128)(2,1)S(1)} collective-permute-done((s16[128,2560]{1,0:T(8,128)(2,1)S(1)}, s16[128,2560]{1,0:T(8,128)(2,1)S(1)}, u32[]{:S(2)}, u32[]{:S(2)}) %collective-permute-start.10) | collective-permute-done | bytes 655392 | tf_op jit(solution)/shard_map/ppermute | solution.py:439
  54.5 3.3 %shard_map.77 = (s16[128,2560]{1,0:T(8,128)(2,1)}, f32[8,8,128]{2,1,0:T(8,128)S(1)}) custom-call(f32[128,2432]{1,0:T(8,128)S(1)} %get-tuple-element.123.own, s16[128,2560]{1,0:T(8,128)(2,1)S(1)} %collective-permute-done.10.q1, s16[128,2560]{1,0:T(8,128)(2,1)S(1)} %collective-permute-done.11.q3), custom_call_target="tpu_custom_call" | custom-call | tf_op jit(solution)/shard_map/pallas_call | solution.py:96
  61.1 14.9 %all_to_all.34.parts = f32[8,8,128]{2,1,0:T(8,128)S(1)} all-to-all(f32[8,8,128]{2,1,0:T(8,128)S(1)} %get-tuple-element.130), channel_id=1, replica_groups=mesh['x'=4,'c'=2,'y'=4,'z'=8] {'z'}, dimensions={0} | all-to-all | bytes 65536 | tf_op jit(solution)/shard_map/all_to_all | solution.py:450
  76.7 7.4 %all-to-all-start.3 = ((f32[32,8,128]{2,1,0:T(8,128)}), f32[32,8,128]{2,1,0:T(8,128)S(1)}, u32[]{:S(2)}, u32[]{:S(2)}) async-start(f32[32,8,128]{2,1,0:T(8,128)} %shard_map.78), calls=%async_computation.5 | async-start | bytes 262144 | tf_op jit(solution)/shard_map/all_to_all | solution.py:457
  84.1 7.7 %all-to-all-done.3.parts = f32[32,8,128]{2,1,0:T(8,128)S(1)} async-done(((f32[32,8,128]{2,1,0:T(8,128)}), f32[32,8,128]{2,1,0:T(8,128)S(1)}, u32[]{:S(2)}, u32[]{:S(2)}) %all-to-all-start.3) | async-done | bytes 131104 | tf_op jit(solution)/shard_map/all_to_all | solution.py:457
  91.8 2.2 %shard_map.79 = (f32[8,128]{1,0:T(8,128)S(1)}, f32[8,128]{1,0:T(8,128)S(1)}, f32[8,128]{1,0:T(8,128)S(1)}, f32[8,128]{1,0:T(8,128)S(1)}, f32[8,128]{1,0:T(8,128)S(1)}, /*index=5*/s32[1,1]{1,0:T(1,128)}) custom-call(f32[32,8,128]{2,1,0:T(8,128)S(1)} %all-to-all-done.3.parts), custom_call_target="tpu_custom_call" | custom-call | tf_op jit(solution)/shard_map/pallas_call | solution.py:96
  94.7 48.9 %conditional.1 = (f32[32,640]{1,0:T(8,128)}, f32[640,2432]{1,0:T(8,128)}) conditional(s32[]{:T(128)} %bitcast.15, (s32[6]{0:T(128)S(1)}, f32[8,128]{1,0:T(8,128)S(1)}, f32[8,128]{1,0:T(8,128)S(1)}, f32[8,128]{1,0:T(8,128)S(1)}, f32[8,128]{1,0:T(8,128)S(1)}, /*index=5*/s16[128,2560]{1,0:T(8,128)(2,1)}, s16[128,2560]{1,0:T(8,128)(2,1)}, ...), branch_computations={%region_0.0_spmd, %region_1.16_spmd} | conditional | flops 9566442496 | bytes 125846592 | solution.py:520
  94.7 13.4 %branch_0_fun.5.mine = bf16[256,2432]{1,0:T(8,128)(2,1)S(1)} custom-call(s32[6]{0:T(128)S(1)} %get-tuple-element.60.at, f32[8,128]{1,0:T(8,128)S(1)} %get-tuple-element.61.coef_all, f32[8,128]{1,0:T(8,128)S(1)} %get-tuple-element.62.normal_all, f32[8,128]{1,0:T(8,128)S(1)} %get-tuple-element.63.id_all, f32[8,128]{1,0:T(8,128)S(1)} %get-tuple-element.64.packed_all, ...), custom_call_target="tpu_custom_call" | custom-call | tf_op jit(solution)/shard_map/cond/branch_0_fun/pallas_call | solution.py:96
  108.2 2.8 %collective-permute-done.theirs = bf16[256,2432]{1,0:T(8,128)(2,1)S(1)} collective-permute-done((bf16[256,2432]{1,0:T(8,128)(2,1)S(1)}, bf16[256,2432]{1,0:T(8,128)(2,1)S(1)}, u32[]{:S(2)}, u32[]{:S(2)}) %collective-permute-start) | collective-permute-done | bytes 1245216 | tf_op jit(solution)/shard_map/cond/branch_0_fun/ppermute | solution.py:479
  111.0 1.8 %branch_0_fun.6 = (bf16[256,2432]{1,0:T(8,128)(2,1)S(1)}, bf16[64,640]{1,0:T(8,128)(2,1)S(1)}, bf16[64,640]{1,0:T(8,128)(2,1)S(1)}, bf16[64,640]{1,0:T(8,128)(2,1)S(1)}, bf16[64,640]{1,0:T(8,128)(2,1)S(1)}) custom-call(s32[6]{0:T(128)S(1)} %get-tuple-element.60.at, bf16[256,2432]{1,0:T(8,128)(2,1)S(1)} %branch_0_fun.5.mine, ...), custom_call_target="tpu_custom_call" | custom-call | tf_op jit(solution)/shard_map/cond/branch_0_fun/pallas_call | solution.py:96
  113.3 2.4 %collective-permute-start.2 = (bf16[64,640]{1,0:T(8,128)(2,1)S(1)}, bf16[64,640]{1,0:T(8,128)(2,1)S(1)}, u32[]{:S(2)}, u32[]{:S(2)}) collective-permute-start(bf16[64,640]{1,0:T(8,128)(2,1)S(1)} %get-tuple-element.72), channel_id=1, source_target_pairs={{0,16},{8,24},{16,0},{24,8},{1,17},{9,25},{17,1},{25,9},{2,18},{10... | collective-permute-start | bytes 245768 | tf_op jit(solution)/shard_map/cond/branch_0_fun/ppermute | solution.py:483
  116.8 3.5 %collective-permute-done.1.r1 = bf16[64,640]{1,0:T(8,128)(2,1)S(1)} collective-permute-done((bf16[64,640]{1,0:T(8,128)(2,1)S(1)}, bf16[64,640]{1,0:T(8,128)(2,1)S(1)}, u32[]{:S(2)}, u32[]{:S(2)}) %collective-permute-start.1) | collective-permute-done | bytes 81952 | tf_op jit(solution)/shard_map/cond/branch_0_fun/ppermute | solution.py:483
  120.9 1.8 %branch_0_fun.7 = f32[128,640]{1,0:T(8,128)} custom-call(s32[6]{0:T(128)S(1)} %get-tuple-element.60.at, bf16[64,640]{1,0:T(8,128)(2,1)S(1)} %get-tuple-element.70.r0, bf16[64,640]{1,0:T(8,128)(2,1)S(1)} %collective-permute-done.1.r1, bf16[64,640]{1,0:T(8,128)(2,1)S(1)} %collective-permute-done.2.r2, bf16[64,640]{1,0:T(8,128)(2,1)S(1)} %collective-permute-done.3.r3, ...), custom_call_target="tpu_custom_call" | custom-call | tf_op jit(solution)/shard_map/cond/branch_0_fun/pallas_call | solution.py:96
  122.7 8.5 %all-to-all-start = ((f32[8,16,640]{2,1,0:T(8,128)}), f32[8,16,640]{2,1,0:T(8,128)S(1)}, u32[]{:S(2)}, u32[]{:S(2)}) async-start(f32[8,16,640]{2,1,0:T(8,128)} %bitcast), calls=%async_computation | async-start | bytes 655360 | tf_op jit(solution)/shard_map/cond/branch_0_fun/all_to_all | solution.py:507
  131.2 5.5 %branch_0_fun.9 = f32[640,2432]{1,0:T(8,128)} custom-call(s32[6]{0:T(128)S(1)} %get-tuple-element.60.at, f32[8,128]{1,0:T(8,128)S(1)} %get-tuple-element.64.packed_all, bf16[512,640]{1,0:T(8,128)(2,1)S(1)} %get-tuple-element.75.hid_mine, bf16[512,640]{1,0:T(8,128)(2,1)S(1)} %get-tuple-element.76.hid_theirs, bf16[256,2432]{1,0:T(8,128)(2,1)S(1)} %get-tuple-element.77.slopes), custom_call_target="tpu_custom_call" | custom-call | flops 796917760 | bytes 1245184 | tf_op jit(solution)/shard_map/cond/branch_0_fun/pallas_call | solution.py:485
  136.7 5.5 %all-to-all-done = f32[8,16,640]{2,1,0:T(8,128)S(1)} async-done(((f32[8,16,640]{2,1,0:T(8,128)}), f32[8,16,640]{2,1,0:T(8,128)S(1)}, u32[]{:S(2)}, u32[]{:S(2)}) %all-to-all-start) | async-done | bytes 327712 | tf_op jit(solution)/shard_map/cond/branch_0_fun/all_to_all | solution.py:507
  (40 shorter events, 15.0 us)
Async XLA Ops:
  7.2 13.8 %collective-permute-start.5 = (bf16[640,2432]{1,0:T(8,128)(2,1)}, bf16[640,2432]{1,0:T(8,128)(2,1)S(1)}, u32[]{:S(2)}, u32[]{:S(2)}) collective-permute-start(bf16[640,2432]{1,0:T(8,128)(2,1)} %head.1), channel_id=1, source_target_pairs={{0,32},{32,0},{1,33},{33,1},{2,34},{34,2},{3,35},{35,3},{4,36},{36... | collective-permute-start | bytes 9338888 | tf_op jit(solution)/shard_map/ppermute | solution.py:410
  8.8 12.1 %collective-permute-start.4 = (bf16[128,1280]{1,0:T(8,128)(2,1)S(1)}, bf16[128,1280]{1,0:T(8,128)(2,1)S(1)}, u32[]{:S(2)}, u32[]{:S(2)}) collective-permute-start(bf16[128,1280]{1,0:T(8,128)(2,1)S(1)} %get-tuple-element.117), channel_id=1, source_target_pairs={{0,128},{64,192},{128,0},{192,64},{1,129},{65,193},{129,1},{193,65... | collective-permute-start | bytes 983048 | tf_op jit(solution)/shard_map/ppermute | solution.py:414
  11.9 15.6 %collective-permute-start.6 = (bf16[128,1280]{1,0:T(8,128)(2,1)S(1)}, bf16[128,1280]{1,0:T(8,128)(2,1)S(1)}, u32[]{:S(2)}, u32[]{:S(2)}) collective-permute-start(bf16[128,1280]{1,0:T(8,128)(2,1)S(1)} %get-tuple-element.121), channel_id=1, source_target_pairs={{0,64},{64,128},{128,192},{192,0},{1,65},{65,129},{129,193},{193,1... | collective-permute-start | bytes 983048 | tf_op jit(solution)/shard_map/ppermute | solution.py:414
  12.5 15.5 %collective-permute-start.7 = (bf16[128,1280]{1,0:T(8,128)(2,1)S(1)}, bf16[128,1280]{1,0:T(8,128)(2,1)S(1)}, u32[]{:S(2)}, u32[]{:S(2)}) collective-permute-start(bf16[128,1280]{1,0:T(8,128)(2,1)S(1)} %get-tuple-element.122), channel_id=1, source_target_pairs={{0,192},{64,0},{128,64},{192,128},{1,193},{65,1},{129,65},{193,129... | collective-permute-start | bytes 983048 | tf_op jit(solution)/shard_map/ppermute | solution.py:414
  24.6 10.0 %collective-permute-start.8 = (s16[64,2560]{1,0:T(8,128)(2,1)S(1)}, s16[64,2560]{1,0:T(8,128)(2,1)S(1)}, u32[]{:S(2)}, u32[]{:S(2)}) collective-permute-start(s16[64,2560]{1,0:T(8,128)(2,1)S(1)} %get-tuple-element.126), channel_id=1, source_target_pairs={{0,192},{64,0},{128,64},{192,128},{1,193},{65,1},{129,65},{193,129... | collective-permute-start | bytes 983048 | tf_op jit(solution)/shard_map/ppermute | solution.py:427
  27.5 9.8 %collective-permute-start.9 = (s16[64,2560]{1,0:T(8,128)(2,1)S(1)}, s16[64,2560]{1,0:T(8,128)(2,1)S(1)}, u32[]{:S(2)}, u32[]{:S(2)}) collective-permute-start(s16[64,2560]{1,0:T(8,128)(2,1)S(1)} %get-tuple-element.127), channel_id=1, source_target_pairs={{0,64},{64,128},{128,192},{192,0},{1,65},{65,129},{129,193},{193,1... | collective-permute-start | bytes 983048 | tf_op jit(solution)/shard_map/ppermute | solution.py:427
  38.0 14.8 %collective-permute-start.10 = (s16[128,2560]{1,0:T(8,128)(2,1)S(1)}, s16[128,2560]{1,0:T(8,128)(2,1)S(1)}, u32[]{:S(2)}, u32[]{:S(2)}) collective-permute-start(s16[128,2560]{1,0:T(8,128)(2,1)S(1)} %get-tuple-element.128), channel_id=1, source_target_pairs={{0,192},{64,0},{128,64},{192,128},{1,193},{65,1},{129,65},{193,129... | collective-permute-start | bytes 1966088 | tf_op jit(solution)/shard_map/ppermute | solution.py:439
  38.4 16.1 %collective-permute-start.11 = (s16[128,2560]{1,0:T(8,128)(2,1)S(1)}, s16[128,2560]{1,0:T(8,128)(2,1)S(1)}, u32[]{:S(2)}, u32[]{:S(2)}) collective-permute-start(s16[128,2560]{1,0:T(8,128)(2,1)S(1)} %get-tuple-element.129), channel_id=1, source_target_pairs={{0,64},{64,128},{128,192},{192,0},{1,65},{65,129},{129,193},{193,1... | collective-permute-start | bytes 1966088 | tf_op jit(solution)/shard_map/ppermute | solution.py:439
  40.1 54.5 %collective-permute-start.15 = (bf16[512,640]{1,0:T(8,128)(2,1)}, bf16[512,640]{1,0:T(8,128)(2,1)S(1)}, u32[]{:S(2)}, u32[]{:S(2)}) collective-permute-start(bf16[512,640]{1,0:T(8,128)(2,1)} %get-tuple-element.140), channel_id=1, source_target_pairs={{0,32},{32,0},{1,33},{33,1},{2,34},{34,2},{3,35},{35,3},{4,36},{36... | collective-permute-start | bytes 1966088 | tf_op jit(solution)/shard_map/ppermute | solution.py:440
  54.5 21.5 %copy-start.4 = (s32[128]{0:T(128)S(1)}, s32[128]{0:T(128)}, u32[]{:S(2)}) copy-start(s32[128]{0:T(128)} %param.12) | copy-start | bytes 1540
  54.5 21.5 %copy-start.5 = (f32[128]{0:T(128)S(1)}, f32[128]{0:T(128)}, u32[]{:S(2)}) copy-start(f32[128]{0:T(128)} %param.13) | copy-start | bytes 1540
  54.5 21.5 %copy-start.6 = (s32[128]{0:T(128)S(1)}, s32[128]{0:T(128)}, u32[]{:S(2)}) copy-start(s32[128]{0:T(128)} %param.11) | copy-start | bytes 1540
  54.5 40.1 %copy-start.1 = (bf16[128,5120]{1,0:T(8,128)(2,1)S(1)}, bf16[128,5120]{1,0:T(8,128)(2,1)}, u32[]{:S(2)}) copy-start(bf16[128,5120]{1,0:T(8,128)(2,1)} %hidden.1) | copy-start | bytes 3932164
  54.5 40.1 %copy-start.3 = (bf16[512,640]{1,0:T(8,128)(2,1)S(1)}, bf16[512,640]{1,0:T(8,128)(2,1)}, u32[]{:S(2)}) copy-start(bf16[512,640]{1,0:T(8,128)(2,1)} %get-tuple-element.139) | copy-start | bytes 1966084
  57.9 36.8 %collective-permute-start.12 = (s16[128,2560]{1,0:T(8,128)(2,1)}, s16[128,2560]{1,0:T(8,128)(2,1)}, u32[]{:S(2)}, u32[]{:S(2)}) collective-permute-start(s16[128,2560]{1,0:T(8,128)(2,1)} %get-tuple-element.136), channel_id=1, source_target_pairs={{0,64},{64,128},{128,192},{192,0},{1,65},{65,129},{129,193},{193,1... | collective-permute-start | bytes 1966088 | tf_op jit(solution)/shard_map/ppermute | solution.py:447
  57.9 36.7 %collective-permute-start.13 = (s16[128,2560]{1,0:T(8,128)(2,1)}, s16[128,2560]{1,0:T(8,128)(2,1)}, u32[]{:S(2)}, u32[]{:S(2)}) collective-permute-start(s16[128,2560]{1,0:T(8,128)(2,1)} %get-tuple-element.136), channel_id=1, source_target_pairs={{0,128},{64,192},{128,0},{192,64},{1,129},{65,193},{129,1},{193,65... | collective-permute-start | bytes 1966088 | tf_op jit(solution)/shard_map/ppermute | solution.py:447
  59.6 35.0 %collective-permute-start.14 = (s16[128,2560]{1,0:T(8,128)(2,1)}, s16[128,2560]{1,0:T(8,128)(2,1)}, u32[]{:S(2)}, u32[]{:S(2)}) collective-permute-start(s16[128,2560]{1,0:T(8,128)(2,1)} %get-tuple-element.136), channel_id=1, source_target_pairs={{0,192},{64,0},{128,64},{192,128},{1,193},{65,1},{129,65},{193,129... | collective-permute-start | bytes 1966088 | tf_op jit(solution)/shard_map/ppermute | solution.py:447
  76.7 15.1 %all-to-all-start.3 = ((f32[32,8,128]{2,1,0:T(8,128)}), f32[32,8,128]{2,1,0:T(8,128)S(1)}, u32[]{:S(2)}, u32[]{:S(2)}) async-start(f32[32,8,128]{2,1,0:T(8,128)} %shard_map.78), calls=%async_computation.5 | async-start | bytes 262144 | tf_op jit(solution)/shard_map/all_to_all | solution.py:457
  94.7 16.3 %copy-start.2 = (bf16[2432,640]{1,0:T(8,128)(2,1)S(1)}, bf16[2432,640]{1,0:T(8,128)(2,1)}, u32[]{:S(2)}) copy-start(bf16[2432,640]{1,0:T(8,128)(2,1)} %get-tuple-element.69.turned) | copy-start | bytes 9338884 | tf_op jit(solution)/shard_map/cond
  108.1 2.9 %collective-permute-start = (bf16[256,2432]{1,0:T(8,128)(2,1)S(1)}, bf16[256,2432]{1,0:T(8,128)(2,1)S(1)}, u32[]{:S(2)}, u32[]{:S(2)}) collective-permute-start(bf16[256,2432]{1,0:T(8,128)(2,1)S(1)} %branch_0_fun.5.mine), channel_id=1, source_target_pairs={{0,32},{32,0},{1,33},{33,1},{2,34},{34,2},{3,35},{35,3},{4,36},{36... | collective-permute-start | bytes 3735560 | tf_op jit(solution)/shard_map/cond/branch_0_fun/ppermute | solution.py:479
  112.8 7.5 %collective-permute-start.1 = (bf16[64,640]{1,0:T(8,128)(2,1)S(1)}, bf16[64,640]{1,0:T(8,128)(2,1)S(1)}, u32[]{:S(2)}, u32[]{:S(2)}) collective-permute-start(bf16[64,640]{1,0:T(8,128)(2,1)S(1)} %get-tuple-element.71), channel_id=1, source_target_pairs={{0,8},{8,16},{16,24},{24,0},{1,9},{9,17},{17,25},{25,1},{2,10},{10... | collective-permute-start | bytes 245768 | tf_op jit(solution)/shard_map/cond/branch_0_fun/ppermute | solution.py:483
  113.3 7.1 %collective-permute-start.2 = (bf16[64,640]{1,0:T(8,128)(2,1)S(1)}, bf16[64,640]{1,0:T(8,128)(2,1)S(1)}, u32[]{:S(2)}, u32[]{:S(2)}) collective-permute-start(bf16[64,640]{1,0:T(8,128)(2,1)S(1)} %get-tuple-element.72), channel_id=1, source_target_pairs={{0,16},{8,24},{16,0},{24,8},{1,17},{9,25},{17,1},{25,9},{2,18},{10... | collective-permute-start | bytes 245768 | tf_op jit(solution)/shard_map/cond/branch_0_fun/ppermute | solution.py:483
  115.7 5.2 %collective-permute-start.3 = (bf16[64,640]{1,0:T(8,128)(2,1)S(1)}, bf16[64,640]{1,0:T(8,128)(2,1)S(1)}, u32[]{:S(2)}, u32[]{:S(2)}) collective-permute-start(bf16[64,640]{1,0:T(8,128)(2,1)S(1)} %get-tuple-element.73), channel_id=1, source_target_pairs={{0,24},{8,0},{16,8},{24,16},{1,25},{9,1},{17,9},{25,17},{2,26},{10... | collective-permute-start | bytes 245768 | tf_op jit(solution)/shard_map/cond/branch_0_fun/ppermute | solution.py:483
  122.7 19.5 %all-to-all-start = ((f32[8,16,640]{2,1,0:T(8,128)}), f32[8,16,640]{2,1,0:T(8,128)S(1)}, u32[]{:S(2)}, u32[]{:S(2)}) async-start(f32[8,16,640]{2,1,0:T(8,128)} %bitcast), calls=%async_computation | async-start | bytes 655360 | tf_op jit(solution)/shard_map/cond/branch_0_fun/all_to_all | solution.py:507

commit v4 on v2

--- a/solution.py
+++ b/solution.py
@@ -11,8 +11,9 @@
 ROUNDS = 24
 LEVELS = 6
 CAP = 16
-CAP_OWNER = 48
-ORDER = (0, 1, 3, 2)
+CAP_SMALL = 32
+ORDER = (2, 0, 3, 1)
+NX = 4
 
 ramp_width = 0.5
 DP = ("x", "c")
@@ -121,8 +122,7 @@
         out[...] = hidden[:, pl.ds(pl.multiple_of(to, 128), chip_rows)]
 
 
-def turn_kernel(head, kept, turned):
-    kept[...] = head[...]
+def turn_kernel(tick, head, turned):
     for k in range(head.shape[1] // 128):
         span = slice(k * 128, (k + 1) * 128)
         turned[span, :] = jnp.transpose(head[:, span])
@@ -145,14 +145,8 @@
 
 
 def over_columns(cols, tile):
-    wide = cols // 256
-
-    @pl.loop(0, wide)
-    def _(i):
-        tile(pl.multiple_of(i * 256, 256), 256)
-
-    if cols > wide * 256:
-        tile(wide * 256, cols - wide * 256)
+    for start in range(0, cols, 256):
+        tile(slice(start, min(start + 256, cols)))
 
 
 def halves(at, rows):
@@ -162,13 +156,24 @@
     )
 
 
+def own_kernel(at, block, head, other, own, kept):
+    kept[...] = head[...]
+    here, there = halves(at, head.shape[0])
+
+    def tile(span):
+        own[:, span] = jnp.dot(block[:, here], head[:, span], preferred_element_type=f32) + jnp.dot(
+            block[:, there], other[:, span], preferred_element_type=f32
+        )
+
+    over_columns(head.shape[1], tile)
+
+
 def far_kernel(at, block, head, other, low, high, tick, part):
     tokens = block.shape[0]
     rows, cols = head.shape
     here, there = halves(at, rows)
 
-    def tile(start, size):
-        span = pl.ds(start, size)
+    def tile(span):
         part[:, span] = jnp.dot(block[:, here], head[:, span], preferred_element_type=f32) + jnp.dot(
             block[:, there], other[:, span], preferred_element_type=f32
         )
@@ -184,29 +189,28 @@
             pack(part[pl.ds(source, step), :], out, pl.ds(pl.multiple_of(i * step, step), step))
 
 
-def near_kernel(at, tick, b0, b1, b2, b3, head, other, own, p1, p3, mine, theirs):
+def near_kernel(at, tick, b0, b1, b2, b3, head, other, p1, p3, mine, theirs):
     tokens = b0.shape[0]
     rows, cols = head.shape
     here, there = halves(at, rows)
-    for k, block in enumerate((b0, b1, b3, b2)):
+    for k, block in enumerate((b1, b3, b0, b2)):
         mine[k * tokens : (k + 1) * tokens, :] = block[:, here]
         theirs[k * tokens : (k + 1) * tokens, :] = block[:, there]
 
-    def tile(start, size):
-        span = pl.ds(start, size)
-        part = jnp.dot(mine[0 : 3 * tokens, :], head[:, span], preferred_element_type=f32) + jnp.dot(
-            theirs[0 : 3 * tokens, :], other[:, span], preferred_element_type=f32
-        )
-        own[:, span] = part[0:tokens, :]
-        p1[:, span] = part[tokens : 2 * tokens, :]
-        p3[:, span] = part[2 * tokens :, :]
+    def tile(span):
+        part = jnp.dot(mine[0 : 2 * tokens, :], head[:, span], preferred_element_type=f32) + jnp.dot(
+            theirs[0 : 2 * tokens, :], other[:, span], preferred_element_type=f32
+        )
+        p1[:, span] = part[0:tokens, :]
+        p3[:, span] = part[tokens:, :]
 
     over_columns(cols, tile)
 
 
-def relay_kernel(p1, p3, low, high, q1, q3):
+def relay_kernel(p1, p3, low, high, q1, q3, tick):
     tokens = p1.shape[0]
     half, step = tokens // 2, 32
+    tick[...] = jnp.zeros(tick.shape, f32)
 
     @pl.loop(0, half // step)
     def _(i):
@@ -254,7 +258,7 @@
         sent[i] = out
 
 
-def plan_kernel(start_high, cap_owner, parts, coef_out, normal_out, packed_out, slot_out, flag, rows):
+def plan_kernel(start_high, parts, coef_out, normal_out, packed_out, slot_out, flag, rows):
     owners = 8
     ny = parts.shape[0] // owners
     for o in range(owners):
@@ -289,7 +293,8 @@
     normal_out[...] = normal
     packed_out[...] = jnp.where(active, rank_owner, -1.0)
     slot_out[...] = jnp.where(active, rank_group + start, -1.0)
-    over = jnp.where(active & ((rank_owner >= cap_owner) | (rank_group >= CAP)), 1.0, 0.0)
+    over = jnp.where(active & (rank_owner >= CAP_SMALL), 1.0, 0.0)
+    over = jnp.where(active & (rank_group >= CAP), 2.0, over)
     flag[0, 0] = jnp.max(over).astype(jnp.int32)
 
 
@@ -320,56 +325,62 @@
         out[:, span] = jnp.dot(choose, slopes, preferred_element_type=f32).astype(bf16)
 
 
-def product_kernel(nx, at, mine, theirs, turned, packed_all, slot_all, out, held):
+def owner_of(at, s, k):
+    return lax.rem(at[0] - s + NX, NX) * 2 + lax.rem(at[1] + k, 2)
+
+
+def product_kernel(at, mine, theirs, turned, o0, o1, o2, o3, held):
+    cap = mine.shape[0] // NX
+    for k, rows in enumerate((mine, theirs)):
+        held[k * NX * cap : (k + 1) * NX * cap, :] = jnp.dot(
+            rows[...], turned[...], preferred_element_type=f32
+        ).astype(bf16)
+    for step, out in enumerate((o0, o1, o2, o3)):
+        source = lax.rem(at[0] - at[5] - step + 2 * NX, NX) * cap
+        for k in range(2):
+            rows = pl.ds(pl.multiple_of(source + k * NX * cap, cap), cap)
+            out[k * cap : (k + 1) * cap, :] = held[rows, :]
+
+
+def outer_kernel(at, packed_all, hid_mine, hid_theirs, mine, theirs, out, tick, held):
     half = mine.shape[0]
-    count = half // nx
-    for k, rows in enumerate((mine, theirs)):
-        held[k * half : (k + 1) * half, :] = lax.dot_general(
-            rows[...], turned[...], (((1,), (0,)), ((), ())), preferred_element_type=f32
-        ).astype(bf16)
-    size = out.shape[0] // (2 * nx)
-    for owner in range(2 * nx):
-        to, core = owner // 2, owner % 2
-        source = lax.rem(at[0] - to + nx, nx) * count + lax.rem(at[1] + core, 2) * half
-        block = held[pl.ds(pl.multiple_of(source, 16), count), :]
+    cap = half // NX
+    tick[...] = jnp.zeros(tick.shape, f32)
+    for k, hidden in enumerate((hid_mine, hid_theirs)):
+        for s in range(NX):
+            choose = one_hot(cap, packed_all[pl.ds(owner_of(at, s, k), 1), :])
+            to = k * half + s * cap
+            held[to : to + cap, :] = jnp.dot(
+                choose, hidden[ORDER[s] * 128 : (ORDER[s] + 1) * 128, :], preferred_element_type=f32
+            ).astype(bf16)
+    slopes = jnp.concatenate([mine[...], theirs[...]], axis=0)
+    out[...] = lax.dot_general(held[...], slopes, (((0,), (0,)), ((), ())), preferred_element_type=f32)
+
+
+def spread_kernel(at, tick, r0, r1, r2, r3, packed_all, slot_all, out):
+    size = out.shape[0]
+    cap = r0.shape[0] // 2
+    total = jnp.zeros(out.shape, f32)
+    for k in range(2):
+        core = lax.rem(at[1] + k, 2)
+        me = pl.ds(at[5] * 2 + core, 1)
+        slot = slot_all[me, :]
+        slot = jnp.where(slot >= 0.0, slot + (core * (size // 2)).astype(f32), -1.0)
         spread = lax.dot_general(
-            one_hot(size, slot_all[owner : owner + 1, :]),
-            one_hot(count, packed_all[owner : owner + 1, :]),
+            one_hot(size, slot),
+            one_hot(cap, packed_all[me, :]),
             (((1,), (1,)), ((), ())),
             preferred_element_type=f32,
         ).astype(bf16)
-        out[owner * size : (owner + 1) * size, :] = jnp.dot(
-            spread, block, preferred_element_type=f32
-        ).astype(bf16)
-
-
-def outer_kernel(nx, at, packed_all, hid_mine, hid_theirs, mine, theirs, out, held):
-    half = mine.shape[0]
-    count = half // nx
-    for k, hidden in enumerate((hid_mine, hid_theirs)):
-        for s in range(nx):
-            owner = lax.rem(at[0] - s + nx, nx) * 2 + lax.rem(at[1] + k, 2)
-            choose = one_hot(count, packed_all[pl.ds(owner, 1), :])
-            to = k * half + s * count
-            held[to : to + count, :] = jnp.dot(
-                choose, hidden[ORDER[s] * 128 : (ORDER[s] + 1) * 128, :], preferred_element_type=f32
-            ).astype(bf16)
-    total = jnp.zeros(out.shape, f32)
-    for k, rows in enumerate((mine, theirs)):
-        total = total + lax.dot_general(
-            held[k * half : (k + 1) * half, :],
-            rows[...],
-            (((0,), (0,)), ((), ())),
-            preferred_element_type=f32,
-        )
+        for r in (r0, r1, r2, r3):
+            total = total + jnp.dot(spread, r[k * cap : (k + 1) * cap, :], preferred_element_type=f32)
     out[...] = total
 
 
 def sum_kernel(at, parts, slot_all, out, ranks):
-    n_voc = parts.shape[0] // CAP
-    total = parts[0:CAP, :].astype(f32)
-    for i in range(1, n_voc):
-        total = total + parts[i * CAP : (i + 1) * CAP, :].astype(f32)
+    total = parts[0:CAP, :]
+    for i in range(1, parts.shape[0] // CAP):
+        total = total + parts[i * CAP : (i + 1) * CAP, :]
     group = out.shape[0]
     per_owner = 128 // group
     owner, place = at[4] // per_owner, lax.rem(at[4], per_owner)
@@ -387,7 +398,7 @@
     rows, voc_cols = head.shape
     nx, n_voc, n_dp = lax.axis_size("x"), lax.axis_size(VOC), lax.axis_size(DP)
     x, c, block = lax.axis_index("x"), lax.axis_index("c"), lax.axis_index(VOC)
-    at = jnp.stack([x, c, x * 2 + c, block * voc_cols, block]).astype(jnp.int32)
+    at = jnp.stack([x, c, x * 2 + c, block * voc_cols, block, lax.axis_index("y")]).astype(jnp.int32)
     chip_rows = width // nx
 
     head_other = lax.ppermute(head, "c", SWAP)
@@ -395,31 +406,37 @@
     block_shape = struct((tokens, chip_rows), bf16)
     b0, *leave = call(split_kernel, [block_shape] * 4, [at, hidden_states], smem=1)
     came = {s: lax.ppermute(leave[s - 1], "x", ring(nx, s)) for s in (2, 1, 3)}
-    kept, turned = call(
-        turn_kernel, [struct((rows, voc_cols), bf16), struct((voc_cols, rows), bf16)], [head]
+    partial = struct((tokens, voc_cols), f32)
+    tick_shape = struct((8, 128), f32)
+    own, kept = call(
+        own_kernel,
+        [partial, struct((rows, voc_cols), bf16)],
+        [at, b0, head, head_other],
+        smem=1,
+        cost_estimate=estimate(tokens, chip_rows, voc_cols),
     )
     half = struct((tokens // 2, voc_cols + 128), jnp.int16)
     low, high, tick = call(
         far_kernel,
-        [half, half, struct((8, 128), f32)],
+        [half, half, tick_shape],
         [at, came[2], kept, head_other],
         [pltpu.VMEM((tokens, voc_cols), f32)],
         smem=1,
         cost_estimate=estimate(tokens, chip_rows, voc_cols),
     )
     low, high = lax.ppermute(low, "x", ring(nx, -1)), lax.ppermute(high, "x", ring(nx, 1))
-    partial = struct((tokens, voc_cols), f32)
-    own, p1, p3, hid_mine, hid_send = call(
+    p1, p3, hid_mine, hid_send = call(
         near_kernel,
-        [partial] * 3 + [struct((nx * tokens, rows), bf16)] * 2,
+        [partial] * 2 + [struct((nx * tokens, rows), bf16)] * 2,
         [at, tick, b0, came[1], came[2], came[3], kept, head_other],
         vmem=24,
         smem=1,
-        cost_estimate=estimate(3 * tokens, chip_rows, voc_cols),
+        cost_estimate=estimate(2 * tokens, chip_rows, voc_cols),
     )
     packed = struct((tokens, voc_cols + 128), jnp.int16)
-    q1, q3 = call(relay_kernel, [packed] * 2, [p1, p3, low, high])
+    q1, q3, tick = call(relay_kernel, [packed] * 2 + [tick_shape], [p1, p3, low, high])
     q1, q3 = lax.ppermute(q1, "x", ring(nx, -1)), lax.ppermute(q3, "x", ring(nx, 1))
+    turned = call(turn_kernel, struct((voc_cols, rows), bf16), [tick, kept])
     hid_theirs = lax.ppermute(hid_send, "c", SWAP)
     logits, stats = call(
         total_kernel,
@@ -439,57 +456,61 @@
     start_high = float(np.float32(np.log(np.float32(voc_cols * n_voc))) + np.float32(1.0))
     table = struct((n_dp, tokens), f32)
     coef_all, normal_all, packed_all, slot_all, flag = call(
-        functools.partial(plan_kernel, start_high, CAP_OWNER),
+        functools.partial(plan_kernel, start_high),
         [table] * 4 + [struct((1, 1), jnp.int32)],
         [stats],
         [pltpu.VMEM((n_dp, 8, 128), f32)],
         out_specs=[pl.BlockSpec(memory_space=pltpu.VMEM)] * 4 + [pl.BlockSpec(memory_space=pltpu.SMEM)],
     )
 
-    def sparse(_):
+    def sparse(cap, _):
         piece = call(
             slopes_kernel,
-            struct((CAP_OWNER, voc_cols), bf16),
+            struct((cap, voc_cols), bf16),
             [at, logits, coef_all, normal_all, packed_all, token_ids.reshape(1, tokens)],
             smem=1,
         )
         pieces = {s: lax.ppermute(piece, "x", ring(nx, s)) for s in (2, 1, 3)}
         mine = jnp.concatenate([piece, pieces[1], pieces[2], pieces[3]], axis=0)
         theirs = lax.ppermute(mine, "c", SWAP)
-        product = call(
-            functools.partial(product_kernel, nx),
-            struct((n_voc * CAP, rows), bf16),
-            [at, mine, theirs, turned, packed_all, slot_all],
-            [pltpu.VMEM((2 * nx * CAP_OWNER, rows), bf16)],
+        parts = call(
+            product_kernel,
+            [struct((2 * cap, rows), bf16)] * nx,
+            [at, mine, theirs, turned],
+            [pltpu.VMEM((2 * nx * cap, rows), bf16)],
             smem=1,
         )
-        parts = lax.all_to_all(product, VOC, 0, 0, tiled=True)
+        parts = [parts[0]] + [lax.ppermute(parts[k], "y", ring(nx, k)) for k in range(1, nx)]
         tile = 128
-        head_grad = pl.pallas_call(
-            functools.partial(outer_kernel, nx),
+        whole_block = lambda i: (0, 0)
+        head_grad, tick = pl.pallas_call(
+            outer_kernel,
             grid=(rows // tile,),
             in_specs=[
                 pl.BlockSpec(memory_space=pltpu.SMEM),
-                pl.BlockSpec((n_dp, tokens), lambda i: (0, 0)),
+                pl.BlockSpec((n_dp, tokens), whole_block),
                 pl.BlockSpec((nx * tokens, tile), lambda i: (0, i)),
                 pl.BlockSpec((nx * tokens, tile), lambda i: (0, i)),
-                pl.BlockSpec((nx * CAP_OWNER, voc_cols), lambda i: (0, 0)),
-                pl.BlockSpec((nx * CAP_OWNER, voc_cols), lambda i: (0, 0)),
+                pl.BlockSpec((nx * cap, voc_cols), whole_block),
+                pl.BlockSpec((nx * cap, voc_cols), whole_block),
             ],
-            out_specs=pl.BlockSpec((tile, voc_cols), lambda i: (i, 0)),
-            out_shape=struct((rows, voc_cols), f32),
-            scratch_shapes=[pltpu.VMEM((2 * nx * CAP_OWNER, tile), bf16)],
+            out_specs=[pl.BlockSpec((tile, voc_cols), lambda i: (i, 0)), pl.BlockSpec((8, 128), whole_block)],
+            out_shape=[struct((rows, voc_cols), f32), tick_shape],
+            scratch_shapes=[pltpu.VMEM((2 * nx * cap, tile), bf16)],
             compiler_params=pltpu.CompilerParams(vmem_limit_bytes=24 << 20),
-            cost_estimate=pl.CostEstimate(
-                flops=4 * nx * CAP_OWNER * rows * voc_cols,
-                bytes_accessed=4 * rows * voc_cols,
-                transcendentals=0,
-            ),
+            cost_estimate=estimate(rows, 2 * nx * cap, voc_cols),
         )(at, packed_all, hid_mine, hid_theirs, mine, theirs)
+        spread = call(
+            spread_kernel,
+            struct((n_voc * CAP // nx, rows), f32),
+            [at, tick, *parts, packed_all, slot_all],
+            smem=1,
+        )
+        spread = lax.all_to_all(spread, "z", 0, 0, tiled=True)
         hidden_grad = call(
             sum_kernel,
             struct((tokens * n_dp // n_voc, rows), f32),
-            [at, parts, slot_all],
+            [at, spread, slot_all],
             [pltpu.VMEM((tokens, 8), f32)],
             smem=1,
         )
@@ -498,7 +519,9 @@
     def whole(_):
         return dense(hidden_states, head, token_ids, valid, advantage)
 
-    return lax.cond(flag[0, 0] != 0, whole, sparse, 0)
+    small = functools.partial(sparse, CAP_SMALL)
+    large = functools.partial(sparse, CAP * n_voc // n_dp)
+    return lax.switch(flag[0, 0], [small, large, whole], 0)
 
 
 def solution(mesh):

time: 146 us -> 144 us (0.986)
  blocking collectives: 15 us -> 30.5 us
  waiting for transfers between devices: 56.7 us -> 41.2 us
    all_to_all x0 -> x1, blocking collectives: none -> 15.5 us  [sparse(): spread = lax.all_to_all(spread, 'z', 0, 0, tiled=True)]
    all_to_all x1 -> x0, waiting for transfers between devices: 14.5 us -> none  [sparse(): parts = lax.all_to_all(product, VOC, 0, 0, tiled=True)]
    all_to_all x1 -> x0, starting transfers between devices: 5.01 us -> none  [sparse(): parts = lax.all_to_all(product, VOC, 0, 0, tiled=True)]
    ppermute x0 -> x3, starting transfers between devices: none -> 3.52 us  [sparse(): lax.ppermute(parts[k], 'y', ring(nx, k))]
    ppermute x3, waiting for transfers between devices: 12.4 us -> 9.02 us  [sparse(): pieces = {s: lax.ppermute(piece, 'x', ring(nx, s)) for s in (2, 1, 3)}]
    ppermute x3, waiting for transfers between devices: 1.66 us -> 4.5 us  [shards(): came = {s: lax.ppermute(leave[s - 1], 'x', ring(nx, s)) for s in (2, 1, 3)}]
    all_to_all x1, waiting for transfers between devices: 7.83 us -> 5.04 us  [shards(): stats = lax.all_to_all(stats, everyone, 0, 0, tiled=True)]
    ppermute x1, waiting for transfers between devices: 0.75 us -> 2.86 us  [shards(): lax.ppermute(low, 'x', ring(nx, -1))]
  transfers between devices with their start and end apart: 15 -> 17, of which waited for: 12 -> 12; matrix products, arithmetic and copies ran while one was open for 0% -> 0% of each run, Pallas kernels for 19% -> 18%
where the time goes in v4:
time: 144 us; the launch traced here: 143 us
  waiting for transfers between devices  41.2 us (29%)
  Pallas kernels  33.8 us (23%)
  blocking collectives  30.5 us (21%)
  starting transfers between devices  22.8 us (16%)
  between operations  14.8 us (10%)
    pallas_call x13, Pallas kernels, call(): pl.pallas_call(kernel, in_specs=specs, out_shape=out, scratch_shapes=list...  27.9 us
    all_to_all x1, blocking collectives, sparse(): spread = lax.all_to_all(spread, 'z', 0, 0, tiled=True)  15.5 us
    all_to_all x1, blocking collectives, shards(): stats = lax.all_to_all(stats, 'z', 0, 0, tiled=True)  14.9 us
    ppermute x1, waiting for transfers between devices, shards(): lax.ppermute(q1, 'x', ring(nx, -1))  13.1 us
    ppermute x3, waiting for transfers between devices, sparse(): pieces = {s: lax.ppermute(piece, 'x', ring(nx, s)) for s in (2, 1, 3)}  9.02 us
    ppermute x3, starting transfers between devices, shards(): came = {s: lax.ppermute(leave[s - 1], 'x', ring(nx, s)) for s in (2, 1, 3)}  6.35 us
    pallas_call x1, Pallas kernels, sparse(): pl.pallas_call(outer_kernel, grid=(rows // tile,), in_specs=[pl.BlockSpec...  5.91 us
    all_to_all x1, waiting for transfers between devices, shards(): stats = lax.all_to_all(stats, everyone, 0, 0, tiled=True)  5.04 us
  transfers between devices with their start and end apart: 17, of which 12 were waited for; matrix products, arithmetic and copies ran while one was open for 0% of the time, Pallas kernels for 18%

profile of v4, /device:TPU:32, one launch (start us, length us, event | category | flops | bytes accessed | tf_op | source)
XLA Modules:
  0.0 143.2 jit_solution(1517127972568292070)
XLA Ops:
  8.8 3.1 %collective-permute-start.15 = (bf16[128,1280]{1,0:T(8,128)(2,1)S(1)}, bf16[128,1280]{1,0:T(8,128)(2,1)S(1)}, u32[]{:S(2)}, u32[]{:S(2)}) collective-permute-start(bf16[128,1280]{1,0:T(8,128)(2,1)S(1)} %get-tuple-element.146), channel_id=1, source_target_pairs={{0,128},{64,192},{128,0},{192,64},{1,129},{65,193},{129,1},{193,65... | collective-permute-start | bytes 983048 | tf_op jit(solution)/shard_map/ppermute | solution.py:408
  12.5 2.6 %collective-permute-start.17 = (bf16[128,1280]{1,0:T(8,128)(2,1)S(1)}, bf16[128,1280]{1,0:T(8,128)(2,1)S(1)}, u32[]{:S(2)}, u32[]{:S(2)}) collective-permute-start(bf16[128,1280]{1,0:T(8,128)(2,1)S(1)} %get-tuple-element.150), channel_id=1, source_target_pairs={{0,192},{64,0},{128,64},{192,128},{1,193},{65,1},{129,65},{193,129... | collective-permute-start | bytes 983048 | tf_op jit(solution)/shard_map/ppermute | solution.py:408
  15.1 3.3 %shard_map.72 = (f32[128,2432]{1,0:T(8,128)S(1)}, bf16[640,2432]{1,0:T(8,128)(2,1)S(1)}) custom-call(s32[6]{0:T(128)S(1)} %stack.27.at, bf16[128,1280]{1,0:T(8,128)(2,1)S(1)} %get-tuple-element.144.block.b0, bf16[640,2432]{1,0:T(8,128)(2,1)} %head.1, bf16[640,2432]{1,0:T(8,128)(2,1)S(1)} %collective-permute-done.14.other), custom_call_target="tpu_custom_call" | custom-call | flops 796917760 | bytes 6225920 | tf_op jit(solution)/shard_map/pallas_call | solution.py:96
  18.4 2.5 %collective-permute-done.15.block.b2 = bf16[128,1280]{1,0:T(8,128)(2,1)S(1)} collective-permute-done((bf16[128,1280]{1,0:T(8,128)(2,1)S(1)}, bf16[128,1280]{1,0:T(8,128)(2,1)S(1)}, u32[]{:S(2)}, u32[]{:S(2)}) %collective-permute-start.15) | collective-permute-done | bytes 327712 | tf_op jit(solution)/shard_map/ppermute | solution.py:408
  20.9 2.3 %shard_map.73 = (s16[64,2560]{1,0:T(8,128)(2,1)S(1)}, s16[64,2560]{1,0:T(8,128)(2,1)S(1)}, f32[8,128]{1,0:T(8,128)S(1)}) custom-call(s32[6]{0:T(128)S(1)} %stack.27.at, bf16[128,1280]{1,0:T(8,128)(2,1)S(1)} %collective-permute-done.15.block.b2, bf16[640,2432]{1,0:T(8,128)(2,1)S(1)} %get-tuple-element.147.head, ...), custom_call_target="tpu_custom_call" | custom-call | flops 796917760 | bytes 6225920 | tf_op jit(solution)/shard_map/pallas_call | solution.py:96
  23.2 2.8 %collective-permute-start.18 = (s16[64,2560]{1,0:T(8,128)(2,1)S(1)}, s16[64,2560]{1,0:T(8,128)(2,1)S(1)}, u32[]{:S(2)}, u32[]{:S(2)}) collective-permute-start(s16[64,2560]{1,0:T(8,128)(2,1)S(1)} %get-tuple-element.153), channel_id=1, source_target_pairs={{0,192},{64,0},{128,64},{192,128},{1,193},{65,1},{129,65},{193,129... | collective-permute-start | bytes 983048 | tf_op jit(solution)/shard_map/ppermute | solution.py:427
  28.0 3.7 %shard_map.74 = (f32[128,2432]{1,0:T(8,128)S(1)}, f32[128,2432]{1,0:T(8,128)S(1)}, bf16[512,640]{1,0:T(8,128)(2,1)}, bf16[512,640]{1,0:T(8,128)(2,1)}) custom-call(s32[6]{0:T(128)S(1)} %stack.27.at, f32[8,128]{1,0:T(8,128)S(1)} %get-tuple-element.148.tick, bf16[128,1280]{1,0:T(8,128)(2,1)S(1)} %get-tuple-element.144.block.b0, ...), custom_call_target="tpu_custom_call" | custom-call | flops 1593835520 | bytes 6225920 | tf_op jit(solution)/shard_map/pallas_call | solution.py:96
  31.8 2.9 %collective-permute-done.18.low = s16[64,2560]{1,0:T(8,128)(2,1)S(1)} collective-permute-done((s16[64,2560]{1,0:T(8,128)(2,1)S(1)}, s16[64,2560]{1,0:T(8,128)(2,1)S(1)}, u32[]{:S(2)}, u32[]{:S(2)}) %collective-permute-start.18) | collective-permute-done | bytes 327712 | tf_op jit(solution)/shard_map/ppermute | solution.py:427
  38.7 13.1 %collective-permute-done.20.q1 = s16[128,2560]{1,0:T(8,128)(2,1)S(1)} collective-permute-done((s16[128,2560]{1,0:T(8,128)(2,1)S(1)}, s16[128,2560]{1,0:T(8,128)(2,1)S(1)}, u32[]{:S(2)}, u32[]{:S(2)}) %collective-permute-start.20) | collective-permute-done | bytes 655392 | tf_op jit(solution)/shard_map/ppermute | solution.py:438
  51.8 3.4 %collective-permute-done.21.q3 = s16[128,2560]{1,0:T(8,128)(2,1)S(1)} collective-permute-done((s16[128,2560]{1,0:T(8,128)(2,1)S(1)}, s16[128,2560]{1,0:T(8,128)(2,1)S(1)}, u32[]{:S(2)}, u32[]{:S(2)}) %collective-permute-start.21) | collective-permute-done | bytes 655392 | tf_op jit(solution)/shard_map/ppermute | solution.py:438
  55.1 3.2 %shard_map.76 = (f32[128,2432]{1,0:T(8,128)}, f32[8,8,128]{2,1,0:T(8,128)S(1)}) custom-call(f32[128,2432]{1,0:T(8,128)S(1)} %get-tuple-element.145.own, s16[128,2560]{1,0:T(8,128)(2,1)S(1)} %collective-permute-done.20.q1, s16[128,2560]{1,0:T(8,128)(2,1)S(1)} %collective-permute-done.21.q3), custom_call_target="tpu_custom_call" | custom-call | tf_op jit(solution)/shard_map/pallas_call | solution.py:96
  58.4 14.9 %all_to_all.44.parts = f32[8,8,128]{2,1,0:T(8,128)S(1)} all-to-all(f32[8,8,128]{2,1,0:T(8,128)S(1)} %get-tuple-element.157), channel_id=1, replica_groups=mesh['x'=4,'c'=2,'y'=4,'z'=8] {'z'}, dimensions={0} | all-to-all | bytes 65536 | tf_op jit(solution)/shard_map/all_to_all | solution.py:448
  74.0 5.0 %all-to-all-start.4 = ((f32[32,8,128]{2,1,0:T(8,128)}), f32[32,8,128]{2,1,0:T(8,128)S(1)}, u32[]{:S(2)}, u32[]{:S(2)}) async-start(f32[32,8,128]{2,1,0:T(8,128)} %shard_map.77), calls=%async_computation.6 | async-start | bytes 262144 | tf_op jit(solution)/shard_map/all_to_all | solution.py:455
  79.1 2.6 %shard_map.79 = bf16[2432,640]{1,0:T(8,128)(2,1)} custom-call(f32[8,128]{1,0:T(8,128)S(1)} %get-tuple-element.165.tick, bf16[640,2432]{1,0:T(8,128)(2,1)S(1)} %copy-done.1), custom_call_target="tpu_custom_call" | custom-call | tf_op jit(solution)/shard_map/pallas_call | solution.py:96
  81.7 5.0 %all-to-all-done.4.parts = f32[32,8,128]{2,1,0:T(8,128)S(1)} async-done(((f32[32,8,128]{2,1,0:T(8,128)}), f32[32,8,128]{2,1,0:T(8,128)S(1)}, u32[]{:S(2)}, u32[]{:S(2)}) %all-to-all-start.4) | async-done | bytes 131104 | tf_op jit(solution)/shard_map/all_to_all | solution.py:455
  86.7 2.1 %shard_map.78 = (f32[8,128]{1,0:T(8,128)S(1)}, f32[8,128]{1,0:T(8,128)S(1)}, f32[8,128]{1,0:T(8,128)S(1)}, f32[8,128]{1,0:T(8,128)S(1)}, s32[1,1]{1,0:T(1,128)}) custom-call(f32[32,8,128]{2,1,0:T(8,128)S(1)} %all-to-all-done.4.parts), custom_call_target="tpu_custom_call" | custom-call | tf_op jit(solution)/shard_map/pallas_call | solution.py:96
  89.5 46.9 %conditional.1 = (f32[32,640]{1,0:T(8,128)}, f32[640,2432]{1,0:T(8,128)}) conditional(s32[]{:T(128)} %bitcast.18, (s32[128]{0:T(128)S(1)}, s32[6]{0:T(128)S(1)}, f32[128,2432]{1,0:T(8,128)}, f32[8,128]{1,0:T(8,128)S(1)}, f32[8,128]{1,0:T(8,128)S(1)}, /*index=5*/f32[8,128]{1,0:T(8,128)S(1)}, bf16[512,640]{1,0:T(8,128)(2,1)}, ...), branch_computations={%region_0.0_spmd, %region_1.0_spmd, %region_2.17_spmd} | conditional | flops 9566442496 | bytes 125846592 | solution.py:524
  94.1 4.2 %collective-permute-done.2 = bf16[32,2432]{1,0:T(8,128)(2,1)S(1)} collective-permute-done((bf16[32,2432]{1,0:T(8,128)(2,1)S(1)}, bf16[32,2432]{1,0:T(8,128)(2,1)S(1)}, u32[]{:S(2)}, u32[]{:S(2)}) %collective-permute-start.2) | collective-permute-done | bytes 155680 | tf_op jit(solution)/shard_map/cond/branch_0_fun/ppermute | solution.py:473
  98.3 2.6 %collective-permute-done.1 = bf16[32,2432]{1,0:T(8,128)(2,1)S(1)} collective-permute-done((bf16[32,2432]{1,0:T(8,128)(2,1)S(1)}, bf16[32,2432]{1,0:T(8,128)(2,1)S(1)}, u32[]{:S(2)}, u32[]{:S(2)}) %collective-permute-start.1) | collective-permute-done | bytes 155680 | tf_op jit(solution)/shard_map/cond/branch_0_fun/ppermute | solution.py:473
  101.0 2.2 %collective-permute-done = bf16[32,2432]{1,0:T(8,128)(2,1)S(1)} collective-permute-done((bf16[32,2432]{1,0:T(8,128)(2,1)S(1)}, bf16[32,2432]{1,0:T(8,128)(2,1)S(1)}, u32[]{:S(2)}, u32[]{:S(2)}) %collective-permute-start) | collective-permute-done | bytes 155680 | tf_op jit(solution)/shard_map/cond/branch_0_fun/ppermute | solution.py:473
  103.3 2.0 %collective-permute-done.3.theirs = bf16[128,2432]{1,0:T(8,128)(2,1)S(1)} collective-permute-done((bf16[128,2432]{1,0:T(8,128)(2,1)S(1)}, bf16[128,2432]{1,0:T(8,128)(2,1)S(1)}, u32[]{:S(2)}, u32[]{:S(2)}) %collective-permute-start.3) | collective-permute-done | bytes 622624 | tf_op jit(solution)/shard_map/cond/branch_0_fun/ppermute | solution.py:475
  105.4 3.2 %branch_0_fun.7 = (bf16[64,640]{1,0:T(8,128)(2,1)S(1)}, bf16[64,640]{1,0:T(8,128)(2,1)S(1)}, bf16[64,640]{1,0:T(8,128)(2,1)S(1)}, bf16[64,640]{1,0:T(8,128)(2,1)S(1)}) custom-call(s32[6]{0:T(128)S(1)} %get-tuple-element.74.at, bf16[128,2432]{1,0:T(8,128)(2,1)S(1)} %pad_maximum_fusion.mine, bf16[128,2432]{1,0:T(8,128)(2,1)S(1)} %collective-permute-done.3.theirs, ...), custom_call_target="tpu_custom_call" | custom-call | tf_op jit(solution)/shard_map/cond/branch_0_fun/pallas_call | solution.py:96
  112.1 5.9 %branch_0_fun.6 = (f32[640,2432]{1,0:T(8,128)}, f32[8,128]{1,0:T(8,128)S(1)}) custom-call(s32[6]{0:T(128)S(1)} %get-tuple-element.74.at, f32[8,128]{1,0:T(8,128)S(1)} %get-tuple-element.75.packed_all, bf16[512,640]{1,0:T(8,128)(2,1)S(1)} %copy-done.7, bf16[512,640]{1,0:T(8,128)(2,1)} %get-tuple-element.77.hid_theirs, ...), custom_call_target="tpu_custom_call" | custom-call | flops 796917760 | bytes 1245184 | tf_op jit(solution)/shard_map/cond/branch_0_fun/pallas_call | solution.py:486
  119.3 15.5 %all_to_all.41 = f32[8,16,640]{2,1,0:T(8,128)S(1)} all-to-all(f32[8,16,640]{2,1,0:T(8,128)S(1)} %bitcast.27), channel_id=1, replica_groups=mesh['x'=4,'c'=2,'y'=4,'z'=8] {'z'}, dimensions={0} | all-to-all | bytes 655360 | tf_op jit(solution)/shard_map/cond/branch_0_fun/all_to_all | solution.py:509
  (41 shorter events, 20.1 us)
Async XLA Ops:
  7.2 8.0 %collective-permute-start.14 = (bf16[640,2432]{1,0:T(8,128)(2,1)}, bf16[640,2432]{1,0:T(8,128)(2,1)S(1)}, u32[]{:S(2)}, u32[]{:S(2)}) collective-permute-start(bf16[640,2432]{1,0:T(8,128)(2,1)} %head.1), channel_id=1, source_target_pairs={{0,32},{32,0},{1,33},{33,1},{2,34},{34,2},{3,35},{35,3},{4,36},{36... | collective-permute-start | bytes 9338888 | tf_op jit(solution)/shard_map/ppermute | solution.py:404
  8.8 12.1 %collective-permute-start.15 = (bf16[128,1280]{1,0:T(8,128)(2,1)S(1)}, bf16[128,1280]{1,0:T(8,128)(2,1)S(1)}, u32[]{:S(2)}, u32[]{:S(2)}) collective-permute-start(bf16[128,1280]{1,0:T(8,128)(2,1)S(1)} %get-tuple-element.146), channel_id=1, source_target_pairs={{0,128},{64,192},{128,0},{192,64},{1,129},{65,193},{129,1},{193,65... | collective-permute-start | bytes 983048 | tf_op jit(solution)/shard_map/ppermute | solution.py:408
  11.9 15.6 %collective-permute-start.16 = (bf16[128,1280]{1,0:T(8,128)(2,1)S(1)}, bf16[128,1280]{1,0:T(8,128)(2,1)S(1)}, u32[]{:S(2)}, u32[]{:S(2)}) collective-permute-start(bf16[128,1280]{1,0:T(8,128)(2,1)S(1)} %get-tuple-element.149), channel_id=1, source_target_pairs={{0,64},{64,128},{128,192},{192,0},{1,65},{65,129},{129,193},{193,1... | collective-permute-start | bytes 983048 | tf_op jit(solution)/shard_map/ppermute | solution.py:408
  12.5 15.5 %collective-permute-start.17 = (bf16[128,1280]{1,0:T(8,128)(2,1)S(1)}, bf16[128,1280]{1,0:T(8,128)(2,1)S(1)}, u32[]{:S(2)}, u32[]{:S(2)}) collective-permute-start(bf16[128,1280]{1,0:T(8,128)(2,1)S(1)} %get-tuple-element.150), channel_id=1, source_target_pairs={{0,192},{64,0},{128,64},{192,128},{1,193},{65,1},{129,65},{193,129... | collective-permute-start | bytes 983048 | tf_op jit(solution)/shard_map/ppermute | solution.py:408
  18.4 9.6 %copy-start = (bf16[640,2432]{1,0:T(8,128)(2,1)}, bf16[640,2432]{1,0:T(8,128)(2,1)S(1)}, u32[]{:S(2)}) copy-start(bf16[640,2432]{1,0:T(8,128)(2,1)S(1)} %get-tuple-element.147.head) | copy-start | bytes 9338884
  23.2 11.5 %collective-permute-start.18 = (s16[64,2560]{1,0:T(8,128)(2,1)S(1)}, s16[64,2560]{1,0:T(8,128)(2,1)S(1)}, u32[]{:S(2)}, u32[]{:S(2)}) collective-permute-start(s16[64,2560]{1,0:T(8,128)(2,1)S(1)} %get-tuple-element.153), channel_id=1, source_target_pairs={{0,192},{64,0},{128,64},{192,128},{1,193},{65,1},{129,65},{193,129... | collective-permute-start | bytes 983048 | tf_op jit(solution)/shard_map/ppermute | solution.py:427
  26.0 9.8 %collective-permute-start.19 = (s16[64,2560]{1,0:T(8,128)(2,1)S(1)}, s16[64,2560]{1,0:T(8,128)(2,1)S(1)}, u32[]{:S(2)}, u32[]{:S(2)}) collective-permute-start(s16[64,2560]{1,0:T(8,128)(2,1)S(1)} %get-tuple-element.154), channel_id=1, source_target_pairs={{0,64},{64,128},{128,192},{192,0},{1,65},{65,129},{129,193},{193,1... | collective-permute-start | bytes 983048 | tf_op jit(solution)/shard_map/ppermute | solution.py:427
  35.9 43.2 %copy-start.1 = (bf16[640,2432]{1,0:T(8,128)(2,1)S(1)}, bf16[640,2432]{1,0:T(8,128)(2,1)}, u32[]{:S(2)}) copy-start(bf16[640,2432]{1,0:T(8,128)(2,1)} %copy-done) | copy-start | bytes 9338884
  36.6 15.2 %collective-permute-start.20 = (s16[128,2560]{1,0:T(8,128)(2,1)S(1)}, s16[128,2560]{1,0:T(8,128)(2,1)S(1)}, u32[]{:S(2)}, u32[]{:S(2)}) collective-permute-start(s16[128,2560]{1,0:T(8,128)(2,1)S(1)} %get-tuple-element.155), channel_id=1, source_target_pairs={{0,192},{64,0},{128,64},{192,128},{1,193},{65,1},{129,65},{193,129... | collective-permute-start | bytes 1966088 | tf_op jit(solution)/shard_map/ppermute | solution.py:438
  38.1 17.1 %collective-permute-start.21 = (s16[128,2560]{1,0:T(8,128)(2,1)S(1)}, s16[128,2560]{1,0:T(8,128)(2,1)S(1)}, u32[]{:S(2)}, u32[]{:S(2)}) collective-permute-start(s16[128,2560]{1,0:T(8,128)(2,1)S(1)} %get-tuple-element.156), channel_id=1, source_target_pairs={{0,64},{64,128},{128,192},{192,0},{1,65},{65,129},{129,193},{193,1... | collective-permute-start | bytes 1966088 | tf_op jit(solution)/shard_map/ppermute | solution.py:438
  38.7 50.8 %collective-permute-start.22 = (bf16[512,640]{1,0:T(8,128)(2,1)}, bf16[512,640]{1,0:T(8,128)(2,1)}, u32[]{:S(2)}, u32[]{:S(2)}) collective-permute-start(bf16[512,640]{1,0:T(8,128)(2,1)} %get-tuple-element.164), channel_id=1, source_target_pairs={{0,32},{32,0},{1,33},{33,1},{2,34},{34,2},{3,35},{35,3},{4,36},{36... | collective-permute-start | bytes 1966088 | tf_op jit(solution)/shard_map/ppermute | solution.py:440
  55.1 18.2 %copy-start.5 = (s32[128]{0:T(128)S(1)}, s32[128]{0:T(128)}, u32[]{:S(2)}) copy-start(s32[128]{0:T(128)} %param.13) | copy-start | bytes 1540
  55.1 18.2 %copy-start.6 = (f32[128]{0:T(128)S(1)}, f32[128]{0:T(128)}, u32[]{:S(2)}) copy-start(f32[128]{0:T(128)} %param.14) | copy-start | bytes 1540
  74.0 12.7 %all-to-all-start.4 = ((f32[32,8,128]{2,1,0:T(8,128)}), f32[32,8,128]{2,1,0:T(8,128)S(1)}, u32[]{:S(2)}, u32[]{:S(2)}) async-start(f32[32,8,128]{2,1,0:T(8,128)} %shard_map.77), calls=%async_computation.6 | async-start | bytes 262144 | tf_op jit(solution)/shard_map/all_to_all | solution.py:455
  79.1 10.4 %copy-start.4 = (s32[128]{0:T(128)S(1)}, s32[128]{0:T(128)}, u32[]{:S(2)}) copy-start(s32[128]{0:T(128)} %param.12) | copy-start | bytes 1540
  91.4 7.0 %collective-permute-start.2 = (bf16[32,2432]{1,0:T(8,128)(2,1)S(1)}, bf16[32,2432]{1,0:T(8,128)(2,1)S(1)}, u32[]{:S(2)}, u32[]{:S(2)}) collective-permute-start(bf16[32,2432]{1,0:T(8,128)(2,1)S(1)} %branch_0_fun.5), channel_id=1, source_target_pairs={{0,192},{64,0},{128,64},{192,128},{1,193},{65,1},{129,65},{193,129... | collective-permute-start | bytes 466952 | tf_op jit(solution)/shard_map/cond/branch_0_fun/ppermute | solution.py:473
  92.6 8.4 %collective-permute-start.1 = (bf16[32,2432]{1,0:T(8,128)(2,1)S(1)}, bf16[32,2432]{1,0:T(8,128)(2,1)S(1)}, u32[]{:S(2)}, u32[]{:S(2)}) collective-permute-start(bf16[32,2432]{1,0:T(8,128)(2,1)S(1)} %branch_0_fun.5), channel_id=1, source_target_pairs={{0,128},{64,192},{128,0},{192,64},{1,129},{65,193},{129,1},{193,65... | collective-permute-start | bytes 466952 | tf_op jit(solution)/shard_map/cond/branch_0_fun/ppermute | solution.py:473
  94.1 9.1 %collective-permute-start = (bf16[32,2432]{1,0:T(8,128)(2,1)S(1)}, bf16[32,2432]{1,0:T(8,128)(2,1)S(1)}, u32[]{:S(2)}, u32[]{:S(2)}) collective-permute-start(bf16[32,2432]{1,0:T(8,128)(2,1)S(1)} %branch_0_fun.5), channel_id=1, source_target_pairs={{0,64},{64,128},{128,192},{192,0},{1,65},{65,129},{129,193},{193,1... | collective-permute-start | bytes 466952 | tf_op jit(solution)/shard_map/cond/branch_0_fun/ppermute | solution.py:473
  103.2 2.1 %collective-permute-start.3 = (bf16[128,2432]{1,0:T(8,128)(2,1)S(1)}, bf16[128,2432]{1,0:T(8,128)(2,1)S(1)}, u32[]{:S(2)}, u32[]{:S(2)}) collective-permute-start(bf16[128,2432]{1,0:T(8,128)(2,1)S(1)} %pad_maximum_fusion.mine), channel_id=1, source_target_pairs={{0,32},{32,0},{1,33},{33,1},{2,34},{34,2},{3,35},{35,3},{4,36},{36... | collective-permute-start | bytes 1867784 | tf_op jit(solution)/shard_map/cond/branch_0_fun/ppermute | solution.py:475
  105.4 6.7 %copy-start.7 = (bf16[512,640]{1,0:T(8,128)(2,1)S(1)}, bf16[512,640]{1,0:T(8,128)(2,1)}, u32[]{:S(2)}) copy-start(bf16[512,640]{1,0:T(8,128)(2,1)} %get-tuple-element.76.hid_mine) | copy-start | bytes 1966084 | tf_op jit(solution)/shard_map/cond
  108.5 9.4 %collective-permute-start.4 = (bf16[64,640]{1,0:T(8,128)(2,1)S(1)}, bf16[64,640]{1,0:T(8,128)(2,1)S(1)}, u32[]{:S(2)}, u32[]{:S(2)}) collective-permute-start(bf16[64,640]{1,0:T(8,128)(2,1)S(1)} %get-tuple-element.85), channel_id=1, source_target_pairs={{0,8},{8,16},{16,24},{24,0},{1,9},{9,17},{17,25},{25,1},{2,10},{10... | collective-permute-start | bytes 245768 | tf_op jit(solution)/shard_map/cond/branch_0_fun/ppermute | solution.py:483
  109.1 8.8 %collective-permute-start.5 = (bf16[64,640]{1,0:T(8,128)(2,1)S(1)}, bf16[64,640]{1,0:T(8,128)(2,1)S(1)}, u32[]{:S(2)}, u32[]{:S(2)}) collective-permute-start(bf16[64,640]{1,0:T(8,128)(2,1)S(1)} %get-tuple-element.86), channel_id=1, source_target_pairs={{0,16},{8,24},{16,0},{24,8},{1,17},{9,25},{17,1},{25,9},{2,18},{10... | collective-permute-start | bytes 245768 | tf_op jit(solution)/shard_map/cond/branch_0_fun/ppermute | solution.py:483
  111.0 7.0 %collective-permute-start.6 = (bf16[64,640]{1,0:T(8,128)(2,1)S(1)}, bf16[64,640]{1,0:T(8,128)(2,1)S(1)}, u32[]{:S(2)}, u32[]{:S(2)}) collective-permute-start(bf16[64,640]{1,0:T(8,128)(2,1)S(1)} %get-tuple-element.87), channel_id=1, source_target_pairs={{0,24},{8,0},{16,8},{24,16},{1,25},{9,1},{17,9},{25,17},{2,26},{10... | collective-permute-start | bytes 245768 | tf_op jit(solution)/shard_map/cond/branch_0_fun/ppermute | solution.py:483

commit v5 on v4

--- a/solution.py
+++ b/solution.py
@@ -90,9 +90,10 @@
     return high[:, :1]
 
 
-def call(kernel, out, args, scratch=(), vmem=16, smem=0, **kw):
+def call(kernel, out, args, scratch=(), vmem=16, smem=0, loose=0, **kw):
     specs = [pl.BlockSpec(memory_space=pltpu.SMEM)] * smem
-    specs += [pl.BlockSpec(memory_space=pltpu.VMEM)] * (len(args) - smem)
+    specs += [pl.BlockSpec(memory_space=pltpu.VMEM)] * (len(args) - smem - loose)
+    specs += [pl.BlockSpec(memory_space=pl.ANY)] * loose
     return pl.pallas_call(
         kernel,
         in_specs=specs,
@@ -222,16 +223,13 @@
         pack(p3[far, :] + unpack(high, near), q3, far)
 
 
-def total_kernel(own, q1, q3, logits, sent, stats):
+def total_kernel(own, q1, q3, turned, theirs, logits, sent, stats):
     tokens = own.shape[0]
     step = 16
     lane = lax.broadcasted_iota(jnp.int32, (step, 128), 1)
-
-    @pl.loop(0, tokens // step)
-    def _(i):
-        at = pl.ds(pl.multiple_of(i * step, step), step)
-        value = own[at, :]
-        value = value + unpack(q1, at) + unpack(q3, at)
+    for start in range(0, tokens, step):
+        at = slice(start, start + step)
+        value = own[at, :] + unpack(q1, at) + unpack(q3, at)
         logits[at, :] = value
         high = jnp.max(value, axis=1, keepdims=True)
         shifted = jnp.exp(value - high)
@@ -329,21 +327,21 @@
     return lax.rem(at[0] - s + NX, NX) * 2 + lax.rem(at[1] + k, 2)
 
 
-def product_kernel(at, mine, theirs, turned, o0, o1, o2, o3, held):
-    cap = mine.shape[0] // NX
-    for k, rows in enumerate((mine, theirs)):
-        held[k * NX * cap : (k + 1) * NX * cap, :] = jnp.dot(
-            rows[...], turned[...], preferred_element_type=f32
-        ).astype(bf16)
+def product_kernel(at, mine, theirs, turned, slopes, o0, o1, o2, o3, held):
+    half = mine.shape[0]
+    cap = half // NX
+    slopes[0:half, :] = mine[...]
+    slopes[half:, :] = theirs[...]
+    held[...] = jnp.dot(slopes[...], turned[...], preferred_element_type=f32).astype(bf16)
     for step, out in enumerate((o0, o1, o2, o3)):
         source = lax.rem(at[0] - at[5] - step + 2 * NX, NX) * cap
         for k in range(2):
-            rows = pl.ds(pl.multiple_of(source + k * NX * cap, cap), cap)
+            rows = pl.ds(pl.multiple_of(source + k * half, cap), cap)
             out[k * cap : (k + 1) * cap, :] = held[rows, :]
 
 
-def outer_kernel(at, packed_all, hid_mine, hid_theirs, mine, theirs, out, tick, held):
-    half = mine.shape[0]
+def outer_kernel(at, packed_all, hid_mine, hid_theirs, slopes, above, after, out, tick, held):
+    half = slopes.shape[0] // 2
     cap = half // NX
     tick[...] = jnp.zeros(tick.shape, f32)
     for k, hidden in enumerate((hid_mine, hid_theirs)):
@@ -353,13 +351,42 @@
             held[to : to + cap, :] = jnp.dot(
                 choose, hidden[ORDER[s] * 128 : (ORDER[s] + 1) * 128, :], preferred_element_type=f32
             ).astype(bf16)
-    slopes = jnp.concatenate([mine[...], theirs[...]], axis=0)
-    out[...] = lax.dot_general(held[...], slopes, (((0,), (0,)), ((), ())), preferred_element_type=f32)
-
-
-def spread_kernel(at, tick, r0, r1, r2, r3, packed_all, slot_all, out):
+    out[...] = lax.dot_general(
+        held[...], slopes[...], (((0,), (0,)), ((), ())), preferred_element_type=f32
+    )
+
+
+def outer(at, packed_all, hid_mine, hid_theirs, slopes, first, count, above, after):
+    (tokens, rows), (depth, cols) = hid_mine.shape, slopes.shape
+    tile = 128
+    whole_block = lambda i: (0, 0)
+    in_specs = [
+        pl.BlockSpec(memory_space=pltpu.SMEM),
+        pl.BlockSpec(packed_all.shape, whole_block),
+        pl.BlockSpec((tokens, tile), lambda i: (0, i + first)),
+        pl.BlockSpec((tokens, tile), lambda i: (0, i + first)),
+        pl.BlockSpec((depth, cols), whole_block),
+        pl.BlockSpec(memory_space=pl.ANY),
+        pl.BlockSpec(memory_space=pl.ANY),
+    ]
+    aliases = {5: 0} if above.shape == (rows, cols) else {}
+    return pl.pallas_call(
+        outer_kernel,
+        grid=(count,),
+        in_specs=in_specs,
+        out_specs=[pl.BlockSpec((tile, cols), lambda i: (i + first, 0)), pl.BlockSpec((8, 128), whole_block)],
+        out_shape=[struct((rows, cols), f32), struct((8, 128), f32)],
+        scratch_shapes=[pltpu.VMEM((depth, tile), bf16)],
+        input_output_aliases=aliases,
+        compiler_params=pltpu.CompilerParams(vmem_limit_bytes=24 << 20),
+        cost_estimate=estimate(count * tile, depth, cols),
+    )(at, packed_all, hid_mine, hid_theirs, slopes, above, after)
+
+
+def spread_kernel(at, before, r0, r1, r2, r3, packed_all, slot_all, out, tick):
     size = out.shape[0]
     cap = r0.shape[0] // 2
+    tick[...] = jnp.zeros(tick.shape, f32)
     total = jnp.zeros(out.shape, f32)
     for k in range(2):
         core = lax.rem(at[1] + k, 2)
@@ -441,8 +468,9 @@
     logits, stats = call(
         total_kernel,
         [partial, struct((lax.axis_size("z"), 8, 128), f32)],
-        [own, q1, q3],
+        [own, q1, q3, turned, hid_theirs],
         [pltpu.VMEM((tokens, 128), f32)],
+        loose=2,
     )
 
     stats = lax.all_to_all(stats, "z", 0, 0, tiled=True)
@@ -463,7 +491,7 @@
         out_specs=[pl.BlockSpec(memory_space=pltpu.VMEM)] * 4 + [pl.BlockSpec(memory_space=pltpu.SMEM)],
     )
 
-    def sparse(cap, _):
+    def backward(cap):
         piece = call(
             slopes_kernel,
             struct((cap, voc_cols), bf16),
@@ -473,40 +501,28 @@
         pieces = {s: lax.ppermute(piece, "x", ring(nx, s)) for s in (2, 1, 3)}
         mine = jnp.concatenate([piece, pieces[1], pieces[2], pieces[3]], axis=0)
         theirs = lax.ppermute(mine, "c", SWAP)
-        parts = call(
+        return call(
             product_kernel,
-            [struct((2 * cap, rows), bf16)] * nx,
+            [struct((2 * nx * cap, voc_cols), bf16)] + [struct((2 * cap, rows), bf16)] * nx,
             [at, mine, theirs, turned],
             [pltpu.VMEM((2 * nx * cap, rows), bf16)],
             smem=1,
         )
+
+    def finish(slopes, *parts):
         parts = [parts[0]] + [lax.ppermute(parts[k], "y", ring(nx, k)) for k in range(1, nx)]
-        tile = 128
-        whole_block = lambda i: (0, 0)
-        head_grad, tick = pl.pallas_call(
-            outer_kernel,
-            grid=(rows // tile,),
-            in_specs=[
-                pl.BlockSpec(memory_space=pltpu.SMEM),
-                pl.BlockSpec((n_dp, tokens), whole_block),
-                pl.BlockSpec((nx * tokens, tile), lambda i: (0, i)),
-                pl.BlockSpec((nx * tokens, tile), lambda i: (0, i)),
-                pl.BlockSpec((nx * cap, voc_cols), whole_block),
-                pl.BlockSpec((nx * cap, voc_cols), whole_block),
-            ],
-            out_specs=[pl.BlockSpec((tile, voc_cols), lambda i: (i, 0)), pl.BlockSpec((8, 128), whole_block)],
-            out_shape=[struct((rows, voc_cols), f32), tick_shape],
-            scratch_shapes=[pltpu.VMEM((2 * nx * cap, tile), bf16)],
-            compiler_params=pltpu.CompilerParams(vmem_limit_bytes=24 << 20),
-            cost_estimate=estimate(rows, 2 * nx * cap, voc_cols),
-        )(at, packed_all, hid_mine, hid_theirs, mine, theirs)
-        spread = call(
+        sides = (at, packed_all, hid_mine, hid_theirs, slopes)
+        blocks = rows // 128
+        early = (blocks + 1) // 2
+        head_grad, tick = outer(*sides, 0, early, packed_all, packed_all)
+        spread, tick = call(
             spread_kernel,
-            struct((n_voc * CAP // nx, rows), f32),
+            [struct((n_voc * CAP // nx, rows), f32), tick_shape],
             [at, tick, *parts, packed_all, slot_all],
             smem=1,
         )
         spread = lax.all_to_all(spread, "z", 0, 0, tiled=True)
+        head_grad, _ = outer(*sides, early, blocks - early, head_grad, tick)
         hidden_grad = call(
             sum_kernel,
             struct((tokens * n_dp // n_voc, rows), f32),
@@ -519,8 +535,14 @@
     def whole(_):
         return dense(hidden_states, head, token_ids, valid, advantage)
 
-    small = functools.partial(sparse, CAP_SMALL)
-    large = functools.partial(sparse, CAP * n_voc // n_dp)
+    packed_rows = backward(CAP_SMALL)
+
+    def small(_):
+        return finish(*packed_rows)
+
+    def large(_):
+        return finish(*backward(CAP * n_voc // n_dp))
+
     return lax.switch(flag[0, 0], [small, large, whole], 0)
 
 

time: 144 us -> 139 us (0.965)
  Pallas kernels: 33.8 us -> 27.5 us
  waiting for transfers between devices: 41.2 us -> 44.5 us
  blocking collectives: 30.5 us -> 27.4 us
    pallas_call x13, Pallas kernels: 27.9 us -> 20.6 us  [call(): pl.pallas_call(kernel, in_specs=specs, out_shape=out, scratch_shapes=list...]
    all_to_all x1, waiting for transfers between devices: 5.04 us -> 8.21 us  [finish(): spread = lax.all_to_all(spread, 'z', 0, 0, tiled=True)]
    all_to_all x1, blocking collectives: 15.5 us -> 12.5 us  [shards(): stats = lax.all_to_all(stats, everyone, 0, 0, tiled=True)]
    pallas_call x1 -> x2, Pallas kernels: 5.91 us -> 6.86 us  [outer(): pl.pallas_call(outer_kernel, grid=(count,), in_specs=in_specs, out_specs=...]
  transfers between devices with their start and end apart: 17 -> 17, of which waited for: 12 -> 14; matrix products, arithmetic and copies ran while one was open for 0% -> 0% of each run, Pallas kernels for 18% -> 13%
where the time goes in v5:
time: 139 us; the launch traced here: 137 us
  waiting for transfers between devices  44.5 us (32%)
  Pallas kernels  27.5 us (20%)
  blocking collectives  27.4 us (20%)
  starting transfers between devices  22.6 us (16%)
  between operations  14.8 us (11%)
    pallas_call x13, Pallas kernels, call(): pl.pallas_call(kernel, in_specs=specs, out_shape=out, scratch_shapes=list...  20.6 us
    all_to_all x1, blocking collectives, shards(): stats = lax.all_to_all(stats, 'z', 0, 0, tiled=True)  14.9 us
    all_to_all x1, blocking collectives, shards(): stats = lax.all_to_all(stats, everyone, 0, 0, tiled=True)  12.5 us
    ppermute x1, waiting for transfers between devices, shards(): lax.ppermute(q1, 'x', ring(nx, -1))  12.2 us
    ppermute x3, waiting for transfers between devices, backward(): pieces = {s: lax.ppermute(piece, 'x', ring(nx, s)) for s in (2, 1, 3)}  9.02 us
    all_to_all x1, waiting for transfers between devices, finish(): spread = lax.all_to_all(spread, 'z', 0, 0, tiled=True)  8.21 us
    pallas_call x2, Pallas kernels, outer(): pl.pallas_call(outer_kernel, grid=(count,), in_specs=in_specs, out_specs=...  6.86 us
    ppermute x3, starting transfers between devices, shards(): came = {s: lax.ppermute(leave[s - 1], 'x', ring(nx, s)) for s in (2, 1, 3)}  6.35 us
  transfers between devices with their start and end apart: 17, of which 14 were waited for; matrix products, arithmetic and copies ran while one was open for 0% of the time, Pallas kernels for 13%

profile of v5, /device:TPU:32, one launch (start us, length us, event | category | flops | bytes accessed | tf_op | source)
XLA Modules:
  0.0 137.0 jit_solution(8033370311965696943)
XLA Ops:
  8.8 3.1 %collective-permute-start.11 = (bf16[128,1280]{1,0:T(8,128)(2,1)S(1)}, bf16[128,1280]{1,0:T(8,128)(2,1)S(1)}, u32[]{:S(2)}, u32[]{:S(2)}) collective-permute-start(bf16[128,1280]{1,0:T(8,128)(2,1)S(1)} %get-tuple-element.154), channel_id=1, source_target_pairs={{0,128},{64,192},{128,0},{192,64},{1,129},{65,193},{129,1},{193,65... | collective-permute-start | bytes 983048 | tf_op jit(solution)/shard_map/ppermute | solution.py:435
  12.5 2.6 %collective-permute-start.13 = (bf16[128,1280]{1,0:T(8,128)(2,1)S(1)}, bf16[128,1280]{1,0:T(8,128)(2,1)S(1)}, u32[]{:S(2)}, u32[]{:S(2)}) collective-permute-start(bf16[128,1280]{1,0:T(8,128)(2,1)S(1)} %get-tuple-element.158), channel_id=1, source_target_pairs={{0,192},{64,0},{128,64},{192,128},{1,193},{65,1},{129,65},{193,129... | collective-permute-start | bytes 983048 | tf_op jit(solution)/shard_map/ppermute | solution.py:435
  15.1 3.3 %shard_map.72 = (f32[128,2432]{1,0:T(8,128)S(1)}, bf16[640,2432]{1,0:T(8,128)(2,1)S(1)}) custom-call(s32[6]{0:T(128)S(1)} %stack.27.at, bf16[128,1280]{1,0:T(8,128)(2,1)S(1)} %get-tuple-element.152.block.b0, bf16[640,2432]{1,0:T(8,128)(2,1)} %head.1, bf16[640,2432]{1,0:T(8,128)(2,1)S(1)} %collective-permute-done.10.other), custom_call_target="tpu_custom_call" | custom-call | flops 796917760 | bytes 6225920 | tf_op jit(solution)/shard_map/pallas_call | solution.py:97
  18.4 2.5 %collective-permute-done.11.block.b2 = bf16[128,1280]{1,0:T(8,128)(2,1)S(1)} collective-permute-done((bf16[128,1280]{1,0:T(8,128)(2,1)S(1)}, bf16[128,1280]{1,0:T(8,128)(2,1)S(1)}, u32[]{:S(2)}, u32[]{:S(2)}) %collective-permute-start.11) | collective-permute-done | bytes 327712 | tf_op jit(solution)/shard_map/ppermute | solution.py:435
  20.9 2.3 %shard_map.73 = (s16[64,2560]{1,0:T(8,128)(2,1)S(1)}, s16[64,2560]{1,0:T(8,128)(2,1)S(1)}, f32[8,128]{1,0:T(8,128)S(1)}) custom-call(s32[6]{0:T(128)S(1)} %stack.27.at, bf16[128,1280]{1,0:T(8,128)(2,1)S(1)} %collective-permute-done.11.block.b2, bf16[640,2432]{1,0:T(8,128)(2,1)S(1)} %get-tuple-element.155.head, ...), custom_call_target="tpu_custom_call" | custom-call | flops 796917760 | bytes 6225920 | tf_op jit(solution)/shard_map/pallas_call | solution.py:97
  23.2 2.8 %collective-permute-start.14 = (s16[64,2560]{1,0:T(8,128)(2,1)S(1)}, s16[64,2560]{1,0:T(8,128)(2,1)S(1)}, u32[]{:S(2)}, u32[]{:S(2)}) collective-permute-start(s16[64,2560]{1,0:T(8,128)(2,1)S(1)} %get-tuple-element.161), channel_id=1, source_target_pairs={{0,192},{64,0},{128,64},{192,128},{1,193},{65,1},{129,65},{193,129... | collective-permute-start | bytes 983048 | tf_op jit(solution)/shard_map/ppermute | solution.py:454
  28.0 2.7 %shard_map.74 = (f32[128,2432]{1,0:T(8,128)S(1)}, f32[128,2432]{1,0:T(8,128)S(1)}, bf16[512,640]{1,0:T(8,128)(2,1)S(1)}, bf16[512,640]{1,0:T(8,128)(2,1)S(1)}) custom-call(s32[6]{0:T(128)S(1)} %stack.27.at, f32[8,128]{1,0:T(8,128)S(1)} %get-tuple-element.156.tick, bf16[128,1280]{1,0:T(8,128)(2,1)S(1)} %get-tuple-element.152.block.b0, ...), custom_call_target="tpu_custom_call" | custom-call | flops 1593835520 | bytes 6225920 | tf_op jit(solution)/shard_map/pallas_call | solution.py:97
  30.9 3.8 %collective-permute-done.14.low = s16[64,2560]{1,0:T(8,128)(2,1)S(1)} collective-permute-done((s16[64,2560]{1,0:T(8,128)(2,1)S(1)}, s16[64,2560]{1,0:T(8,128)(2,1)S(1)}, u32[]{:S(2)}, u32[]{:S(2)}) %collective-permute-start.14) | collective-permute-done | bytes 327712 | tf_op jit(solution)/shard_map/ppermute | solution.py:454
  39.6 12.2 %collective-permute-done.16.q1 = s16[128,2560]{1,0:T(8,128)(2,1)S(1)} collective-permute-done((s16[128,2560]{1,0:T(8,128)(2,1)S(1)}, s16[128,2560]{1,0:T(8,128)(2,1)S(1)}, u32[]{:S(2)}, u32[]{:S(2)}) %collective-permute-start.16) | collective-permute-done | bytes 655392 | tf_op jit(solution)/shard_map/ppermute | solution.py:465
  51.8 3.4 %collective-permute-done.17.q3 = s16[128,2560]{1,0:T(8,128)(2,1)S(1)} collective-permute-done((s16[128,2560]{1,0:T(8,128)(2,1)S(1)}, s16[128,2560]{1,0:T(8,128)(2,1)S(1)}, u32[]{:S(2)}, u32[]{:S(2)}) %collective-permute-start.17) | collective-permute-done | bytes 655392 | tf_op jit(solution)/shard_map/ppermute | solution.py:465
  56.0 14.9 %all_to_all.42.parts = f32[8,8,128]{2,1,0:T(8,128)S(1)} all-to-all(f32[8,8,128]{2,1,0:T(8,128)S(1)} %get-tuple-element.167), channel_id=1, replica_groups=mesh['x'=4,'c'=2,'y'=4,'z'=8] {'z'}, dimensions={0} | all-to-all | bytes 65536 | tf_op jit(solution)/shard_map/all_to_all | solution.py:476
  71.0 12.5 %all_to_all.43.parts = f32[32,8,128]{2,1,0:T(8,128)S(1)} all-to-all(f32[32,8,128]{2,1,0:T(8,128)S(1)} %shard_map.78), channel_id=1, replica_groups=mesh['x'=4,'c'=2,'y'=4,'z'=8] {'x','c','y'}, dimensions={0} | all-to-all | bytes 262144 | tf_op jit(solution)/shard_map/all_to_all | solution.py:483
  83.5 2.1 %shard_map.79 = (f32[8,128]{1,0:T(8,128)S(1)}, f32[8,128]{1,0:T(8,128)S(1)}, f32[8,128]{1,0:T(8,128)S(1)}, f32[8,128]{1,0:T(8,128)S(1)}, s32[1,1]{1,0:T(1,128)}) custom-call(f32[32,8,128]{2,1,0:T(8,128)S(1)} %all_to_all.43.parts), custom_call_target="tpu_custom_call" | custom-call | tf_op jit(solution)/shard_map/pallas_call | solution.py:97
  89.5 4.2 %collective-permute-done.21 = bf16[32,2432]{1,0:T(8,128)(2,1)S(1)} collective-permute-done((bf16[32,2432]{1,0:T(8,128)(2,1)S(1)}, bf16[32,2432]{1,0:T(8,128)(2,1)S(1)}, u32[]{:S(2)}, u32[]{:S(2)}) %collective-permute-start.21) | collective-permute-done | bytes 155680 | tf_op jit(solution)/shard_map/ppermute | solution.py:501
  93.7 2.6 %collective-permute-done.20 = bf16[32,2432]{1,0:T(8,128)(2,1)S(1)} collective-permute-done((bf16[32,2432]{1,0:T(8,128)(2,1)S(1)}, bf16[32,2432]{1,0:T(8,128)(2,1)S(1)}, u32[]{:S(2)}, u32[]{:S(2)}) %collective-permute-start.20) | collective-permute-done | bytes 155680 | tf_op jit(solution)/shard_map/ppermute | solution.py:501
  96.3 2.2 %collective-permute-done.19 = bf16[32,2432]{1,0:T(8,128)(2,1)S(1)} collective-permute-done((bf16[32,2432]{1,0:T(8,128)(2,1)S(1)}, bf16[32,2432]{1,0:T(8,128)(2,1)S(1)}, u32[]{:S(2)}, u32[]{:S(2)}) %collective-permute-start.19) | collective-permute-done | bytes 155680 | tf_op jit(solution)/shard_map/ppermute | solution.py:501
  100.7 1.7 %shard_map.81 = (bf16[256,2432]{1,0:T(8,128)(2,1)S(1)}, bf16[64,640]{1,0:T(8,128)(2,1)S(1)}, bf16[64,640]{1,0:T(8,128)(2,1)S(1)}, bf16[64,640]{1,0:T(8,128)(2,1)S(1)}, bf16[64,640]{1,0:T(8,128)(2,1)S(1)}) custom-call(s32[6]{0:T(128)S(1)} %stack.27.at, bf16[128,2432]{1,0:T(8,128)(2,1)S(1)} %pad_maximum_fusion.1.mine, ...), custom_call_target="tpu_custom_call" | custom-call | tf_op jit(solution)/shard_map/pallas_call | solution.py:97
  102.4 27.8 %conditional.1 = (f32[32,640]{1,0:T(8,128)}, f32[640,2432]{1,0:T(8,128)}) conditional(s32[]{:T(128)} %bitcast.17, (s32[6]{0:T(128)S(1)}, f32[8,128]{1,0:T(8,128)S(1)}, bf16[512,640]{1,0:T(8,128)(2,1)S(1)}, bf16[512,640]{1,0:T(8,128)(2,1)S(1)}, bf16[256,2432]{1,0:T(8,128)(2,1)S(1)}, /*index=5*/bf16[64,640]{1,0:T(8,128)(2,1)S(1)}, ...), branch_computations={%region_0.0_spmd, %region_1.0_spmd, %region_2.17_spmd} | conditional | flops 9566442496 | bytes 125846592 | solution.py:546
  103.0 1.9 %collective-permute-start.1 = (bf16[64,640]{1,0:T(8,128)(2,1)S(1)}, bf16[64,640]{1,0:T(8,128)(2,1)S(1)}, u32[]{:S(2)}, u32[]{:S(2)}) collective-permute-start(bf16[64,640]{1,0:T(8,128)(2,1)S(1)} %get-tuple-element.82), channel_id=1, source_target_pairs={{0,16},{8,24},{16,0},{24,8},{1,17},{9,25},{17,1},{25,9},{2,18},{10... | collective-permute-start | bytes 245768 | tf_op jit(solution)/shard_map/cond/branch_0_fun/ppermute | solution.py:513
  106.0 3.8 %branch_0_fun.4 = (f32[640,2432]{1,0:T(8,128)}, f32[8,128]{1,0:T(8,128)S(1)}) custom-call(s32[6]{0:T(128)S(1)} %get-tuple-element.74.at, f32[8,128]{1,0:T(8,128)S(1)} %get-tuple-element.75.packed_all.above.after, bf16[512,640]{1,0:T(8,128)(2,1)S(1)} %get-tuple-element.76.hid_mine, bf16[512,640]{1,0:T(8,128)(2,1)S(1)} %get-tuple-element.77.hid_theirs, ...), custom_call_target="tpu_custom_call" | custom-call | flops 478150656 | bytes 1245184 | tf_op jit(solution)/shard_map/cond/branch_0_fun/pallas_call | solution.py:373
  110.5 2.1 %branch_0_fun.5 = (f32[128,640]{1,0:T(8,128)}, f32[8,128]{1,0:T(8,128)S(1)}) custom-call(s32[6]{0:T(128)S(1)} %get-tuple-element.74.at, f32[8,128]{1,0:T(8,128)S(1)} %get-tuple-element.79.before, bf16[64,640]{1,0:T(8,128)(2,1)S(1)} %get-tuple-element.80.r0, bf16[64,640]{1,0:T(8,128)(2,1)S(1)} %collective-permute-done.r1, ...), custom_call_target="tpu_custom_call" | custom-call | tf_op jit(solution)/shard_map/cond/branch_0_fun/pallas_call | solution.py:97
  112.6 4.8 %all-to-all-start = ((f32[8,16,640]{2,1,0:T(8,128)}), f32[8,16,640]{2,1,0:T(8,128)S(1)}, u32[]{:S(2)}, u32[]{:S(2)}) async-start(f32[8,16,640]{2,1,0:T(8,128)} %bitcast), calls=%async_computation | async-start | bytes 655360 | tf_op jit(solution)/shard_map/cond/branch_0_fun/all_to_all | solution.py:524
  117.4 3.1 %branch_0_fun.7 = (f32[640,2432]{1,0:T(8,128)}, f32[8,128]{1,0:T(8,128)}) custom-call(s32[6]{0:T(128)S(1)} %get-tuple-element.74.at, f32[8,128]{1,0:T(8,128)S(1)} %get-tuple-element.75.packed_all.above.after, bf16[512,640]{1,0:T(8,128)(2,1)} %copy-done.2, bf16[512,640]{1,0:T(8,128)(2,1)S(1)} %get-tuple-element.77.hid_theirs, ...), custom_call_target="tpu_custom_call", output_to_operand_aliasing={{0}: (5, {})} | custom-call | flops 318767104 | bytes 1245184 | tf_op jit(solution)/shard_map/cond/branch_0_fun/pallas_call | solution.py:373
  120.5 8.2 %all-to-all-done = f32[8,16,640]{2,1,0:T(8,128)S(1)} async-done(((f32[8,16,640]{2,1,0:T(8,128)}), f32[8,16,640]{2,1,0:T(8,128)S(1)}, u32[]{:S(2)}, u32[]{:S(2)}) %all-to-all-start) | async-done | bytes 327712 | tf_op jit(solution)/shard_map/cond/branch_0_fun/all_to_all | solution.py:524
  (38 shorter events, 19.4 us)
Async XLA Ops:
  7.2 8.0 %collective-permute-start.10 = (bf16[640,2432]{1,0:T(8,128)(2,1)}, bf16[640,2432]{1,0:T(8,128)(2,1)S(1)}, u32[]{:S(2)}, u32[]{:S(2)}) collective-permute-start(bf16[640,2432]{1,0:T(8,128)(2,1)} %head.1), channel_id=1, source_target_pairs={{0,32},{32,0},{1,33},{33,1},{2,34},{34,2},{3,35},{35,3},{4,36},{36... | collective-permute-start | bytes 9338888 | tf_op jit(solution)/shard_map/ppermute | solution.py:431
  8.8 12.1 %collective-permute-start.11 = (bf16[128,1280]{1,0:T(8,128)(2,1)S(1)}, bf16[128,1280]{1,0:T(8,128)(2,1)S(1)}, u32[]{:S(2)}, u32[]{:S(2)}) collective-permute-start(bf16[128,1280]{1,0:T(8,128)(2,1)S(1)} %get-tuple-element.154), channel_id=1, source_target_pairs={{0,128},{64,192},{128,0},{192,64},{1,129},{65,193},{129,1},{193,65... | collective-permute-start | bytes 983048 | tf_op jit(solution)/shard_map/ppermute | solution.py:435
  11.9 15.6 %collective-permute-start.12 = (bf16[128,1280]{1,0:T(8,128)(2,1)S(1)}, bf16[128,1280]{1,0:T(8,128)(2,1)S(1)}, u32[]{:S(2)}, u32[]{:S(2)}) collective-permute-start(bf16[128,1280]{1,0:T(8,128)(2,1)S(1)} %get-tuple-element.157), channel_id=1, source_target_pairs={{0,64},{64,128},{128,192},{192,0},{1,65},{65,129},{129,193},{193,1... | collective-permute-start | bytes 983048 | tf_op jit(solution)/shard_map/ppermute | solution.py:435
  12.5 15.5 %collective-permute-start.13 = (bf16[128,1280]{1,0:T(8,128)(2,1)S(1)}, bf16[128,1280]{1,0:T(8,128)(2,1)S(1)}, u32[]{:S(2)}, u32[]{:S(2)}) collective-permute-start(bf16[128,1280]{1,0:T(8,128)(2,1)S(1)} %get-tuple-element.158), channel_id=1, source_target_pairs={{0,192},{64,0},{128,64},{192,128},{1,193},{65,1},{129,65},{193,129... | collective-permute-start | bytes 983048 | tf_op jit(solution)/shard_map/ppermute | solution.py:435
  23.2 11.5 %collective-permute-start.14 = (s16[64,2560]{1,0:T(8,128)(2,1)S(1)}, s16[64,2560]{1,0:T(8,128)(2,1)S(1)}, u32[]{:S(2)}, u32[]{:S(2)}) collective-permute-start(s16[64,2560]{1,0:T(8,128)(2,1)S(1)} %get-tuple-element.161), channel_id=1, source_target_pairs={{0,192},{64,0},{128,64},{192,128},{1,193},{65,1},{129,65},{193,129... | collective-permute-start | bytes 983048 | tf_op jit(solution)/shard_map/ppermute | solution.py:454
  26.0 9.8 %collective-permute-start.15 = (s16[64,2560]{1,0:T(8,128)(2,1)S(1)}, s16[64,2560]{1,0:T(8,128)(2,1)S(1)}, u32[]{:S(2)}, u32[]{:S(2)}) collective-permute-start(s16[64,2560]{1,0:T(8,128)(2,1)S(1)} %get-tuple-element.162), channel_id=1, source_target_pairs={{0,64},{64,128},{128,192},{192,0},{1,65},{65,129},{129,193},{193,1... | collective-permute-start | bytes 983048 | tf_op jit(solution)/shard_map/ppermute | solution.py:454
  30.8 8.8 %collective-permute-start.18 = (bf16[512,640]{1,0:T(8,128)(2,1)S(1)}, bf16[512,640]{1,0:T(8,128)(2,1)S(1)}, u32[]{:S(2)}, u32[]{:S(2)}) collective-permute-start(bf16[512,640]{1,0:T(8,128)(2,1)S(1)} %get-tuple-element.166), channel_id=1, source_target_pairs={{0,32},{32,0},{1,33},{33,1},{2,34},{34,2},{3,35},{35,3},{4,36},{36... | collective-permute-start | bytes 1966088 | tf_op jit(solution)/shard_map/ppermute | solution.py:467
  36.6 15.2 %collective-permute-start.16 = (s16[128,2560]{1,0:T(8,128)(2,1)S(1)}, s16[128,2560]{1,0:T(8,128)(2,1)S(1)}, u32[]{:S(2)}, u32[]{:S(2)}) collective-permute-start(s16[128,2560]{1,0:T(8,128)(2,1)S(1)} %get-tuple-element.163), channel_id=1, source_target_pairs={{0,192},{64,0},{128,64},{192,128},{1,193},{65,1},{129,65},{193,129... | collective-permute-start | bytes 1966088 | tf_op jit(solution)/shard_map/ppermute | solution.py:465
  38.1 17.1 %collective-permute-start.17 = (s16[128,2560]{1,0:T(8,128)(2,1)S(1)}, s16[128,2560]{1,0:T(8,128)(2,1)S(1)}, u32[]{:S(2)}, u32[]{:S(2)}) collective-permute-start(s16[128,2560]{1,0:T(8,128)(2,1)S(1)} %get-tuple-element.164), channel_id=1, source_target_pairs={{0,64},{64,128},{128,192},{192,0},{1,65},{65,129},{129,193},{193,1... | collective-permute-start | bytes 1966088 | tf_op jit(solution)/shard_map/ppermute | solution.py:465
  55.1 15.8 %copy-start.5 = (s32[128]{0:T(128)S(1)}, s32[128]{0:T(128)}, u32[]{:S(2)}) copy-start(s32[128]{0:T(128)} %param.13) | copy-start | bytes 1540
  55.1 15.8 %copy-start.6 = (f32[128]{0:T(128)S(1)}, f32[128]{0:T(128)}, u32[]{:S(2)}) copy-start(f32[128]{0:T(128)} %param.14) | copy-start | bytes 1540
  55.1 30.4 %copy-start.4 = (s32[128]{0:T(128)S(1)}, s32[128]{0:T(128)}, u32[]{:S(2)}) copy-start(s32[128]{0:T(128)} %param.12) | copy-start | bytes 1540
  86.7 6.9 %collective-permute-start.21 = (bf16[32,2432]{1,0:T(8,128)(2,1)S(1)}, bf16[32,2432]{1,0:T(8,128)(2,1)S(1)}, u32[]{:S(2)}, u32[]{:S(2)}) collective-permute-start(bf16[32,2432]{1,0:T(8,128)(2,1)S(1)} %shard_map.80), channel_id=1, source_target_pairs={{0,192},{64,0},{128,64},{192,128},{1,193},{65,1},{129,65},{193,129... | collective-permute-start | bytes 466952 | tf_op jit(solution)/shard_map/ppermute | solution.py:501
  87.9 8.4 %collective-permute-start.20 = (bf16[32,2432]{1,0:T(8,128)(2,1)S(1)}, bf16[32,2432]{1,0:T(8,128)(2,1)S(1)}, u32[]{:S(2)}, u32[]{:S(2)}) collective-permute-start(bf16[32,2432]{1,0:T(8,128)(2,1)S(1)} %shard_map.80), channel_id=1, source_target_pairs={{0,128},{64,192},{128,0},{192,64},{1,129},{65,193},{129,1},{193,65... | collective-permute-start | bytes 466952 | tf_op jit(solution)/shard_map/ppermute | solution.py:501
  89.4 9.1 %collective-permute-start.19 = (bf16[32,2432]{1,0:T(8,128)(2,1)S(1)}, bf16[32,2432]{1,0:T(8,128)(2,1)S(1)}, u32[]{:S(2)}, u32[]{:S(2)}) collective-permute-start(bf16[32,2432]{1,0:T(8,128)(2,1)S(1)} %shard_map.80), channel_id=1, source_target_pairs={{0,64},{64,128},{128,192},{192,0},{1,65},{65,129},{129,193},{193,1... | collective-permute-start | bytes 466952 | tf_op jit(solution)/shard_map/ppermute | solution.py:501
  98.5 2.1 %collective-permute-start.22 = (bf16[128,2432]{1,0:T(8,128)(2,1)S(1)}, bf16[128,2432]{1,0:T(8,128)(2,1)S(1)}, u32[]{:S(2)}, u32[]{:S(2)}) collective-permute-start(bf16[128,2432]{1,0:T(8,128)(2,1)S(1)} %pad_maximum_fusion.1.mine), channel_id=1, source_target_pairs={{0,32},{32,0},{1,33},{33,1},{2,34},{34,2},{3,35},{35,3},{4,36},{36... | collective-permute-start | bytes 1867784 | tf_op jit(solution)/shard_map/ppermute | solution.py:503
  102.4 10.2 %copy-start.2 = (bf16[512,640]{1,0:T(8,128)(2,1)}, bf16[512,640]{1,0:T(8,128)(2,1)S(1)}, u32[]{:S(2)}) copy-start(bf16[512,640]{1,0:T(8,128)(2,1)S(1)} %get-tuple-element.76.hid_mine) | copy-start | bytes 1966084 | tf_op jit(solution)/shard_map/cond
  102.4 7.5 %collective-permute-start = (bf16[64,640]{1,0:T(8,128)(2,1)S(1)}, bf16[64,640]{1,0:T(8,128)(2,1)S(1)}, u32[]{:S(2)}, u32[]{:S(2)}) collective-permute-start(bf16[64,640]{1,0:T(8,128)(2,1)S(1)} %get-tuple-element.81), channel_id=1, source_target_pairs={{0,8},{8,16},{16,24},{24,0},{1,9},{9,17},{17,25},{25,1},{2,10},{10... | collective-permute-start | bytes 245768 | tf_op jit(solution)/shard_map/cond/branch_0_fun/ppermute | solution.py:513
  103.0 6.9 %collective-permute-start.1 = (bf16[64,640]{1,0:T(8,128)(2,1)S(1)}, bf16[64,640]{1,0:T(8,128)(2,1)S(1)}, u32[]{:S(2)}, u32[]{:S(2)}) collective-permute-start(bf16[64,640]{1,0:T(8,128)(2,1)S(1)} %get-tuple-element.82), channel_id=1, source_target_pairs={{0,16},{8,24},{16,0},{24,8},{1,17},{9,25},{17,1},{25,9},{2,18},{10... | collective-permute-start | bytes 245768 | tf_op jit(solution)/shard_map/cond/branch_0_fun/ppermute | solution.py:513
  104.9 5.6 %collective-permute-start.2 = (bf16[64,640]{1,0:T(8,128)(2,1)S(1)}, bf16[64,640]{1,0:T(8,128)(2,1)S(1)}, u32[]{:S(2)}, u32[]{:S(2)}) collective-permute-start(bf16[64,640]{1,0:T(8,128)(2,1)S(1)} %get-tuple-element.83), channel_id=1, source_target_pairs={{0,24},{8,0},{16,8},{24,16},{1,25},{9,1},{17,9},{25,17},{2,26},{10... | collective-permute-start | bytes 245768 | tf_op jit(solution)/shard_map/cond/branch_0_fun/ppermute | solution.py:513
  112.6 16.1 %all-to-all-start = ((f32[8,16,640]{2,1,0:T(8,128)}), f32[8,16,640]{2,1,0:T(8,128)S(1)}, u32[]{:S(2)}, u32[]{:S(2)}) async-start(f32[8,16,640]{2,1,0:T(8,128)} %bitcast), calls=%async_computation | async-start | bytes 655360 | tf_op jit(solution)/shard_map/cond/branch_0_fun/all_to_all | solution.py:524

commit v6 on v5

--- a/solution.py
+++ b/solution.py
@@ -139,6 +139,12 @@
     out[to, cols : cols + 128] = wide_power.astype(jnp.int16)
 
 
+def pack_rows(part, start, out):
+    step = 16
+    for row in range(0, out.shape[0], step):
+        pack(part[start + row : start + row + step, :], out, slice(row, row + step))
+
+
 def unpack(ref, at):
     cols = ref.shape[1] - 128
     power = ref[at, cols : cols + 128].astype(jnp.int32).astype(f32)[:, :1]
@@ -181,17 +187,14 @@
 
     over_columns(cols, tile)
     tick[...] = jnp.zeros(tick.shape, f32)
-    step = 32
-    for k, out in enumerate((low, high)):
-
-        @pl.loop(0, tokens // 2 // step)
-        def _(i, k=k, out=out):
-            source = pl.multiple_of(k * (tokens // 2) + i * step, step)
-            pack(part[pl.ds(source, step), :], out, pl.ds(pl.multiple_of(i * step, step), step))
-
-
-def near_kernel(at, tick, b0, b1, b2, b3, head, other, p1, p3, mine, theirs):
+    half = tokens // 2
+    pack_rows(part, 0, low)
+    pack_rows(part, half, high)
+
+
+def near_kernel(at, tick, b0, b1, b2, b3, head, other, p1, p3, q1, q3, mine, theirs, part):
     tokens = b0.shape[0]
+    half = tokens // 2
     rows, cols = head.shape
     here, there = halves(at, rows)
     for k, block in enumerate((b1, b3, b0, b2)):
@@ -199,37 +202,36 @@
         theirs[k * tokens : (k + 1) * tokens, :] = block[:, there]
 
     def tile(span):
-        part = jnp.dot(mine[0 : 2 * tokens, :], head[:, span], preferred_element_type=f32) + jnp.dot(
+        both = jnp.dot(mine[0 : 2 * tokens, :], head[:, span], preferred_element_type=f32) + jnp.dot(
             theirs[0 : 2 * tokens, :], other[:, span], preferred_element_type=f32
         )
-        p1[:, span] = part[0:tokens, :]
-        p3[:, span] = part[tokens:, :]
+        p1[:, span] = both[0:half, :]
+        part[:, span] = both[half : tokens + half, :]
+        p3[:, span] = both[tokens + half :, :]
 
     over_columns(cols, tile)
+    pack_rows(part, 0, q1)
+    pack_rows(part, half, q3)
 
 
 def relay_kernel(p1, p3, low, high, q1, q3, tick):
-    tokens = p1.shape[0]
-    half, step = tokens // 2, 32
+    step = 16
     tick[...] = jnp.zeros(tick.shape, f32)
-
-    @pl.loop(0, half // step)
-    def _(i):
-        near = pl.ds(pl.multiple_of(i * step, step), step)
-        far = pl.ds(pl.multiple_of(half + i * step, step), step)
-        pack(p1[near, :] + unpack(low, near), q1, near)
-        pack(p1[far, :], q1, far)
-        pack(p3[near, :], q3, near)
-        pack(p3[far, :] + unpack(high, near), q3, far)
-
-
-def total_kernel(own, q1, q3, turned, theirs, logits, sent, stats):
+    for start in range(0, p1.shape[0], step):
+        at = slice(start, start + step)
+        pack(p1[at, :] + unpack(low, at), q1, at)
+        pack(p3[at, :] + unpack(high, at), q3, at)
+
+
+def total_kernel(own, q1_low, q1_high, q3_low, q3_high, turned, theirs, logits, sent, stats):
     tokens = own.shape[0]
     step = 16
     lane = lax.broadcasted_iota(jnp.int32, (step, 128), 1)
     for start in range(0, tokens, step):
         at = slice(start, start + step)
-        value = own[at, :] + unpack(q1, at) + unpack(q3, at)
+        q1, q3 = (q1_low, q3_low) if start < tokens // 2 else (q1_high, q3_high)
+        part = slice(start % (tokens // 2), start % (tokens // 2) + step)
+        value = own[at, :] + unpack(q1, part) + unpack(q3, part)
         logits[at, :] = value
         high = jnp.max(value, axis=1, keepdims=True)
         shifted = jnp.exp(value - high)
@@ -387,20 +389,23 @@
     size = out.shape[0]
     cap = r0.shape[0] // 2
     tick[...] = jnp.zeros(tick.shape, f32)
-    total = jnp.zeros(out.shape, f32)
+    spread = []
     for k in range(2):
         core = lax.rem(at[1] + k, 2)
         me = pl.ds(at[5] * 2 + core, 1)
         slot = slot_all[me, :]
         slot = jnp.where(slot >= 0.0, slot + (core * (size // 2)).astype(f32), -1.0)
-        spread = lax.dot_general(
+        part = lax.dot_general(
             one_hot(size, slot),
             one_hot(cap, packed_all[me, :]),
             (((1,), (1,)), ((), ())),
             preferred_element_type=f32,
-        ).astype(bf16)
-        for r in (r0, r1, r2, r3):
-            total = total + jnp.dot(spread, r[k * cap : (k + 1) * cap, :], preferred_element_type=f32)
+        )
+        spread.append(part.astype(bf16))
+    spread = jnp.concatenate(spread, axis=1)
+    total = jnp.zeros(out.shape, f32)
+    for r in (r0, r1, r2, r3):
+        total = total + jnp.dot(spread, r[...], preferred_element_type=f32)
     out[...] = total
 
 
@@ -452,23 +457,25 @@
         cost_estimate=estimate(tokens, chip_rows, voc_cols),
     )
     low, high = lax.ppermute(low, "x", ring(nx, -1)), lax.ppermute(high, "x", ring(nx, 1))
-    p1, p3, hid_mine, hid_send = call(
+    half_partial = struct((tokens // 2, voc_cols), f32)
+    p1, p3, q1_high, q3_low, hid_mine, hid_send = call(
         near_kernel,
-        [partial] * 2 + [struct((nx * tokens, rows), bf16)] * 2,
+        [half_partial] * 2 + [half] * 2 + [struct((nx * tokens, rows), bf16)] * 2,
         [at, tick, b0, came[1], came[2], came[3], kept, head_other],
+        [pltpu.VMEM((tokens, voc_cols), f32)],
         vmem=24,
         smem=1,
         cost_estimate=estimate(2 * tokens, chip_rows, voc_cols),
     )
-    packed = struct((tokens, voc_cols + 128), jnp.int16)
-    q1, q3, tick = call(relay_kernel, [packed] * 2 + [tick_shape], [p1, p3, low, high])
-    q1, q3 = lax.ppermute(q1, "x", ring(nx, -1)), lax.ppermute(q3, "x", ring(nx, 1))
+    q1_high, q3_low = lax.ppermute(q1_high, "x", ring(nx, -1)), lax.ppermute(q3_low, "x", ring(nx, 1))
+    q1_low, q3_high, tick = call(relay_kernel, [half] * 2 + [tick_shape], [p1, p3, low, high])
+    q1_low, q3_high = lax.ppermute(q1_low, "x", ring(nx, -1)), lax.ppermute(q3_high, "x", ring(nx, 1))
     turned = call(turn_kernel, struct((voc_cols, rows), bf16), [tick, kept])
     hid_theirs = lax.ppermute(hid_send, "c", SWAP)
     logits, stats = call(
         total_kernel,
         [partial, struct((lax.axis_size("z"), 8, 128), f32)],
-        [own, q1, q3, turned, hid_theirs],
+        [own, q1_low, q1_high, q3_low, q3_high, turned, hid_theirs],
         [pltpu.VMEM((tokens, 128), f32)],
         loose=2,
     )

time: 139 us -> 135 us (0.971)
  waiting for transfers between devices: 44.5 us -> 38.7 us
  starting transfers between devices: 22.6 us -> 25.2 us
    ppermute x2 -> x4, waiting for transfers between devices: 15.6 us -> 12.4 us  [the longest x1 3.45 us: shards(): lax.ppermute(q1_low, 'x', ring(nx, -1))]
    ppermute x2 -> x4, starting transfers between devices: 2.1 us -> 4.68 us  [the longest x1 2.39 us: shards(): lax.ppermute(q1_high, 'x', ring(nx, -1))]
    ppermute x1, waiting for transfers between devices: 3.77 us -> 1.57 us  [shards(): lax.ppermute(low, 'x', ring(nx, -1))]
  transfers between devices with their start and end apart: 17 -> 19, of which waited for: 14 -> 16; matrix products, arithmetic and copies ran while one was open for 0% -> 0% of each run, Pallas kernels for 13% -> 13%
where the time goes in v6:
time: 135 us; the launch traced here: 133 us
  waiting for transfers between devices  38.7 us (29%)
  blocking collectives  27.4 us (20%)
  Pallas kernels  26.7 us (20%)
  starting transfers between devices  25.2 us (19%)
  between operations  14.8 us (11%)
    pallas_call x13, Pallas kernels, call(): pl.pallas_call(kernel, in_specs=specs, out_shape=out, scratch_shapes=list...  19.9 us
    all_to_all x1, blocking collectives, shards(): stats = lax.all_to_all(stats, 'z', 0, 0, tiled=True)  14.9 us
    all_to_all x1, blocking collectives, shards(): stats = lax.all_to_all(stats, everyone, 0, 0, tiled=True)  12.5 us
    ppermute x3, waiting for transfers between devices, backward(): pieces = {s: lax.ppermute(piece, 'x', ring(nx, s)) for s in (2, 1, 3)}  9.02 us
    all_to_all x1, waiting for transfers between devices, finish(): spread = lax.all_to_all(spread, 'z', 0, 0, tiled=True)  8.19 us
    pallas_call x2, Pallas kernels, outer(): pl.pallas_call(outer_kernel, grid=(count,), in_specs=in_specs, out_specs=...  6.87 us
    ppermute x3, starting transfers between devices, shards(): came = {s: lax.ppermute(leave[s - 1], 'x', ring(nx, s)) for s in (2, 1, 3)}  6.35 us
    ppermute x3, waiting for transfers between devices, shards(): came = {s: lax.ppermute(leave[s - 1], 'x', ring(nx, s)) for s in (2, 1, 3)}  4.83 us
  transfers between devices with their start and end apart: 19, of which 16 were waited for; matrix products, arithmetic and copies ran while one was open for 0% of the time, Pallas kernels for 13%

profile of v6, /device:TPU:32, one launch (start us, length us, event | category | flops | bytes accessed | tf_op | source)
XLA Modules:
  0.0 133.1 jit_solution(1927348826176648847)
XLA Ops:
  8.8 3.1 %collective-permute-start.11 = (bf16[128,1280]{1,0:T(8,128)(2,1)S(1)}, bf16[128,1280]{1,0:T(8,128)(2,1)S(1)}, u32[]{:S(2)}, u32[]{:S(2)}) collective-permute-start(bf16[128,1280]{1,0:T(8,128)(2,1)S(1)} %get-tuple-element.156), channel_id=1, source_target_pairs={{0,128},{64,192},{128,0},{192,64},{1,129},{65,193},{129,1},{193,65... | collective-permute-start | bytes 983048 | tf_op jit(solution)/shard_map/ppermute | solution.py:440
  12.5 2.6 %collective-permute-start.13 = (bf16[128,1280]{1,0:T(8,128)(2,1)S(1)}, bf16[128,1280]{1,0:T(8,128)(2,1)S(1)}, u32[]{:S(2)}, u32[]{:S(2)}) collective-permute-start(bf16[128,1280]{1,0:T(8,128)(2,1)S(1)} %get-tuple-element.160), channel_id=1, source_target_pairs={{0,192},{64,0},{128,64},{192,128},{1,193},{65,1},{129,65},{193,129... | collective-permute-start | bytes 983048 | tf_op jit(solution)/shard_map/ppermute | solution.py:440
  15.1 3.3 %shard_map.72 = (f32[128,2432]{1,0:T(8,128)S(1)}, bf16[640,2432]{1,0:T(8,128)(2,1)S(1)}) custom-call(s32[6]{0:T(128)S(1)} %stack.27.at, bf16[128,1280]{1,0:T(8,128)(2,1)S(1)} %get-tuple-element.154.block.b0, bf16[640,2432]{1,0:T(8,128)(2,1)} %head.1, bf16[640,2432]{1,0:T(8,128)(2,1)S(1)} %collective-permute-done.10.other), custom_call_target="tpu_custom_call" | custom-call | flops 796917760 | bytes 6225920 | tf_op jit(solution)/shard_map/pallas_call | solution.py:97
  18.4 2.5 %collective-permute-done.11.block.b2 = bf16[128,1280]{1,0:T(8,128)(2,1)S(1)} collective-permute-done((bf16[128,1280]{1,0:T(8,128)(2,1)S(1)}, bf16[128,1280]{1,0:T(8,128)(2,1)S(1)}, u32[]{:S(2)}, u32[]{:S(2)}) %collective-permute-start.11) | collective-permute-done | bytes 327712 | tf_op jit(solution)/shard_map/ppermute | solution.py:440
  20.9 1.9 %shard_map.73 = (s16[64,2560]{1,0:T(8,128)(2,1)S(1)}, s16[64,2560]{1,0:T(8,128)(2,1)S(1)}, f32[8,128]{1,0:T(8,128)S(1)}) custom-call(s32[6]{0:T(128)S(1)} %stack.27.at, bf16[128,1280]{1,0:T(8,128)(2,1)S(1)} %collective-permute-done.11.block.b2, bf16[640,2432]{1,0:T(8,128)(2,1)S(1)} %get-tuple-element.157.head, ...), custom_call_target="tpu_custom_call" | custom-call | flops 796917760 | bytes 6225920 | tf_op jit(solution)/shard_map/pallas_call | solution.py:97
  22.9 2.8 %collective-permute-start.14 = (s16[64,2560]{1,0:T(8,128)(2,1)S(1)}, s16[64,2560]{1,0:T(8,128)(2,1)S(1)}, u32[]{:S(2)}, u32[]{:S(2)}) collective-permute-start(s16[64,2560]{1,0:T(8,128)(2,1)S(1)} %get-tuple-element.163), channel_id=1, source_target_pairs={{0,192},{64,0},{128,64},{192,128},{1,193},{65,1},{129,65},{193,129... | collective-permute-start | bytes 983048 | tf_op jit(solution)/shard_map/ppermute | solution.py:459
  28.0 2.9 %shard_map.74 = (f32[64,2432]{1,0:T(8,128)S(1)}, f32[64,2432]{1,0:T(8,128)S(1)}, s16[64,2560]{1,0:T(8,128)(2,1)S(1)}, s16[64,2560]{1,0:T(8,128)(2,1)S(1)}, bf16[...) custom-call(s32[6]{0:T(128)S(1)} %stack.27.at, f32[8,128]{1,0:T(8,128)S(1)} %get-tuple-element.158.tick, ...), custom_call_target="tpu_custom_call" | custom-call | flops 1593835520 | bytes 6225920 | tf_op jit(solution)/shard_map/pallas_call | solution.py:97
  31.1 2.4 %collective-permute-start.17 = (s16[64,2560]{1,0:T(8,128)(2,1)S(1)}, s16[64,2560]{1,0:T(8,128)(2,1)S(1)}, u32[]{:S(2)}, u32[]{:S(2)}) collective-permute-start(s16[64,2560]{1,0:T(8,128)(2,1)S(1)} %get-tuple-element.166), channel_id=1, source_target_pairs={{0,192},{64,0},{128,64},{192,128},{1,193},{65,1},{129,65},{193,129... | collective-permute-start | bytes 983048 | tf_op jit(solution)/shard_map/ppermute | solution.py:470
  35.9 2.0 %collective-permute-start.16 = (s16[64,2560]{1,0:T(8,128)(2,1)S(1)}, s16[64,2560]{1,0:T(8,128)(2,1)S(1)}, u32[]{:S(2)}, u32[]{:S(2)}) collective-permute-start(s16[64,2560]{1,0:T(8,128)(2,1)S(1)} %get-tuple-element.165), channel_id=1, source_target_pairs={{0,192},{64,0},{128,64},{192,128},{1,193},{65,1},{129,65},{193,129... | collective-permute-start | bytes 983048 | tf_op jit(solution)/shard_map/ppermute | solution.py:472
  39.1 3.0 %collective-permute-done.17.q1_high = s16[64,2560]{1,0:T(8,128)(2,1)S(1)} collective-permute-done((s16[64,2560]{1,0:T(8,128)(2,1)S(1)}, s16[64,2560]{1,0:T(8,128)(2,1)S(1)}, u32[]{:S(2)}, u32[]{:S(2)}) %collective-permute-start.17) | collective-permute-done | bytes 327712 | tf_op jit(solution)/shard_map/ppermute | solution.py:470
  42.1 3.2 %collective-permute-done.18.q3_low = s16[64,2560]{1,0:T(8,128)(2,1)S(1)} collective-permute-done((s16[64,2560]{1,0:T(8,128)(2,1)S(1)}, s16[64,2560]{1,0:T(8,128)(2,1)S(1)}, u32[]{:S(2)}, u32[]{:S(2)}) %collective-permute-start.18) | collective-permute-done | bytes 327712 | tf_op jit(solution)/shard_map/ppermute | solution.py:470
  45.2 3.4 %collective-permute-done.16.q1_low = s16[64,2560]{1,0:T(8,128)(2,1)S(1)} collective-permute-done((s16[64,2560]{1,0:T(8,128)(2,1)S(1)}, s16[64,2560]{1,0:T(8,128)(2,1)S(1)}, u32[]{:S(2)}, u32[]{:S(2)}) %collective-permute-start.16) | collective-permute-done | bytes 327712 | tf_op jit(solution)/shard_map/ppermute | solution.py:472
  48.7 2.8 %collective-permute-done.19.q3_high = s16[64,2560]{1,0:T(8,128)(2,1)S(1)} collective-permute-done((s16[64,2560]{1,0:T(8,128)(2,1)S(1)}, s16[64,2560]{1,0:T(8,128)(2,1)S(1)}, u32[]{:S(2)}, u32[]{:S(2)}) %collective-permute-start.19) | collective-permute-done | bytes 327712 | tf_op jit(solution)/shard_map/ppermute | solution.py:472
  52.3 14.9 %all_to_all.42.parts = f32[8,8,128]{2,1,0:T(8,128)S(1)} all-to-all(f32[8,8,128]{2,1,0:T(8,128)S(1)} %get-tuple-element.171), channel_id=1, replica_groups=mesh['x'=4,'c'=2,'y'=4,'z'=8] {'z'}, dimensions={0} | all-to-all | bytes 65536 | tf_op jit(solution)/shard_map/all_to_all | solution.py:483
  67.3 12.5 %all_to_all.43.parts = f32[32,8,128]{2,1,0:T(8,128)S(1)} all-to-all(f32[32,8,128]{2,1,0:T(8,128)S(1)} %shard_map.78), channel_id=1, replica_groups=mesh['x'=4,'c'=2,'y'=4,'z'=8] {'x','c','y'}, dimensions={0} | all-to-all | bytes 262144 | tf_op jit(solution)/shard_map/all_to_all | solution.py:490
  79.8 2.1 %shard_map.79 = (f32[8,128]{1,0:T(8,128)S(1)}, f32[8,128]{1,0:T(8,128)S(1)}, f32[8,128]{1,0:T(8,128)S(1)}, f32[8,128]{1,0:T(8,128)S(1)}, s32[1,1]{1,0:T(1,128)}) custom-call(f32[32,8,128]{2,1,0:T(8,128)S(1)} %all_to_all.43.parts), custom_call_target="tpu_custom_call" | custom-call | tf_op jit(solution)/shard_map/pallas_call | solution.py:97
  85.8 4.2 %collective-permute-done.23 = bf16[32,2432]{1,0:T(8,128)(2,1)S(1)} collective-permute-done((bf16[32,2432]{1,0:T(8,128)(2,1)S(1)}, bf16[32,2432]{1,0:T(8,128)(2,1)S(1)}, u32[]{:S(2)}, u32[]{:S(2)}) %collective-permute-start.23) | collective-permute-done | bytes 155680 | tf_op jit(solution)/shard_map/ppermute | solution.py:508
  90.0 2.6 %collective-permute-done.22 = bf16[32,2432]{1,0:T(8,128)(2,1)S(1)} collective-permute-done((bf16[32,2432]{1,0:T(8,128)(2,1)S(1)}, bf16[32,2432]{1,0:T(8,128)(2,1)S(1)}, u32[]{:S(2)}, u32[]{:S(2)}) %collective-permute-start.22) | collective-permute-done | bytes 155680 | tf_op jit(solution)/shard_map/ppermute | solution.py:508
  92.7 2.2 %collective-permute-done.21 = bf16[32,2432]{1,0:T(8,128)(2,1)S(1)} collective-permute-done((bf16[32,2432]{1,0:T(8,128)(2,1)S(1)}, bf16[32,2432]{1,0:T(8,128)(2,1)S(1)}, u32[]{:S(2)}, u32[]{:S(2)}) %collective-permute-start.21) | collective-permute-done | bytes 155680 | tf_op jit(solution)/shard_map/ppermute | solution.py:508
  98.8 27.5 %conditional.1 = (f32[32,640]{1,0:T(8,128)}, f32[640,2432]{1,0:T(8,128)}) conditional(s32[]{:T(128)} %bitcast.17, (s32[6]{0:T(128)S(1)}, f32[8,128]{1,0:T(8,128)S(1)}, bf16[512,640]{1,0:T(8,128)(2,1)S(1)}, bf16[512,640]{1,0:T(8,128)(2,1)S(1)}, bf16[256,2432]{1,0:T(8,128)(2,1)S(1)}, /*index=5*/bf16[64,640]{1,0:T(8,128)(2,1)S(1)}, ...), branch_computations={%region_0.0_spmd, %region_1.0_spmd, %region_2.17_spmd} | conditional | flops 9566442496 | bytes 125846592 | solution.py:553
  102.3 3.8 %branch_0_fun.4 = (f32[640,2432]{1,0:T(8,128)}, f32[8,128]{1,0:T(8,128)S(1)}) custom-call(s32[6]{0:T(128)S(1)} %get-tuple-element.74.at, f32[8,128]{1,0:T(8,128)S(1)} %get-tuple-element.75.packed_all.above.after, bf16[512,640]{1,0:T(8,128)(2,1)S(1)} %get-tuple-element.76.hid_mine, bf16[512,640]{1,0:T(8,128)(2,1)S(1)} %get-tuple-element.77.hid_theirs, ...), custom_call_target="tpu_custom_call" | custom-call | flops 478150656 | bytes 1245184 | tf_op jit(solution)/shard_map/cond/branch_0_fun/pallas_call | solution.py:375
  108.7 4.8 %all-to-all-start = ((f32[8,16,640]{2,1,0:T(8,128)}), f32[8,16,640]{2,1,0:T(8,128)S(1)}, u32[]{:S(2)}, u32[]{:S(2)}) async-start(f32[8,16,640]{2,1,0:T(8,128)} %bitcast), calls=%async_computation | async-start | bytes 655360 | tf_op jit(solution)/shard_map/cond/branch_0_fun/all_to_all | solution.py:531
  113.5 3.1 %branch_0_fun.7 = (f32[640,2432]{1,0:T(8,128)}, f32[8,128]{1,0:T(8,128)}) custom-call(s32[6]{0:T(128)S(1)} %get-tuple-element.74.at, f32[8,128]{1,0:T(8,128)S(1)} %get-tuple-element.75.packed_all.above.after, bf16[512,640]{1,0:T(8,128)(2,1)} %copy-done.2, bf16[512,640]{1,0:T(8,128)(2,1)S(1)} %get-tuple-element.77.hid_theirs, ...), custom_call_target="tpu_custom_call", output_to_operand_aliasing={{0}: (5, {})} | custom-call | flops 318767104 | bytes 1245184 | tf_op jit(solution)/shard_map/cond/branch_0_fun/pallas_call | solution.py:375
  116.6 8.2 %all-to-all-done = f32[8,16,640]{2,1,0:T(8,128)S(1)} async-done(((f32[8,16,640]{2,1,0:T(8,128)}), f32[8,16,640]{2,1,0:T(8,128)S(1)}, u32[]{:S(2)}, u32[]{:S(2)}) %all-to-all-start) | async-done | bytes 327712 | tf_op jit(solution)/shard_map/cond/branch_0_fun/all_to_all | solution.py:531
  (42 shorter events, 23.8 us)
Async XLA Ops:
  7.2 8.0 %collective-permute-start.10 = (bf16[640,2432]{1,0:T(8,128)(2,1)}, bf16[640,2432]{1,0:T(8,128)(2,1)S(1)}, u32[]{:S(2)}, u32[]{:S(2)}) collective-permute-start(bf16[640,2432]{1,0:T(8,128)(2,1)} %head.1), channel_id=1, source_target_pairs={{0,32},{32,0},{1,33},{33,1},{2,34},{34,2},{3,35},{35,3},{4,36},{36... | collective-permute-start | bytes 9338888 | tf_op jit(solution)/shard_map/ppermute | solution.py:436
  8.8 12.1 %collective-permute-start.11 = (bf16[128,1280]{1,0:T(8,128)(2,1)S(1)}, bf16[128,1280]{1,0:T(8,128)(2,1)S(1)}, u32[]{:S(2)}, u32[]{:S(2)}) collective-permute-start(bf16[128,1280]{1,0:T(8,128)(2,1)S(1)} %get-tuple-element.156), channel_id=1, source_target_pairs={{0,128},{64,192},{128,0},{192,64},{1,129},{65,193},{129,1},{193,65... | collective-permute-start | bytes 983048 | tf_op jit(solution)/shard_map/ppermute | solution.py:440
  11.9 15.6 %collective-permute-start.12 = (bf16[128,1280]{1,0:T(8,128)(2,1)S(1)}, bf16[128,1280]{1,0:T(8,128)(2,1)S(1)}, u32[]{:S(2)}, u32[]{:S(2)}) collective-permute-start(bf16[128,1280]{1,0:T(8,128)(2,1)S(1)} %get-tuple-element.159), channel_id=1, source_target_pairs={{0,64},{64,128},{128,192},{192,0},{1,65},{65,129},{129,193},{193,1... | collective-permute-start | bytes 983048 | tf_op jit(solution)/shard_map/ppermute | solution.py:440
  12.5 15.5 %collective-permute-start.13 = (bf16[128,1280]{1,0:T(8,128)(2,1)S(1)}, bf16[128,1280]{1,0:T(8,128)(2,1)S(1)}, u32[]{:S(2)}, u32[]{:S(2)}) collective-permute-start(bf16[128,1280]{1,0:T(8,128)(2,1)S(1)} %get-tuple-element.160), channel_id=1, source_target_pairs={{0,192},{64,0},{128,64},{192,128},{1,193},{65,1},{129,65},{193,129... | collective-permute-start | bytes 983048 | tf_op jit(solution)/shard_map/ppermute | solution.py:440
  22.9 12.2 %collective-permute-start.14 = (s16[64,2560]{1,0:T(8,128)(2,1)S(1)}, s16[64,2560]{1,0:T(8,128)(2,1)S(1)}, u32[]{:S(2)}, u32[]{:S(2)}) collective-permute-start(s16[64,2560]{1,0:T(8,128)(2,1)S(1)} %get-tuple-element.163), channel_id=1, source_target_pairs={{0,192},{64,0},{128,64},{192,128},{1,193},{65,1},{129,65},{193,129... | collective-permute-start | bytes 983048 | tf_op jit(solution)/shard_map/ppermute | solution.py:459
  25.7 9.8 %collective-permute-start.15 = (s16[64,2560]{1,0:T(8,128)(2,1)S(1)}, s16[64,2560]{1,0:T(8,128)(2,1)S(1)}, u32[]{:S(2)}, u32[]{:S(2)}) collective-permute-start(s16[64,2560]{1,0:T(8,128)(2,1)S(1)} %get-tuple-element.164), channel_id=1, source_target_pairs={{0,64},{64,128},{128,192},{192,0},{1,65},{65,129},{129,193},{193,1... | collective-permute-start | bytes 983048 | tf_op jit(solution)/shard_map/ppermute | solution.py:459
  31.0 20.5 %collective-permute-start.20 = (bf16[512,640]{1,0:T(8,128)(2,1)S(1)}, bf16[512,640]{1,0:T(8,128)(2,1)S(1)}, u32[]{:S(2)}, u32[]{:S(2)}) collective-permute-start(bf16[512,640]{1,0:T(8,128)(2,1)S(1)} %get-tuple-element.170), channel_id=1, source_target_pairs={{0,32},{32,0},{1,33},{33,1},{2,34},{34,2},{3,35},{35,3},{4,36},{36... | collective-permute-start | bytes 1966088 | tf_op jit(solution)/shard_map/ppermute | solution.py:474
  31.1 11.0 %collective-permute-start.17 = (s16[64,2560]{1,0:T(8,128)(2,1)S(1)}, s16[64,2560]{1,0:T(8,128)(2,1)S(1)}, u32[]{:S(2)}, u32[]{:S(2)}) collective-permute-start(s16[64,2560]{1,0:T(8,128)(2,1)S(1)} %get-tuple-element.166), channel_id=1, source_target_pairs={{0,192},{64,0},{128,64},{192,128},{1,193},{65,1},{129,65},{193,129... | collective-permute-start | bytes 983048 | tf_op jit(solution)/shard_map/ppermute | solution.py:470
  33.5 11.8 %collective-permute-start.18 = (s16[64,2560]{1,0:T(8,128)(2,1)S(1)}, s16[64,2560]{1,0:T(8,128)(2,1)S(1)}, u32[]{:S(2)}, u32[]{:S(2)}) collective-permute-start(s16[64,2560]{1,0:T(8,128)(2,1)S(1)} %get-tuple-element.167), channel_id=1, source_target_pairs={{0,64},{64,128},{128,192},{192,0},{1,65},{65,129},{129,193},{193,1... | collective-permute-start | bytes 983048 | tf_op jit(solution)/shard_map/ppermute | solution.py:470
  35.9 12.8 %collective-permute-start.16 = (s16[64,2560]{1,0:T(8,128)(2,1)S(1)}, s16[64,2560]{1,0:T(8,128)(2,1)S(1)}, u32[]{:S(2)}, u32[]{:S(2)}) collective-permute-start(s16[64,2560]{1,0:T(8,128)(2,1)S(1)} %get-tuple-element.165), channel_id=1, source_target_pairs={{0,192},{64,0},{128,64},{192,128},{1,193},{65,1},{129,65},{193,129... | collective-permute-start | bytes 983048 | tf_op jit(solution)/shard_map/ppermute | solution.py:472
  37.9 13.6 %collective-permute-start.19 = (s16[64,2560]{1,0:T(8,128)(2,1)S(1)}, s16[64,2560]{1,0:T(8,128)(2,1)S(1)}, u32[]{:S(2)}, u32[]{:S(2)}) collective-permute-start(s16[64,2560]{1,0:T(8,128)(2,1)S(1)} %get-tuple-element.168), channel_id=1, source_target_pairs={{0,64},{64,128},{128,192},{192,0},{1,65},{65,129},{129,193},{193,1... | collective-permute-start | bytes 983048 | tf_op jit(solution)/shard_map/ppermute | solution.py:472
  51.5 15.8 %copy-start.5 = (s32[128]{0:T(128)S(1)}, s32[128]{0:T(128)}, u32[]{:S(2)}) copy-start(s32[128]{0:T(128)} %param.13) | copy-start | bytes 1540
  51.5 15.8 %copy-start.6 = (f32[128]{0:T(128)S(1)}, f32[128]{0:T(128)}, u32[]{:S(2)}) copy-start(f32[128]{0:T(128)} %param.14) | copy-start | bytes 1540
  51.5 30.4 %copy-start.4 = (s32[128]{0:T(128)S(1)}, s32[128]{0:T(128)}, u32[]{:S(2)}) copy-start(s32[128]{0:T(128)} %param.12) | copy-start | bytes 1540
  83.1 6.9 %collective-permute-start.23 = (bf16[32,2432]{1,0:T(8,128)(2,1)S(1)}, bf16[32,2432]{1,0:T(8,128)(2,1)S(1)}, u32[]{:S(2)}, u32[]{:S(2)}) collective-permute-start(bf16[32,2432]{1,0:T(8,128)(2,1)S(1)} %shard_map.80), channel_id=1, source_target_pairs={{0,192},{64,0},{128,64},{192,128},{1,193},{65,1},{129,65},{193,129... | collective-permute-start | bytes 466952 | tf_op jit(solution)/shard_map/ppermute | solution.py:508
  84.2 8.4 %collective-permute-start.22 = (bf16[32,2432]{1,0:T(8,128)(2,1)S(1)}, bf16[32,2432]{1,0:T(8,128)(2,1)S(1)}, u32[]{:S(2)}, u32[]{:S(2)}) collective-permute-start(bf16[32,2432]{1,0:T(8,128)(2,1)S(1)} %shard_map.80), channel_id=1, source_target_pairs={{0,128},{64,192},{128,0},{192,64},{1,129},{65,193},{129,1},{193,65... | collective-permute-start | bytes 466952 | tf_op jit(solution)/shard_map/ppermute | solution.py:508
  85.8 9.1 %collective-permute-start.21 = (bf16[32,2432]{1,0:T(8,128)(2,1)S(1)}, bf16[32,2432]{1,0:T(8,128)(2,1)S(1)}, u32[]{:S(2)}, u32[]{:S(2)}) collective-permute-start(bf16[32,2432]{1,0:T(8,128)(2,1)S(1)} %shard_map.80), channel_id=1, source_target_pairs={{0,64},{64,128},{128,192},{192,0},{1,65},{65,129},{129,193},{193,1... | collective-permute-start | bytes 466952 | tf_op jit(solution)/shard_map/ppermute | solution.py:508
  94.9 2.1 %collective-permute-start.24 = (bf16[128,2432]{1,0:T(8,128)(2,1)S(1)}, bf16[128,2432]{1,0:T(8,128)(2,1)S(1)}, u32[]{:S(2)}, u32[]{:S(2)}) collective-permute-start(bf16[128,2432]{1,0:T(8,128)(2,1)S(1)} %pad_maximum_fusion.1.mine), channel_id=1, source_target_pairs={{0,32},{32,0},{1,33},{33,1},{2,34},{34,2},{3,35},{35,3},{4,36},{36... | collective-permute-start | bytes 1867784 | tf_op jit(solution)/shard_map/ppermute | solution.py:510
  98.8 9.9 %copy-start.2 = (bf16[512,640]{1,0:T(8,128)(2,1)}, bf16[512,640]{1,0:T(8,128)(2,1)S(1)}, u32[]{:S(2)}) copy-start(bf16[512,640]{1,0:T(8,128)(2,1)S(1)} %get-tuple-element.76.hid_mine) | copy-start | bytes 1966084 | tf_op jit(solution)/shard_map/cond
  98.8 7.5 %collective-permute-start = (bf16[64,640]{1,0:T(8,128)(2,1)S(1)}, bf16[64,640]{1,0:T(8,128)(2,1)S(1)}, u32[]{:S(2)}, u32[]{:S(2)}) collective-permute-start(bf16[64,640]{1,0:T(8,128)(2,1)S(1)} %get-tuple-element.81), channel_id=1, source_target_pairs={{0,8},{8,16},{16,24},{24,0},{1,9},{9,17},{17,25},{25,1},{2,10},{10... | collective-permute-start | bytes 245768 | tf_op jit(solution)/shard_map/cond/branch_0_fun/ppermute | solution.py:520
  99.4 6.9 %collective-permute-start.1 = (bf16[64,640]{1,0:T(8,128)(2,1)S(1)}, bf16[64,640]{1,0:T(8,128)(2,1)S(1)}, u32[]{:S(2)}, u32[]{:S(2)}) collective-permute-start(bf16[64,640]{1,0:T(8,128)(2,1)S(1)} %get-tuple-element.82), channel_id=1, source_target_pairs={{0,16},{8,24},{16,0},{24,8},{1,17},{9,25},{17,1},{25,9},{2,18},{10... | collective-permute-start | bytes 245768 | tf_op jit(solution)/shard_map/cond/branch_0_fun/ppermute | solution.py:520
  101.3 5.6 %collective-permute-start.2 = (bf16[64,640]{1,0:T(8,128)(2,1)S(1)}, bf16[64,640]{1,0:T(8,128)(2,1)S(1)}, u32[]{:S(2)}, u32[]{:S(2)}) collective-permute-start(bf16[64,640]{1,0:T(8,128)(2,1)S(1)} %get-tuple-element.83), channel_id=1, source_target_pairs={{0,24},{8,0},{16,8},{24,16},{1,25},{9,1},{17,9},{25,17},{2,26},{10... | collective-permute-start | bytes 245768 | tf_op jit(solution)/shard_map/cond/branch_0_fun/ppermute | solution.py:520
  108.7 16.1 %all-to-all-start = ((f32[8,16,640]{2,1,0:T(8,128)}), f32[8,16,640]{2,1,0:T(8,128)S(1)}, u32[]{:S(2)}, u32[]{:S(2)}) async-start(f32[8,16,640]{2,1,0:T(8,128)} %bitcast), calls=%async_computation | async-start | bytes 655360 | tf_op jit(solution)/shard_map/cond/branch_0_fun/all_to_all | solution.py:531

commit v7 on v6

--- a/solution.py
+++ b/solution.py
@@ -115,12 +115,17 @@
 LN2_64 = float(np.log(2.0) / 64.0)
 
 
-def split_kernel(at, hidden, b0, b1, b2, b3):
+def split_kernel(at, hidden, b0, b1, b2, b3, sems):
     chip_rows = b0.shape[1]
-    nx = hidden.shape[1] // chip_rows
+    copies = []
     for s, out in enumerate((b0, b1, b2, b3)):
-        to = lax.rem(at[0] + s, nx) * chip_rows
-        out[...] = hidden[:, pl.ds(pl.multiple_of(to, 128), chip_rows)]
+        to = lax.rem(at[0] + s, NX) * chip_rows
+        block = hidden.at[:, pl.ds(pl.multiple_of(to, 128), chip_rows)]
+        copies.append(pltpu.make_async_copy(block, out, sems.at[s]))
+    for copy in copies:
+        copy.start()
+    for copy in copies:
+        copy.wait()
 
 
 def turn_kernel(tick, head, turned):
@@ -403,16 +408,16 @@
         )
         spread.append(part.astype(bf16))
     spread = jnp.concatenate(spread, axis=1)
-    total = jnp.zeros(out.shape, f32)
+    total = jnp.zeros((size, r0.shape[1]), f32)
     for r in (r0, r1, r2, r3):
         total = total + jnp.dot(spread, r[...], preferred_element_type=f32)
-    out[...] = total
+    pack(total, out, slice(0, size))
 
 
 def sum_kernel(at, parts, slot_all, out, ranks):
-    total = parts[0:CAP, :]
+    total = unpack(parts, slice(0, CAP))
     for i in range(1, parts.shape[0] // CAP):
-        total = total + parts[i * CAP : (i + 1) * CAP, :]
+        total = total + unpack(parts, slice(i * CAP, (i + 1) * CAP))
     group = out.shape[0]
     per_owner = 128 // group
     owner, place = at[4] // per_owner, lax.rem(at[4], per_owner)
@@ -436,7 +441,15 @@
     head_other = lax.ppermute(head, "c", SWAP)
 
     block_shape = struct((tokens, chip_rows), bf16)
-    b0, *leave = call(split_kernel, [block_shape] * 4, [at, hidden_states], smem=1)
+    b0, *leave = call(
+        split_kernel,
+        [block_shape] * 4,
+        [at, hidden_states],
+        [pltpu.SemaphoreType.DMA((nx,))],
+        smem=1,
+        loose=1,
+        out_specs=[pl.BlockSpec(memory_space=pltpu.VMEM)] * 4,
+    )
     came = {s: lax.ppermute(leave[s - 1], "x", ring(nx, s)) for s in (2, 1, 3)}
     partial = struct((tokens, voc_cols), f32)
     tick_shape = struct((8, 128), f32)
@@ -524,7 +537,7 @@
         head_grad, tick = outer(*sides, 0, early, packed_all, packed_all)
         spread, tick = call(
             spread_kernel,
-            [struct((n_voc * CAP // nx, rows), f32), tick_shape],
+            [struct((n_voc * CAP // nx, rows + 128), jnp.int16), tick_shape],
             [at, tick, *parts, packed_all, slot_all],
             smem=1,
         )

time: 135 us -> 133 us (0.985)
  waiting for transfers between devices: 38.7 us -> 36.1 us
    all_to_all x1, waiting for transfers between devices: 8.19 us -> 5.39 us  [finish(): spread = lax.all_to_all(spread, 'z', 0, 0, tiled=True)]
  transfers between devices with their start and end apart: 19 -> 19, of which waited for: 16 -> 16; matrix products, arithmetic and copies ran while one was open for 0% -> 0% of each run, Pallas kernels for 13% -> 14%
where the time goes in v7:
time: 133 us; the launch traced here: 131 us
  waiting for transfers between devices  36.1 us (27%)
  blocking collectives  27.4 us (21%)
  Pallas kernels  27.3 us (21%)
  starting transfers between devices  25 us (19%)
  between operations  14.8 us (11%)
    pallas_call x13, Pallas kernels, call(): pl.pallas_call(kernel, in_specs=specs, out_shape=out, scratch_shapes=list...  20.4 us
    all_to_all x1, blocking collectives, shards(): stats = lax.all_to_all(stats, 'z', 0, 0, tiled=True)  14.9 us
    all_to_all x1, blocking collectives, shards(): stats = lax.all_to_all(stats, everyone, 0, 0, tiled=True)  12.5 us
    ppermute x3, waiting for transfers between devices, backward(): pieces = {s: lax.ppermute(piece, 'x', ring(nx, s)) for s in (2, 1, 3)}  9.02 us
    pallas_call x2, Pallas kernels, outer(): pl.pallas_call(outer_kernel, grid=(count,), in_specs=in_specs, out_specs=...  6.87 us
    ppermute x3, starting transfers between devices, shards(): came = {s: lax.ppermute(leave[s - 1], 'x', ring(nx, s)) for s in (2, 1, 3)}  6.35 us
    all_to_all x1, waiting for transfers between devices, finish(): spread = lax.all_to_all(spread, 'z', 0, 0, tiled=True)  5.39 us
    ppermute x3, waiting for transfers between devices, shards(): came = {s: lax.ppermute(leave[s - 1], 'x', ring(nx, s)) for s in (2, 1, 3)}  4.83 us
  transfers between devices with their start and end apart: 19, of which 16 were waited for; matrix products, arithmetic and copies ran while one was open for 0% of the time, Pallas kernels for 14%

profile of v7, /device:TPU:32, one launch (start us, length us, event | category | flops | bytes accessed | tf_op | source)
XLA Modules:
  0.0 130.7 jit_solution(9532894014918321338)
XLA Ops:
  9.2 3.1 %collective-permute-start.11 = (bf16[128,1280]{1,0:T(8,128)(2,1)S(1)}, bf16[128,1280]{1,0:T(8,128)(2,1)S(1)}, u32[]{:S(2)}, u32[]{:S(2)}) collective-permute-start(bf16[128,1280]{1,0:T(8,128)(2,1)S(1)} %get-tuple-element.156), channel_id=1, source_target_pairs={{0,128},{64,192},{128,0},{192,64},{1,129},{65,193},{129,1},{193,65... | collective-permute-start | bytes 983048 | tf_op jit(solution)/shard_map/ppermute | solution.py:453
  12.9 2.6 %collective-permute-start.13 = (bf16[128,1280]{1,0:T(8,128)(2,1)S(1)}, bf16[128,1280]{1,0:T(8,128)(2,1)S(1)}, u32[]{:S(2)}, u32[]{:S(2)}) collective-permute-start(bf16[128,1280]{1,0:T(8,128)(2,1)S(1)} %get-tuple-element.160), channel_id=1, source_target_pairs={{0,192},{64,0},{128,64},{192,128},{1,193},{65,1},{129,65},{193,129... | collective-permute-start | bytes 983048 | tf_op jit(solution)/shard_map/ppermute | solution.py:453
  15.6 3.3 %shard_map.72 = (f32[128,2432]{1,0:T(8,128)S(1)}, bf16[640,2432]{1,0:T(8,128)(2,1)S(1)}) custom-call(s32[6]{0:T(128)S(1)} %stack.27.at, bf16[128,1280]{1,0:T(8,128)(2,1)S(1)} %get-tuple-element.154.block.b0, bf16[640,2432]{1,0:T(8,128)(2,1)} %head.1, bf16[640,2432]{1,0:T(8,128)(2,1)S(1)} %collective-permute-done.10.other), custom_call_target="tpu_custom_call" | custom-call | flops 796917760 | bytes 6225920 | tf_op jit(solution)/shard_map/pallas_call | solution.py:97
  18.9 2.5 %collective-permute-done.11.block.b2 = bf16[128,1280]{1,0:T(8,128)(2,1)S(1)} collective-permute-done((bf16[128,1280]{1,0:T(8,128)(2,1)S(1)}, bf16[128,1280]{1,0:T(8,128)(2,1)S(1)}, u32[]{:S(2)}, u32[]{:S(2)}) %collective-permute-start.11) | collective-permute-done | bytes 327712 | tf_op jit(solution)/shard_map/ppermute | solution.py:453
  21.4 1.9 %shard_map.73 = (s16[64,2560]{1,0:T(8,128)(2,1)S(1)}, s16[64,2560]{1,0:T(8,128)(2,1)S(1)}, f32[8,128]{1,0:T(8,128)S(1)}) custom-call(s32[6]{0:T(128)S(1)} %stack.27.at, bf16[128,1280]{1,0:T(8,128)(2,1)S(1)} %collective-permute-done.11.block.b2, bf16[640,2432]{1,0:T(8,128)(2,1)S(1)} %get-tuple-element.157.head, ...), custom_call_target="tpu_custom_call" | custom-call | flops 796917760 | bytes 6225920 | tf_op jit(solution)/shard_map/pallas_call | solution.py:97
  23.3 2.8 %collective-permute-start.14 = (s16[64,2560]{1,0:T(8,128)(2,1)S(1)}, s16[64,2560]{1,0:T(8,128)(2,1)S(1)}, u32[]{:S(2)}, u32[]{:S(2)}) collective-permute-start(s16[64,2560]{1,0:T(8,128)(2,1)S(1)} %get-tuple-element.163), channel_id=1, source_target_pairs={{0,192},{64,0},{128,64},{192,128},{1,193},{65,1},{129,65},{193,129... | collective-permute-start | bytes 983048 | tf_op jit(solution)/shard_map/ppermute | solution.py:472
  28.5 2.9 %shard_map.74 = (f32[64,2432]{1,0:T(8,128)S(1)}, f32[64,2432]{1,0:T(8,128)S(1)}, s16[64,2560]{1,0:T(8,128)(2,1)S(1)}, s16[64,2560]{1,0:T(8,128)(2,1)S(1)}, bf16[...) custom-call(s32[6]{0:T(128)S(1)} %stack.27.at, f32[8,128]{1,0:T(8,128)S(1)} %get-tuple-element.158.tick, ...), custom_call_target="tpu_custom_call" | custom-call | flops 1593835520 | bytes 6225920 | tf_op jit(solution)/shard_map/pallas_call | solution.py:97
  31.5 2.4 %collective-permute-start.17 = (s16[64,2560]{1,0:T(8,128)(2,1)S(1)}, s16[64,2560]{1,0:T(8,128)(2,1)S(1)}, u32[]{:S(2)}, u32[]{:S(2)}) collective-permute-start(s16[64,2560]{1,0:T(8,128)(2,1)S(1)} %get-tuple-element.166), channel_id=1, source_target_pairs={{0,192},{64,0},{128,64},{192,128},{1,193},{65,1},{129,65},{193,129... | collective-permute-start | bytes 983048 | tf_op jit(solution)/shard_map/ppermute | solution.py:483
  39.3 3.2 %collective-permute-done.17.q1_high = s16[64,2560]{1,0:T(8,128)(2,1)S(1)} collective-permute-done((s16[64,2560]{1,0:T(8,128)(2,1)S(1)}, s16[64,2560]{1,0:T(8,128)(2,1)S(1)}, u32[]{:S(2)}, u32[]{:S(2)}) %collective-permute-start.17) | collective-permute-done | bytes 327712 | tf_op jit(solution)/shard_map/ppermute | solution.py:483
  42.5 3.2 %collective-permute-done.18.q3_low = s16[64,2560]{1,0:T(8,128)(2,1)S(1)} collective-permute-done((s16[64,2560]{1,0:T(8,128)(2,1)S(1)}, s16[64,2560]{1,0:T(8,128)(2,1)S(1)}, u32[]{:S(2)}, u32[]{:S(2)}) %collective-permute-start.18) | collective-permute-done | bytes 327712 | tf_op jit(solution)/shard_map/ppermute | solution.py:483
  45.7 3.4 %collective-permute-done.16.q1_low = s16[64,2560]{1,0:T(8,128)(2,1)S(1)} collective-permute-done((s16[64,2560]{1,0:T(8,128)(2,1)S(1)}, s16[64,2560]{1,0:T(8,128)(2,1)S(1)}, u32[]{:S(2)}, u32[]{:S(2)}) %collective-permute-start.16) | collective-permute-done | bytes 327712 | tf_op jit(solution)/shard_map/ppermute | solution.py:485
  49.1 2.8 %collective-permute-done.19.q3_high = s16[64,2560]{1,0:T(8,128)(2,1)S(1)} collective-permute-done((s16[64,2560]{1,0:T(8,128)(2,1)S(1)}, s16[64,2560]{1,0:T(8,128)(2,1)S(1)}, u32[]{:S(2)}, u32[]{:S(2)}) %collective-permute-start.19) | collective-permute-done | bytes 327712 | tf_op jit(solution)/shard_map/ppermute | solution.py:485
  52.8 14.9 %all_to_all.42.parts = f32[8,8,128]{2,1,0:T(8,128)S(1)} all-to-all(f32[8,8,128]{2,1,0:T(8,128)S(1)} %get-tuple-element.171), channel_id=1, replica_groups=mesh['x'=4,'c'=2,'y'=4,'z'=8] {'z'}, dimensions={0} | all-to-all | bytes 65536 | tf_op jit(solution)/shard_map/all_to_all | solution.py:496
  67.8 12.5 %all_to_all.43.parts = f32[32,8,128]{2,1,0:T(8,128)S(1)} all-to-all(f32[32,8,128]{2,1,0:T(8,128)S(1)} %shard_map.78), channel_id=1, replica_groups=mesh['x'=4,'c'=2,'y'=4,'z'=8] {'x','c','y'}, dimensions={0} | all-to-all | bytes 262144 | tf_op jit(solution)/shard_map/all_to_all | solution.py:503
  80.3 2.1 %shard_map.79 = (f32[8,128]{1,0:T(8,128)S(1)}, f32[8,128]{1,0:T(8,128)S(1)}, f32[8,128]{1,0:T(8,128)S(1)}, f32[8,128]{1,0:T(8,128)S(1)}, s32[1,1]{1,0:T(1,128)}) custom-call(f32[32,8,128]{2,1,0:T(8,128)S(1)} %all_to_all.43.parts), custom_call_target="tpu_custom_call" | custom-call | tf_op jit(solution)/shard_map/pallas_call | solution.py:97
  86.3 4.2 %collective-permute-done.23 = bf16[32,2432]{1,0:T(8,128)(2,1)S(1)} collective-permute-done((bf16[32,2432]{1,0:T(8,128)(2,1)S(1)}, bf16[32,2432]{1,0:T(8,128)(2,1)S(1)}, u32[]{:S(2)}, u32[]{:S(2)}) %collective-permute-start.23) | collective-permute-done | bytes 155680 | tf_op jit(solution)/shard_map/ppermute | solution.py:521
  90.4 2.6 %collective-permute-done.22 = bf16[32,2432]{1,0:T(8,128)(2,1)S(1)} collective-permute-done((bf16[32,2432]{1,0:T(8,128)(2,1)S(1)}, bf16[32,2432]{1,0:T(8,128)(2,1)S(1)}, u32[]{:S(2)}, u32[]{:S(2)}) %collective-permute-start.22) | collective-permute-done | bytes 155680 | tf_op jit(solution)/shard_map/ppermute | solution.py:521
  93.1 2.2 %collective-permute-done.21 = bf16[32,2432]{1,0:T(8,128)(2,1)S(1)} collective-permute-done((bf16[32,2432]{1,0:T(8,128)(2,1)S(1)}, bf16[32,2432]{1,0:T(8,128)(2,1)S(1)}, u32[]{:S(2)}, u32[]{:S(2)}) %collective-permute-start.21) | collective-permute-done | bytes 155680 | tf_op jit(solution)/shard_map/ppermute | solution.py:521
  99.2 24.7 %conditional.1 = (f32[32,640]{1,0:T(8,128)}, f32[640,2432]{1,0:T(8,128)}) conditional(s32[]{:T(128)} %bitcast.17, (s32[6]{0:T(128)S(1)}, f32[8,128]{1,0:T(8,128)S(1)}, bf16[512,640]{1,0:T(8,128)(2,1)S(1)}, bf16[512,640]{1,0:T(8,128)(2,1)S(1)}, bf16[256,2432]{1,0:T(8,128)(2,1)S(1)}, /*index=5*/bf16[64,640]{1,0:T(8,128)(2,1)S(1)}, ...), branch_computations={%region_0.0_spmd, %region_1.0_spmd, %region_2.17_spmd} | conditional | flops 9566442496 | bytes 125846592 | solution.py:566
  99.8 1.9 %collective-permute-start.1 = (bf16[64,640]{1,0:T(8,128)(2,1)S(1)}, bf16[64,640]{1,0:T(8,128)(2,1)S(1)}, u32[]{:S(2)}, u32[]{:S(2)}) collective-permute-start(bf16[64,640]{1,0:T(8,128)(2,1)S(1)} %get-tuple-element.82), channel_id=1, source_target_pairs={{0,16},{8,24},{16,0},{24,8},{1,17},{9,25},{17,1},{25,9},{2,18},{10... | collective-permute-start | bytes 245768 | tf_op jit(solution)/shard_map/cond/branch_0_fun/ppermute | solution.py:533
  102.8 3.8 %branch_0_fun.4 = (f32[640,2432]{1,0:T(8,128)}, f32[8,128]{1,0:T(8,128)S(1)}) custom-call(s32[6]{0:T(128)S(1)} %get-tuple-element.74.at, f32[8,128]{1,0:T(8,128)S(1)} %get-tuple-element.75.packed_all.above.after, bf16[512,640]{1,0:T(8,128)(2,1)S(1)} %get-tuple-element.76.hid_mine, bf16[512,640]{1,0:T(8,128)(2,1)S(1)} %get-tuple-element.77.hid_theirs, ...), custom_call_target="tpu_custom_call" | custom-call | flops 478150656 | bytes 1245184 | tf_op jit(solution)/shard_map/cond/branch_0_fun/pallas_call | solution.py:380
  109.2 4.8 %all-to-all-start = ((s16[8,16,768]{2,1,0:T(8,128)(2,1)}), s16[8,16,768]{2,1,0:T(8,128)(2,1)S(1)}, u32[]{:S(2)}, u32[]{:S(2)}) async-start(s16[8,16,768]{2,1,0:T(8,128)(2,1)} %bitcast), calls=%async_computation | async-start | bytes 393216 | tf_op jit(solution)/shard_map/cond/branch_0_fun/all_to_all | solution.py:544
  114.0 3.1 %branch_0_fun.7 = (f32[640,2432]{1,0:T(8,128)}, f32[8,128]{1,0:T(8,128)}) custom-call(s32[6]{0:T(128)S(1)} %get-tuple-element.74.at, f32[8,128]{1,0:T(8,128)S(1)} %get-tuple-element.75.packed_all.above.after, bf16[512,640]{1,0:T(8,128)(2,1)} %copy-done.2, bf16[512,640]{1,0:T(8,128)(2,1)S(1)} %get-tuple-element.77.hid_theirs, ...), custom_call_target="tpu_custom_call", output_to_operand_aliasing={{0}: (5, {})} | custom-call | flops 318767104 | bytes 1245184 | tf_op jit(solution)/shard_map/cond/branch_0_fun/pallas_call | solution.py:380
  117.0 5.4 %all-to-all-done = s16[8,16,768]{2,1,0:T(8,128)(2,1)S(1)} async-done(((s16[8,16,768]{2,1,0:T(8,128)(2,1)}), s16[8,16,768]{2,1,0:T(8,128)(2,1)S(1)}, u32[]{:S(2)}, u32[]{:S(2)}) %all-to-all-start) | async-done | bytes 196640 | tf_op jit(solution)/shard_map/cond/branch_0_fun/all_to_all | solution.py:544
  (42 shorter events, 24.3 us)
Async XLA Ops:
  7.2 8.4 %collective-permute-start.10 = (bf16[640,2432]{1,0:T(8,128)(2,1)}, bf16[640,2432]{1,0:T(8,128)(2,1)S(1)}, u32[]{:S(2)}, u32[]{:S(2)}) collective-permute-start(bf16[640,2432]{1,0:T(8,128)(2,1)} %head.1), channel_id=1, source_target_pairs={{0,32},{32,0},{1,33},{33,1},{2,34},{34,2},{3,35},{35,3},{4,36},{36... | collective-permute-start | bytes 9338888 | tf_op jit(solution)/shard_map/ppermute | solution.py:441
  9.2 12.1 %collective-permute-start.11 = (bf16[128,1280]{1,0:T(8,128)(2,1)S(1)}, bf16[128,1280]{1,0:T(8,128)(2,1)S(1)}, u32[]{:S(2)}, u32[]{:S(2)}) collective-permute-start(bf16[128,1280]{1,0:T(8,128)(2,1)S(1)} %get-tuple-element.156), channel_id=1, source_target_pairs={{0,128},{64,192},{128,0},{192,64},{1,129},{65,193},{129,1},{193,65... | collective-permute-start | bytes 983048 | tf_op jit(solution)/shard_map/ppermute | solution.py:453
  12.3 15.6 %collective-permute-start.12 = (bf16[128,1280]{1,0:T(8,128)(2,1)S(1)}, bf16[128,1280]{1,0:T(8,128)(2,1)S(1)}, u32[]{:S(2)}, u32[]{:S(2)}) collective-permute-start(bf16[128,1280]{1,0:T(8,128)(2,1)S(1)} %get-tuple-element.159), channel_id=1, source_target_pairs={{0,64},{64,128},{128,192},{192,0},{1,65},{65,129},{129,193},{193,1... | collective-permute-start | bytes 983048 | tf_op jit(solution)/shard_map/ppermute | solution.py:453
  12.9 15.5 %collective-permute-start.13 = (bf16[128,1280]{1,0:T(8,128)(2,1)S(1)}, bf16[128,1280]{1,0:T(8,128)(2,1)S(1)}, u32[]{:S(2)}, u32[]{:S(2)}) collective-permute-start(bf16[128,1280]{1,0:T(8,128)(2,1)S(1)} %get-tuple-element.160), channel_id=1, source_target_pairs={{0,192},{64,0},{128,64},{192,128},{1,193},{65,1},{129,65},{193,129... | collective-permute-start | bytes 983048 | tf_op jit(solution)/shard_map/ppermute | solution.py:453
  23.3 12.2 %collective-permute-start.14 = (s16[64,2560]{1,0:T(8,128)(2,1)S(1)}, s16[64,2560]{1,0:T(8,128)(2,1)S(1)}, u32[]{:S(2)}, u32[]{:S(2)}) collective-permute-start(s16[64,2560]{1,0:T(8,128)(2,1)S(1)} %get-tuple-element.163), channel_id=1, source_target_pairs={{0,192},{64,0},{128,64},{192,128},{1,193},{65,1},{129,65},{193,129... | collective-permute-start | bytes 983048 | tf_op jit(solution)/shard_map/ppermute | solution.py:472
  26.1 9.8 %collective-permute-start.15 = (s16[64,2560]{1,0:T(8,128)(2,1)S(1)}, s16[64,2560]{1,0:T(8,128)(2,1)S(1)}, u32[]{:S(2)}, u32[]{:S(2)}) collective-permute-start(s16[64,2560]{1,0:T(8,128)(2,1)S(1)} %get-tuple-element.164), channel_id=1, source_target_pairs={{0,64},{64,128},{128,192},{192,0},{1,65},{65,129},{129,193},{193,1... | collective-permute-start | bytes 983048 | tf_op jit(solution)/shard_map/ppermute | solution.py:472
  31.4 20.5 %collective-permute-start.20 = (bf16[512,640]{1,0:T(8,128)(2,1)S(1)}, bf16[512,640]{1,0:T(8,128)(2,1)S(1)}, u32[]{:S(2)}, u32[]{:S(2)}) collective-permute-start(bf16[512,640]{1,0:T(8,128)(2,1)S(1)} %get-tuple-element.170), channel_id=1, source_target_pairs={{0,32},{32,0},{1,33},{33,1},{2,34},{34,2},{3,35},{35,3},{4,36},{36... | collective-permute-start | bytes 1966088 | tf_op jit(solution)/shard_map/ppermute | solution.py:487
  31.5 11.0 %collective-permute-start.17 = (s16[64,2560]{1,0:T(8,128)(2,1)S(1)}, s16[64,2560]{1,0:T(8,128)(2,1)S(1)}, u32[]{:S(2)}, u32[]{:S(2)}) collective-permute-start(s16[64,2560]{1,0:T(8,128)(2,1)S(1)} %get-tuple-element.166), channel_id=1, source_target_pairs={{0,192},{64,0},{128,64},{192,128},{1,193},{65,1},{129,65},{193,129... | collective-permute-start | bytes 983048 | tf_op jit(solution)/shard_map/ppermute | solution.py:483
  33.9 11.8 %collective-permute-start.18 = (s16[64,2560]{1,0:T(8,128)(2,1)S(1)}, s16[64,2560]{1,0:T(8,128)(2,1)S(1)}, u32[]{:S(2)}, u32[]{:S(2)}) collective-permute-start(s16[64,2560]{1,0:T(8,128)(2,1)S(1)} %get-tuple-element.167), channel_id=1, source_target_pairs={{0,64},{64,128},{128,192},{192,0},{1,65},{65,129},{129,193},{193,1... | collective-permute-start | bytes 983048 | tf_op jit(solution)/shard_map/ppermute | solution.py:483
  36.4 12.8 %collective-permute-start.16 = (s16[64,2560]{1,0:T(8,128)(2,1)S(1)}, s16[64,2560]{1,0:T(8,128)(2,1)S(1)}, u32[]{:S(2)}, u32[]{:S(2)}) collective-permute-start(s16[64,2560]{1,0:T(8,128)(2,1)S(1)} %get-tuple-element.165), channel_id=1, source_target_pairs={{0,192},{64,0},{128,64},{192,128},{1,193},{65,1},{129,65},{193,129... | collective-permute-start | bytes 983048 | tf_op jit(solution)/shard_map/ppermute | solution.py:485
  38.2 13.7 %collective-permute-start.19 = (s16[64,2560]{1,0:T(8,128)(2,1)S(1)}, s16[64,2560]{1,0:T(8,128)(2,1)S(1)}, u32[]{:S(2)}, u32[]{:S(2)}) collective-permute-start(s16[64,2560]{1,0:T(8,128)(2,1)S(1)} %get-tuple-element.168), channel_id=1, source_target_pairs={{0,64},{64,128},{128,192},{192,0},{1,65},{65,129},{129,193},{193,1... | collective-permute-start | bytes 983048 | tf_op jit(solution)/shard_map/ppermute | solution.py:485
  51.9 15.8 %copy-start.5 = (s32[128]{0:T(128)S(1)}, s32[128]{0:T(128)}, u32[]{:S(2)}) copy-start(s32[128]{0:T(128)} %param.13) | copy-start | bytes 1540
  51.9 15.8 %copy-start.6 = (f32[128]{0:T(128)S(1)}, f32[128]{0:T(128)}, u32[]{:S(2)}) copy-start(f32[128]{0:T(128)} %param.14) | copy-start | bytes 1540
  51.9 30.4 %copy-start.4 = (s32[128]{0:T(128)S(1)}, s32[128]{0:T(128)}, u32[]{:S(2)}) copy-start(s32[128]{0:T(128)} %param.12) | copy-start | bytes 1540
  83.5 6.9 %collective-permute-start.23 = (bf16[32,2432]{1,0:T(8,128)(2,1)S(1)}, bf16[32,2432]{1,0:T(8,128)(2,1)S(1)}, u32[]{:S(2)}, u32[]{:S(2)}) collective-permute-start(bf16[32,2432]{1,0:T(8,128)(2,1)S(1)} %shard_map.80), channel_id=1, source_target_pairs={{0,192},{64,0},{128,64},{192,128},{1,193},{65,1},{129,65},{193,129... | collective-permute-start | bytes 466952 | tf_op jit(solution)/shard_map/ppermute | solution.py:521
  84.7 8.4 %collective-permute-start.22 = (bf16[32,2432]{1,0:T(8,128)(2,1)S(1)}, bf16[32,2432]{1,0:T(8,128)(2,1)S(1)}, u32[]{:S(2)}, u32[]{:S(2)}) collective-permute-start(bf16[32,2432]{1,0:T(8,128)(2,1)S(1)} %shard_map.80), channel_id=1, source_target_pairs={{0,128},{64,192},{128,0},{192,64},{1,129},{65,193},{129,1},{193,65... | collective-permute-start | bytes 466952 | tf_op jit(solution)/shard_map/ppermute | solution.py:521
  86.2 9.1 %collective-permute-start.21 = (bf16[32,2432]{1,0:T(8,128)(2,1)S(1)}, bf16[32,2432]{1,0:T(8,128)(2,1)S(1)}, u32[]{:S(2)}, u32[]{:S(2)}) collective-permute-start(bf16[32,2432]{1,0:T(8,128)(2,1)S(1)} %shard_map.80), channel_id=1, source_target_pairs={{0,64},{64,128},{128,192},{192,0},{1,65},{65,129},{129,193},{193,1... | collective-permute-start | bytes 466952 | tf_op jit(solution)/shard_map/ppermute | solution.py:521
  95.3 2.1 %collective-permute-start.24 = (bf16[128,2432]{1,0:T(8,128)(2,1)S(1)}, bf16[128,2432]{1,0:T(8,128)(2,1)S(1)}, u32[]{:S(2)}, u32[]{:S(2)}) collective-permute-start(bf16[128,2432]{1,0:T(8,128)(2,1)S(1)} %pad_maximum_fusion.1.mine), channel_id=1, source_target_pairs={{0,32},{32,0},{1,33},{33,1},{2,34},{34,2},{3,35},{35,3},{4,36},{36... | collective-permute-start | bytes 1867784 | tf_op jit(solution)/shard_map/ppermute | solution.py:523
  99.2 10.0 %copy-start.2 = (bf16[512,640]{1,0:T(8,128)(2,1)}, bf16[512,640]{1,0:T(8,128)(2,1)S(1)}, u32[]{:S(2)}) copy-start(bf16[512,640]{1,0:T(8,128)(2,1)S(1)} %get-tuple-element.76.hid_mine) | copy-start | bytes 1966084 | tf_op jit(solution)/shard_map/cond
  99.2 7.5 %collective-permute-start = (bf16[64,640]{1,0:T(8,128)(2,1)S(1)}, bf16[64,640]{1,0:T(8,128)(2,1)S(1)}, u32[]{:S(2)}, u32[]{:S(2)}) collective-permute-start(bf16[64,640]{1,0:T(8,128)(2,1)S(1)} %get-tuple-element.81), channel_id=1, source_target_pairs={{0,8},{8,16},{16,24},{24,0},{1,9},{9,17},{17,25},{25,1},{2,10},{10... | collective-permute-start | bytes 245768 | tf_op jit(solution)/shard_map/cond/branch_0_fun/ppermute | solution.py:533
  99.8 6.9 %collective-permute-start.1 = (bf16[64,640]{1,0:T(8,128)(2,1)S(1)}, bf16[64,640]{1,0:T(8,128)(2,1)S(1)}, u32[]{:S(2)}, u32[]{:S(2)}) collective-permute-start(bf16[64,640]{1,0:T(8,128)(2,1)S(1)} %get-tuple-element.82), channel_id=1, source_target_pairs={{0,16},{8,24},{16,0},{24,8},{1,17},{9,25},{17,1},{25,9},{2,18},{10... | collective-permute-start | bytes 245768 | tf_op jit(solution)/shard_map/cond/branch_0_fun/ppermute | solution.py:533
  101.7 5.6 %collective-permute-start.2 = (bf16[64,640]{1,0:T(8,128)(2,1)S(1)}, bf16[64,640]{1,0:T(8,128)(2,1)S(1)}, u32[]{:S(2)}, u32[]{:S(2)}) collective-permute-start(bf16[64,640]{1,0:T(8,128)(2,1)S(1)} %get-tuple-element.83), channel_id=1, source_target_pairs={{0,24},{8,0},{16,8},{24,16},{1,25},{9,1},{17,9},{25,17},{2,26},{10... | collective-permute-start | bytes 245768 | tf_op jit(solution)/shard_map/cond/branch_0_fun/ppermute | solution.py:533
  109.2 13.2 %all-to-all-start = ((s16[8,16,768]{2,1,0:T(8,128)(2,1)}), s16[8,16,768]{2,1,0:T(8,128)(2,1)S(1)}, u32[]{:S(2)}, u32[]{:S(2)}) async-start(s16[8,16,768]{2,1,0:T(8,128)(2,1)} %bitcast), calls=%async_computation | async-start | bytes 393216 | tf_op jit(solution)/shard_map/cond/branch_0_fun/all_to_all | solution.py:544

commit v8 on v6

--- a/solution.py
+++ b/solution.py
@@ -12,6 +12,8 @@
 LEVELS = 6
 CAP = 16
 CAP_SMALL = 32
+VALID = 112
+LOW = 64
 ORDER = (2, 0, 3, 1)
 NX = 4
 
@@ -115,12 +117,36 @@
 LN2_64 = float(np.log(2.0) / 64.0)
 
 
-def split_kernel(at, hidden, b0, b1, b2, b3):
+def valid_ranks(valid):
+    i = lax.broadcasted_iota(jnp.int32, (128, 128), 0)
+    j = lax.broadcasted_iota(jnp.int32, (128, 128), 1)
+    mask = jnp.broadcast_to(valid[...].astype(f32), (8, 128))
+    rank = jnp.dot(mask, (i < j).astype(f32), preferred_element_type=f32)
+    return jnp.where(mask > 0.0, rank, -1.0)[0:1, :]
+
+
+def split_kernel(at, hidden, valid, b0, b1, b2, b3):
     chip_rows = b0.shape[1]
-    nx = hidden.shape[1] // chip_rows
+    choose = one_hot(b0.shape[0], valid_ranks(valid))
     for s, out in enumerate((b0, b1, b2, b3)):
-        to = lax.rem(at[0] + s, nx) * chip_rows
-        out[...] = hidden[:, pl.ds(pl.multiple_of(to, 128), chip_rows)]
+        to = lax.rem(at[0] + s, NX) * chip_rows
+        block = hidden[:, pl.ds(pl.multiple_of(to, 128), chip_rows)]
+        out[...] = jnp.dot(choose, block, preferred_element_type=f32).astype(bf16)
+
+
+def table_kernel(valid, advantage, ids, after, table):
+    rank = valid_ranks(valid)
+    lane = lax.broadcasted_iota(jnp.int32, (128, 128), 1).astype(f32)
+    place = lax.broadcasted_iota(jnp.int32, (1, 128), 1).astype(f32)
+    mask = valid[...].astype(f32)
+    columns = as_columns([rank, mask, advantage[...], ids[...].astype(f32), place])
+    here = columns[:, 0:1] == lane
+    row = lax.broadcasted_iota(jnp.int32, (8, 128), 0)
+    out = jnp.broadcast_to(jnp.sum(mask, axis=1, keepdims=True), (8, 128))
+    for k, to in ((1, 3), (2, 4), (3, 5), (4, 7)):
+        value = jnp.sum(jnp.where(here, columns[:, k : k + 1], 0.0), axis=0, keepdims=True)
+        out = jnp.where(row == to, value, out)
+    table[...] = out
 
 
 def turn_kernel(tick, head, turned):
@@ -176,7 +202,6 @@
 
 
 def far_kernel(at, block, head, other, low, high, tick, part):
-    tokens = block.shape[0]
     rows, cols = head.shape
     here, there = halves(at, rows)
 
@@ -187,50 +212,52 @@
 
     over_columns(cols, tile)
     tick[...] = jnp.zeros(tick.shape, f32)
-    half = tokens // 2
     pack_rows(part, 0, low)
-    pack_rows(part, half, high)
+    pack_rows(part, LOW, high)
 
 
 def near_kernel(at, tick, b0, b1, b2, b3, head, other, p1, p3, q1, q3, mine, theirs, part):
-    tokens = b0.shape[0]
-    half = tokens // 2
+    count = b0.shape[0]
     rows, cols = head.shape
     here, there = halves(at, rows)
     for k, block in enumerate((b1, b3, b0, b2)):
-        mine[k * tokens : (k + 1) * tokens, :] = block[:, here]
-        theirs[k * tokens : (k + 1) * tokens, :] = block[:, there]
+        start = k * 128
+        for stack, half in ((mine, here), (theirs, there)):
+            stack[start : start + count, :] = block[:, half]
+            stack[start + count : start + 128, :] = jnp.zeros((128 - count, rows), bf16)
 
     def tile(span):
-        both = jnp.dot(mine[0 : 2 * tokens, :], head[:, span], preferred_element_type=f32) + jnp.dot(
-            theirs[0 : 2 * tokens, :], other[:, span], preferred_element_type=f32
-        )
-        p1[:, span] = both[0:half, :]
-        part[:, span] = both[half : tokens + half, :]
-        p3[:, span] = both[tokens + half :, :]
+        both = jnp.dot(mine[0:256, :], head[:, span], preferred_element_type=f32) + jnp.dot(
+            theirs[0:256, :], other[:, span], preferred_element_type=f32
+        )
+        p1[:, span] = both[0:LOW, :]
+        part[:, span] = both[LOW : 128 + LOW, :]
+        p3[:, span] = both[128 + LOW : 128 + count, :]
 
     over_columns(cols, tile)
     pack_rows(part, 0, q1)
-    pack_rows(part, half, q3)
+    pack_rows(part, 128 - LOW, q3)
 
 
 def relay_kernel(p1, p3, low, high, q1, q3, tick):
     step = 16
     tick[...] = jnp.zeros(tick.shape, f32)
-    for start in range(0, p1.shape[0], step):
-        at = slice(start, start + step)
-        pack(p1[at, :] + unpack(low, at), q1, at)
-        pack(p3[at, :] + unpack(high, at), q3, at)
+    for part, came, out in ((p1, low, q1), (p3, high, q3)):
+        for start in range(0, part.shape[0], step):
+            at = slice(start, start + step)
+            pack(part[at, :] + unpack(came, at), out, at)
 
 
 def total_kernel(own, q1_low, q1_high, q3_low, q3_high, turned, theirs, logits, sent, stats):
-    tokens = own.shape[0]
+    count = own.shape[0]
     step = 16
     lane = lax.broadcasted_iota(jnp.int32, (step, 128), 1)
-    for start in range(0, tokens, step):
+    logits[count:, :] = jnp.zeros((128 - count, own.shape[1]), f32)
+    stats[count:, :] = jnp.ones((128 - count, 128), f32)
+    for start in range(0, count, step):
         at = slice(start, start + step)
-        q1, q3 = (q1_low, q3_low) if start < tokens // 2 else (q1_high, q3_high)
-        part = slice(start % (tokens // 2), start % (tokens // 2) + step)
+        q1, q3 = (q1_low, q3_low) if start < LOW else (q1_high, q3_high)
+        part = slice(start % LOW, start % LOW + step)
         value = own[at, :] + unpack(q1, part) + unpack(q3, part)
         logits[at, :] = value
         high = jnp.max(value, axis=1, keepdims=True)
@@ -244,7 +271,7 @@
         sent[i] = rows
 
 
-def merge_kernel(parts, valid, advantage, sent):
+def merge_kernel(parts, table, sent):
     high = parts[0, 0:1, :]
     for i in range(1, parts.shape[0]):
         high = jnp.maximum(high, parts[i, 0:1, :])
@@ -252,13 +279,12 @@
     for i in range(parts.shape[0]):
         sums = sums + jnp.exp(parts[i, 0:1, :] - high) * parts[i]
     row = lax.broadcasted_iota(jnp.int32, (8, 128), 0)
-    out = jnp.where(row == 0, high, sums)
-    out = jnp.where(row == 3, valid[...].astype(f32), jnp.where(row == 4, advantage[...], out))
+    out = jnp.where(row == 0, high, jnp.where(row < 3, sums, table[...]))
     for i in range(sent.shape[0]):
         sent[i] = out
 
 
-def plan_kernel(start_high, parts, coef_out, normal_out, packed_out, slot_out, flag, rows):
+def plan_kernel(start_high, parts, coef_out, normal_out, packed_out, slot_out, place_out, flag, rows):
     owners = 8
     ny = parts.shape[0] // owners
     for o in range(owners):
@@ -272,8 +298,8 @@
         normal = high + jnp.log(sums[1:2, :])
         entropy = normal - sums[2:3, :] / sums[1:2, :]
         rows[o] = jnp.where(row == 0, normal, jnp.where(row == 1, entropy, parts[o * ny]))
-    normal, entropy, valid, advantage = (
-        jnp.concatenate([rows[o, k : k + 1, :] for o in range(owners)], axis=0) for k in (0, 1, 3, 4)
+    normal, entropy, valid, advantage, held, place = (
+        jnp.concatenate([rows[o, k : k + 1, :] for o in range(owners)], axis=0) for k in (0, 1, 3, 4, 6, 7)
     )
     counted = jnp.sum(jnp.sum(valid, axis=1, keepdims=True), axis=0, keepdims=True)
     threshold = bisect(jnp.where(valid > 0.0, entropy, -jnp.inf), counted, start_high)
@@ -284,17 +310,23 @@
     i = lax.broadcasted_iota(jnp.int32, (128, 128), 0)
     j = lax.broadcasted_iota(jnp.int32, (128, 128), 1)
     ahead = (i < j).astype(f32)
+    rank_owner = jnp.dot(activef, ahead, preferred_element_type=f32)
     group = 128 // (32 // owners)
-    same = (i // group == j // group).astype(f32)
-    rank_owner = jnp.dot(activef, ahead, preferred_element_type=f32)
-    rank_group = jnp.dot(activef, ahead * same, preferred_element_type=f32)
-    start = (lax.broadcasted_iota(jnp.int32, (8, 128), 1) // group * CAP).astype(f32)
+    start = jnp.zeros((8, 1), f32)
+    slot = jnp.full((8, 128), -1.0, f32)
+    over = jnp.where(active & (rank_owner >= CAP_SMALL), 1.0, 0.0)
+    for g in range(128 // group):
+        member = active & (place >= float(g * group)) & (place < float((g + 1) * group))
+        rank_group = rank_owner - start
+        slot = jnp.where(member, rank_group + float(g * CAP), slot)
+        over = jnp.where(member & (rank_group >= CAP), 2.0, over)
+        start = start + jnp.sum(jnp.where(member, 1.0, 0.0), axis=1, keepdims=True)
+    over = jnp.where(held > float(VALID), 2.0, over)
     coef_out[...] = coef
     normal_out[...] = normal
     packed_out[...] = jnp.where(active, rank_owner, -1.0)
-    slot_out[...] = jnp.where(active, rank_group + start, -1.0)
-    over = jnp.where(active & (rank_owner >= CAP_SMALL), 1.0, 0.0)
-    over = jnp.where(active & (rank_group >= CAP), 2.0, over)
+    slot_out[...] = slot
+    place_out[...] = place
     flag[0, 0] = jnp.max(over).astype(jnp.int32)
 
 
@@ -311,10 +343,10 @@
     return (row == slots).astype(f32).astype(bf16)
 
 
-def slopes_kernel(at, logits, coef_all, normal_all, packed_all, ids, out):
+def slopes_kernel(at, logits, coef_all, normal_all, packed_all, table, out):
     me = pl.ds(at[2], 1)
     count = out.shape[0]
-    columns = as_columns([coef_all[me, :], normal_all[me, :], ids[...].astype(f32)])
+    columns = as_columns([coef_all[me, :], normal_all[me, :], table[5:6, :]])
     coef, normal, token = columns[:, 0:1], columns[:, 1:2], columns[:, 2:3].astype(jnp.int32) - at[3]
     choose = one_hot(count, packed_all[me, :])
     lane = lax.broadcasted_iota(jnp.int32, (128, 128), 1)
@@ -403,22 +435,24 @@
         )
         spread.append(part.astype(bf16))
     spread = jnp.concatenate(spread, axis=1)
-    total = jnp.zeros(out.shape, f32)
+    total = jnp.zeros((size, r0.shape[1]), f32)
     for r in (r0, r1, r2, r3):
         total = total + jnp.dot(spread, r[...], preferred_element_type=f32)
-    out[...] = total
-
-
-def sum_kernel(at, parts, slot_all, out, ranks):
-    total = parts[0:CAP, :]
+    pack(total, out, slice(0, size))
+
+
+def sum_kernel(at, parts, slot_all, place_all, out):
+    total = unpack(parts, slice(0, CAP))
     for i in range(1, parts.shape[0] // CAP):
-        total = total + parts[i * CAP : (i + 1) * CAP, :]
+        total = total + unpack(parts, slice(i * CAP, (i + 1) * CAP))
     group = out.shape[0]
     per_owner = 128 // group
-    owner, place = at[4] // per_owner, lax.rem(at[4], per_owner)
-    ranks[...] = as_columns([slot_all[pl.ds(owner, 1), :]])
-    rank = ranks[pl.ds(pl.multiple_of(place * group, group), group), :][:, 0:1]
-    rank = rank - (place * CAP).astype(f32)
+    me, block = pl.ds(at[4] // per_owner, 1), lax.rem(at[4], per_owner)
+    slot, place = slot_all[me, :], place_all[me, :]
+    token = lax.broadcasted_iota(jnp.int32, (group, 128), 0) + block * group
+    here = (place == token.astype(f32)) & (slot >= 0.0)
+    rank = jnp.sum(jnp.where(here, slot + 1.0, 0.0), axis=1, keepdims=True)
+    rank = rank - 1.0 - (block * CAP).astype(f32)
     rows = jnp.zeros(out.shape, f32)
     for r in range(CAP):
         rows = rows + jnp.where(rank == float(r), total[r : r + 1, :], 0.0)
@@ -435,10 +469,11 @@
 
     head_other = lax.ppermute(head, "c", SWAP)
 
-    block_shape = struct((tokens, chip_rows), bf16)
-    b0, *leave = call(split_kernel, [block_shape] * 4, [at, hidden_states], smem=1)
+    valid_row, advantage_row, id_row = (v.reshape(1, tokens) for v in (valid, advantage, token_ids))
+    block_shape = struct((VALID, chip_rows), bf16)
+    b0, *leave = call(split_kernel, [block_shape] * 4, [at, hidden_states, valid_row], smem=1)
     came = {s: lax.ppermute(leave[s - 1], "x", ring(nx, s)) for s in (2, 1, 3)}
-    partial = struct((tokens, voc_cols), f32)
+    partial = struct((VALID, voc_cols), f32)
     tick_shape = struct((8, 128), f32)
     own, kept = call(
         own_kernel,
@@ -447,20 +482,22 @@
         smem=1,
         cost_estimate=estimate(tokens, chip_rows, voc_cols),
     )
-    half = struct((tokens // 2, voc_cols + 128), jnp.int16)
+    table = call(table_kernel, tick_shape, [valid_row, advantage_row, id_row, own], loose=1)
+    first = struct((LOW, voc_cols + 128), jnp.int16)
+    second = struct((VALID - LOW, voc_cols + 128), jnp.int16)
     low, high, tick = call(
         far_kernel,
-        [half, half, tick_shape],
+        [first, second, tick_shape],
         [at, came[2], kept, head_other],
-        [pltpu.VMEM((tokens, voc_cols), f32)],
+        [pltpu.VMEM((VALID, voc_cols), f32)],
         smem=1,
         cost_estimate=estimate(tokens, chip_rows, voc_cols),
     )
     low, high = lax.ppermute(low, "x", ring(nx, -1)), lax.ppermute(high, "x", ring(nx, 1))
-    half_partial = struct((tokens // 2, voc_cols), f32)
+    relayed = [struct((n, voc_cols), f32) for n in (LOW, VALID - LOW)]
     p1, p3, q1_high, q3_low, hid_mine, hid_send = call(
         near_kernel,
-        [half_partial] * 2 + [half] * 2 + [struct((nx * tokens, rows), bf16)] * 2,
+        relayed + [second, first] + [struct((nx * tokens, rows), bf16)] * 2,
         [at, tick, b0, came[1], came[2], came[3], kept, head_other],
         [pltpu.VMEM((tokens, voc_cols), f32)],
         vmem=24,
@@ -468,13 +505,13 @@
         cost_estimate=estimate(2 * tokens, chip_rows, voc_cols),
     )
     q1_high, q3_low = lax.ppermute(q1_high, "x", ring(nx, -1)), lax.ppermute(q3_low, "x", ring(nx, 1))
-    q1_low, q3_high, tick = call(relay_kernel, [half] * 2 + [tick_shape], [p1, p3, low, high])
+    q1_low, q3_high, tick = call(relay_kernel, [first, second, tick_shape], [p1, p3, low, high])
     q1_low, q3_high = lax.ppermute(q1_low, "x", ring(nx, -1)), lax.ppermute(q3_high, "x", ring(nx, 1))
     turned = call(turn_kernel, struct((voc_cols, rows), bf16), [tick, kept])
     hid_theirs = lax.ppermute(hid_send, "c", SWAP)
     logits, stats = call(
         total_kernel,
-        [partial, struct((lax.axis_size("z"), 8, 128), f32)],
+        [struct((tokens, voc_cols), f32), struct((lax.axis_size("z"), 8, 128), f32)],
         [own, q1_low, q1_high, q3_low, q3_high, turned, hid_theirs],
         [pltpu.VMEM((tokens, 128), f32)],
         loose=2,
@@ -485,24 +522,24 @@
     stats = call(
         merge_kernel,
         struct((lax.axis_size(everyone), 8, 128), f32),
-        [stats, valid.reshape(1, tokens), advantage.reshape(1, tokens)],
+        [stats, table],
     )
     stats = lax.all_to_all(stats, everyone, 0, 0, tiled=True)
     start_high = float(np.float32(np.log(np.float32(voc_cols * n_voc))) + np.float32(1.0))
-    table = struct((n_dp, tokens), f32)
-    coef_all, normal_all, packed_all, slot_all, flag = call(
+    everyones = struct((n_dp, tokens), f32)
+    coef_all, normal_all, packed_all, slot_all, place_all, flag = call(
         functools.partial(plan_kernel, start_high),
-        [table] * 4 + [struct((1, 1), jnp.int32)],
+        [everyones] * 5 + [struct((1, 1), jnp.int32)],
         [stats],
         [pltpu.VMEM((n_dp, 8, 128), f32)],
-        out_specs=[pl.BlockSpec(memory_space=pltpu.VMEM)] * 4 + [pl.BlockSpec(memory_space=pltpu.SMEM)],
+        out_specs=[pl.BlockSpec(memory_space=pltpu.VMEM)] * 5 + [pl.BlockSpec(memory_space=pltpu.SMEM)],
     )
 
     def backward(cap):
         piece = call(
             slopes_kernel,
             struct((cap, voc_cols), bf16),
-            [at, logits, coef_all, normal_all, packed_all, token_ids.reshape(1, tokens)],
+            [at, logits, coef_all, normal_all, packed_all, table],
             smem=1,
         )
         pieces = {s: lax.ppermute(piece, "x", ring(nx, s)) for s in (2, 1, 3)}
@@ -524,7 +561,7 @@
         head_grad, tick = outer(*sides, 0, early, packed_all, packed_all)
         spread, tick = call(
             spread_kernel,
-            [struct((n_voc * CAP // nx, rows), f32), tick_shape],
+            [struct((n_voc * CAP // nx, rows + 128), jnp.int16), tick_shape],
             [at, tick, *parts, packed_all, slot_all],
             smem=1,
         )
@@ -533,8 +570,7 @@
         hidden_grad = call(
             sum_kernel,
             struct((tokens * n_dp // n_voc, rows), f32),
-            [at, spread, slot_all],
-            [pltpu.VMEM((tokens, 8), f32)],
+            [at, spread, slot_all, place_all],
             smem=1,
         )
         return hidden_grad, head_grad

time: 135 us -> 140 us (1.037)
  blocking collectives: 27.4 us -> 14.2 us
  starting transfers between devices: 25.2 us -> 34.1 us
  Pallas kernels: 26.7 us -> 31.3 us
  waiting for transfers between devices: 38.7 us -> 42 us
    all_to_all x1 -> x0, blocking collectives: 14.9 us -> none  [shards(): stats = lax.all_to_all(stats, 'z', 0, 0, tiled=True)]
    all_to_all x0 -> x1, starting transfers between devices: none -> 8.56 us  [shards(): stats = lax.all_to_all(stats, 'z', 0, 0, tiled=True)]
    ppermute x1, waiting for transfers between devices: 0.49 us -> 8 us  [shards(): lax.ppermute(high, 'x', ring(nx, 1))]
    ppermute x1, waiting for transfers between devices: 3 us -> 10.2 us  [shards(): lax.ppermute(q1_high, 'x', ring(nx, -1))]
    all_to_all x0 -> x1, waiting for transfers between devices: none -> 4.89 us  [shards(): stats = lax.all_to_all(stats, 'z', 0, 0, tiled=True)]
    ppermute x1, waiting for transfers between devices: 3.45 us -> 0.01 us  [shards(): lax.ppermute(q1_low, 'x', ring(nx, -1))]
    pallas_call x13 -> x14, Pallas kernels: 19.9 us -> 23.2 us  [call(): pl.pallas_call(kernel, in_specs=specs, out_shape=out, scratch_shapes=list...]
    ppermute x1, waiting for transfers between devices: 3.17 us -> 0.01 us  [shards(): lax.ppermute(q3_low, 'x', ring(nx, 1))]
  transfers between devices with their start and end apart: 19 -> 20, of which waited for: 16 -> 11; matrix products, arithmetic and copies ran while one was open for 0% -> 0% of each run, Pallas kernels for 13% -> 15%
where the time goes in v8:
time: 140 us; the launch traced here: 138 us
  waiting for transfers between devices  42 us (30%)
  starting transfers between devices  34.1 us (24%)
  Pallas kernels  31.3 us (22%)
  between operations  14.8 us (11%)
  blocking collectives  14.2 us (10%)
    pallas_call x14, Pallas kernels, call(): pl.pallas_call(kernel, in_specs=specs, out_shape=out, scratch_shapes=list...  23.2 us
    all_to_all x1, blocking collectives, shards(): stats = lax.all_to_all(stats, everyone, 0, 0, tiled=True)  14.2 us
    ppermute x1, waiting for transfers between devices, shards(): lax.ppermute(q1_high, 'x', ring(nx, -1))  10.2 us
    ppermute x3, waiting for transfers between devices, backward(): pieces = {s: lax.ppermute(piece, 'x', ring(nx, s)) for s in (2, 1, 3)}  9.02 us
    all_to_all x1, starting transfers between devices, shards(): stats = lax.all_to_all(stats, 'z', 0, 0, tiled=True)  8.56 us
    pallas_call x2, Pallas kernels, outer(): pl.pallas_call(outer_kernel, grid=(count,), in_specs=in_specs, out_specs=...  8.11 us
    ppermute x1, waiting for transfers between devices, shards(): lax.ppermute(high, 'x', ring(nx, 1))  8 us
    ppermute x3, starting transfers between devices, shards(): came = {s: lax.ppermute(leave[s - 1], 'x', ring(nx, s)) for s in (2, 1, 3)}  6.35 us
  transfers between devices with their start and end apart: 20, of which 11 were waited for; matrix products, arithmetic and copies ran while one was open for 0% of the time, Pallas kernels for 15%

profile of v8, /device:TPU:32, one launch (start us, length us, event | category | flops | bytes accessed | tf_op | source)
XLA Modules:
  0.0 138.0 jit_solution(14445283790534965076)
XLA Ops:
  7.4 1.9 %shard_map.71 = (bf16[112,1280]{1,0:T(8,128)(2,1)S(1)}, bf16[112,1280]{1,0:T(8,128)(2,1)S(1)}, bf16[112,1280]{1,0:T(8,128)(2,1)S(1)}, bf16[112,1280]{1,0:T(8,128)(2,1)S(1)}) custom-call(s32[6]{0:T(128)S(1)} %stack.27.at, bf16[128,5120]{1,0:T(8,128)(2,1)} %hidden.1, s32[1,128]{1,0:T(1,128)} %bitcast.31), custom_call_target="tpu_custom_call" | custom-call | tf_op jit(solution)/shard_map/pallas_call | solution.py:99
  9.3 3.1 %collective-permute-start.11 = (bf16[112,1280]{1,0:T(8,128)(2,1)S(1)}, bf16[112,1280]{1,0:T(8,128)(2,1)S(1)}, u32[]{:S(2)}, u32[]{:S(2)}) collective-permute-start(bf16[112,1280]{1,0:T(8,128)(2,1)S(1)} %get-tuple-element.163), channel_id=1, source_target_pairs={{0,128},{64,192},{128,0},{192,64},{1,129},{65,193},{129,1},{193,65... | collective-permute-start | bytes 860168 | tf_op jit(solution)/shard_map/ppermute | solution.py:475
  13.0 2.6 %collective-permute-start.13 = (bf16[112,1280]{1,0:T(8,128)(2,1)S(1)}, bf16[112,1280]{1,0:T(8,128)(2,1)S(1)}, u32[]{:S(2)}, u32[]{:S(2)}) collective-permute-start(bf16[112,1280]{1,0:T(8,128)(2,1)S(1)} %get-tuple-element.167), channel_id=1, source_target_pairs={{0,192},{64,0},{128,64},{192,128},{1,193},{65,1},{129,65},{193,129... | collective-permute-start | bytes 860168 | tf_op jit(solution)/shard_map/ppermute | solution.py:475
  15.6 3.3 %shard_map.72 = (f32[112,2432]{1,0:T(8,128)S(1)}, bf16[640,2432]{1,0:T(8,128)(2,1)S(1)}) custom-call(s32[6]{0:T(128)S(1)} %stack.27.at, bf16[112,1280]{1,0:T(8,128)(2,1)S(1)} %get-tuple-element.161.block.b0, bf16[640,2432]{1,0:T(8,128)(2,1)} %head.1, bf16[640,2432]{1,0:T(8,128)(2,1)S(1)} %collective-permute-done.10.other), custom_call_target="tpu_custom_call" | custom-call | flops 796917760 | bytes 6225920 | tf_op jit(solution)/shard_map/pallas_call | solution.py:99
  20.5 1.9 %shard_map.73 = (s16[64,2560]{1,0:T(8,128)(2,1)S(1)}, s16[48,2560]{1,0:T(8,128)(2,1)S(1)}, f32[8,128]{1,0:T(8,128)S(1)}) custom-call(s32[6]{0:T(128)S(1)} %stack.27.at, bf16[112,1280]{1,0:T(8,128)(2,1)S(1)} %collective-permute-done.11.block.b2, bf16[640,2432]{1,0:T(8,128)(2,1)S(1)} %get-tuple-element.164.head, ...), custom_call_target="tpu_custom_call" | custom-call | flops 796917760 | bytes 6225920 | tf_op jit(solution)/shard_map/pallas_call | solution.py:99
  22.4 2.8 %collective-permute-start.14 = (s16[64,2560]{1,0:T(8,128)(2,1)S(1)}, s16[64,2560]{1,0:T(8,128)(2,1)S(1)}, u32[]{:S(2)}, u32[]{:S(2)}) collective-permute-start(s16[64,2560]{1,0:T(8,128)(2,1)S(1)} %get-tuple-element.170), channel_id=1, source_target_pairs={{0,192},{64,0},{128,64},{192,128},{1,193},{65,1},{129,65},{193,129... | collective-permute-start | bytes 983048 | tf_op jit(solution)/shard_map/ppermute | solution.py:496
  26.8 3.8 %shard_map.74 = (f32[64,2432]{1,0:T(8,128)S(1)}, f32[48,2432]{1,0:T(8,128)S(1)}, s16[48,2560]{1,0:T(8,128)(2,1)S(1)}, s16[64,2560]{1,0:T(8,128)(2,1)S(1)}, bf16[...) custom-call(s32[6]{0:T(128)S(1)} %stack.27.at, f32[8,128]{1,0:T(8,128)S(1)} %get-tuple-element.165.tick, ...), custom_call_target="tpu_custom_call" | custom-call | flops 1593835520 | bytes 6225920 | tf_op jit(solution)/shard_map/pallas_call | solution.py:99
  32.5 8.0 %collective-permute-done.15.high = s16[48,2560]{1,0:T(8,128)(2,1)S(1)} collective-permute-done((s16[48,2560]{1,0:T(8,128)(2,1)S(1)}, s16[48,2560]{1,0:T(8,128)(2,1)S(1)}, u32[]{:S(2)}, u32[]{:S(2)}) %collective-permute-start.15) | collective-permute-done | bytes 245792 | tf_op jit(solution)/shard_map/ppermute | solution.py:496
  45.0 10.2 %collective-permute-done.17.q1_high = s16[48,2560]{1,0:T(8,128)(2,1)S(1)} collective-permute-done((s16[48,2560]{1,0:T(8,128)(2,1)S(1)}, s16[48,2560]{1,0:T(8,128)(2,1)S(1)}, u32[]{:S(2)}, u32[]{:S(2)}) %collective-permute-start.17) | collective-permute-done | bytes 245792 | tf_op jit(solution)/shard_map/ppermute | solution.py:507
  56.9 8.6 %all-to-all-start.3 = ((f32[8,8,128]{2,1,0:T(8,128)}), f32[8,8,128]{2,1,0:T(8,128)S(1)}, u32[]{:S(2)}, u32[]{:S(2)}) async-start(f32[8,8,128]{2,1,0:T(8,128)} %get-tuple-element.178), calls=%async_computation.5 | async-start | bytes 65536 | tf_op jit(solution)/shard_map/all_to_all | solution.py:520
  67.2 4.9 %all-to-all-done.3.parts = f32[8,8,128]{2,1,0:T(8,128)S(1)} async-done(((f32[8,8,128]{2,1,0:T(8,128)}), f32[8,8,128]{2,1,0:T(8,128)S(1)}, u32[]{:S(2)}, u32[]{:S(2)}) %all-to-all-start.3) | async-done | bytes 32800 | tf_op jit(solution)/shard_map/all_to_all | solution.py:520
  72.1 14.2 %all_to_all.42.parts = f32[32,8,128]{2,1,0:T(8,128)S(1)} all-to-all(f32[32,8,128]{2,1,0:T(8,128)S(1)} %shard_map.79), channel_id=1, replica_groups=mesh['x'=4,'c'=2,'y'=4,'z'=8] {'x','c','y'}, dimensions={0} | all-to-all | bytes 262144 | tf_op jit(solution)/shard_map/all_to_all | solution.py:527
  86.4 2.1 %shard_map.80 = (f32[8,128]{1,0:T(8,128)S(1)}, f32[8,128]{1,0:T(8,128)S(1)}, f32[8,128]{1,0:T(8,128)S(1)}, f32[8,128]{1,0:T(8,128)S(1)}, f32[8,128]{1,0:T(8,128)S(1)}, /*index=5*/s32[1,1]{1,0:T(1,128)}) custom-call(f32[32,8,128]{2,1,0:T(8,128)S(1)} %all_to_all.42.parts), custom_call_target="tpu_custom_call" | custom-call | tf_op jit(solution)/shard_map/pallas_call | solution.py:99
  88.4 1.9 %shard_map.81 = bf16[32,2432]{1,0:T(8,128)(2,1)S(1)} custom-call(s32[6]{0:T(128)S(1)} %stack.27.at, f32[128,2432]{1,0:T(8,128)} %get-tuple-element.182.logits, f32[8,128]{1,0:T(8,128)S(1)} %get-tuple-element.183.coef_all, f32[8,128]{1,0:T(8,128)S(1)} %get-tuple-element.184.normal_all, f32[8,128]{1,0:T(8,128)S(1)} %get-tuple-element.180.packed_all, ...), custom_call_target="tpu_custom_call" | custom-call | tf_op jit(solution)/shard_map/pallas_call | solution.py:99
  93.1 4.2 %collective-permute-done.23 = bf16[32,2432]{1,0:T(8,128)(2,1)S(1)} collective-permute-done((bf16[32,2432]{1,0:T(8,128)(2,1)S(1)}, bf16[32,2432]{1,0:T(8,128)(2,1)S(1)}, u32[]{:S(2)}, u32[]{:S(2)}) %collective-permute-start.23) | collective-permute-done | bytes 155680 | tf_op jit(solution)/shard_map/ppermute | solution.py:545
  97.3 2.6 %collective-permute-done.22 = bf16[32,2432]{1,0:T(8,128)(2,1)S(1)} collective-permute-done((bf16[32,2432]{1,0:T(8,128)(2,1)S(1)}, bf16[32,2432]{1,0:T(8,128)(2,1)S(1)}, u32[]{:S(2)}, u32[]{:S(2)}) %collective-permute-start.22) | collective-permute-done | bytes 155680 | tf_op jit(solution)/shard_map/ppermute | solution.py:545
  100.0 2.2 %collective-permute-done.21 = bf16[32,2432]{1,0:T(8,128)(2,1)S(1)} collective-permute-done((bf16[32,2432]{1,0:T(8,128)(2,1)S(1)}, bf16[32,2432]{1,0:T(8,128)(2,1)S(1)}, u32[]{:S(2)}, u32[]{:S(2)}) %collective-permute-start.21) | collective-permute-done | bytes 155680 | tf_op jit(solution)/shard_map/ppermute | solution.py:545
  106.1 25.1 %conditional.1 = (f32[32,640]{1,0:T(8,128)}, f32[640,2432]{1,0:T(8,128)}) conditional(s32[]{:T(128)} %bitcast.17, (s32[6]{0:T(128)S(1)}, f32[8,128]{1,0:T(8,128)S(1)}, bf16[512,640]{1,0:T(8,128)(2,1)}, bf16[512,640]{1,0:T(8,128)(2,1)}, bf16[256,2432]{1,0:T(8,128)(2,1)S(1)}, /*index=5*/bf16[64,640]{1,0:T(8,128)(2,1)S(1)}, ...), branch_computations={%region_0.0_spmd, %region_1.0_spmd, %region_2.17_spmd} | conditional | flops 9566442496 | bytes 125846592 | solution.py:589
  106.7 1.9 %collective-permute-start.1 = (bf16[64,640]{1,0:T(8,128)(2,1)S(1)}, bf16[64,640]{1,0:T(8,128)(2,1)S(1)}, u32[]{:S(2)}, u32[]{:S(2)}) collective-permute-start(bf16[64,640]{1,0:T(8,128)(2,1)S(1)} %get-tuple-element.86), channel_id=1, source_target_pairs={{0,16},{8,24},{16,0},{24,8},{1,17},{9,25},{17,1},{25,9},{2,18},{10... | collective-permute-start | bytes 245768 | tf_op jit(solution)/shard_map/cond/branch_0_fun/ppermute | solution.py:557
  109.6 4.6 %branch_0_fun.4 = (f32[640,2432]{1,0:T(8,128)}, f32[8,128]{1,0:T(8,128)S(1)}) custom-call(s32[6]{0:T(128)S(1)} %get-tuple-element.78.at, f32[8,128]{1,0:T(8,128)S(1)} %get-tuple-element.79.packed_all.above.after, bf16[512,640]{1,0:T(8,128)(2,1)} %get-tuple-element.80.hid_mine, bf16[512,640]{1,0:T(8,128)(2,1)} %get-tuple-element.81.hid_theirs, ...), custom_call_target="tpu_custom_call" | custom-call | flops 478150656 | bytes 1245184 | tf_op jit(solution)/shard_map/cond/branch_0_fun/pallas_call | solution.py:407
  114.2 1.8 %branch_0_fun.5 = (s16[128,768]{1,0:T(8,128)(2,1)}, f32[8,128]{1,0:T(8,128)S(1)}) custom-call(s32[6]{0:T(128)S(1)} %get-tuple-element.78.at, f32[8,128]{1,0:T(8,128)S(1)} %get-tuple-element.83.before, bf16[64,640]{1,0:T(8,128)(2,1)S(1)} %get-tuple-element.84.r0, bf16[64,640]{1,0:T(8,128)(2,1)S(1)} %collective-permute-done.r1, ...), custom_call_target="tpu_custom_call" | custom-call | tf_op jit(solution)/shard_map/cond/branch_0_fun/pallas_call | solution.py:99
  116.1 4.8 %all-to-all-start = ((s16[8,16,768]{2,1,0:T(8,128)(2,1)}), s16[8,16,768]{2,1,0:T(8,128)(2,1)S(1)}, u32[]{:S(2)}, u32[]{:S(2)}) async-start(s16[8,16,768]{2,1,0:T(8,128)(2,1)} %bitcast), calls=%async_computation | async-start | bytes 393216 | tf_op jit(solution)/shard_map/cond/branch_0_fun/all_to_all | solution.py:568
  120.8 3.5 %branch_0_fun.7 = (f32[640,2432]{1,0:T(8,128)}, f32[8,128]{1,0:T(8,128)}) custom-call(s32[6]{0:T(128)S(1)} %get-tuple-element.78.at, f32[8,128]{1,0:T(8,128)S(1)} %get-tuple-element.79.packed_all.above.after, bf16[512,640]{1,0:T(8,128)(2,1)S(1)} %copy-done.7, bf16[512,640]{1,0:T(8,128)(2,1)S(1)} %copy-done.4, ...), custom_call_target="tpu_custom_call", output_to_operand_aliasing={{0}: (5, {})} | custom-call | flops 318767104 | bytes 1245184 | tf_op jit(solution)/shard_map/cond/branch_0_fun/pallas_call | solution.py:407
  124.4 5.4 %all-to-all-done = s16[8,16,768]{2,1,0:T(8,128)(2,1)S(1)} async-done(((s16[8,16,768]{2,1,0:T(8,128)(2,1)}), s16[8,16,768]{2,1,0:T(8,128)(2,1)S(1)}, u32[]{:S(2)}, u32[]{:S(2)}) %all-to-all-start) | async-done | bytes 196640 | tf_op jit(solution)/shard_map/cond/branch_0_fun/all_to_all | solution.py:568
  (54 shorter events, 22.7 us)
Async XLA Ops:
  7.2 8.5 %collective-permute-start.10 = (bf16[640,2432]{1,0:T(8,128)(2,1)}, bf16[640,2432]{1,0:T(8,128)(2,1)S(1)}, u32[]{:S(2)}, u32[]{:S(2)}) collective-permute-start(bf16[640,2432]{1,0:T(8,128)(2,1)} %head.1), channel_id=1, source_target_pairs={{0,32},{32,0},{1,33},{33,1},{2,34},{34,2},{3,35},{35,3},{4,36},{36... | collective-permute-start | bytes 9338888 | tf_op jit(solution)/shard_map/ppermute | solution.py:470
  9.3 11.3 %collective-permute-start.11 = (bf16[112,1280]{1,0:T(8,128)(2,1)S(1)}, bf16[112,1280]{1,0:T(8,128)(2,1)S(1)}, u32[]{:S(2)}, u32[]{:S(2)}) collective-permute-start(bf16[112,1280]{1,0:T(8,128)(2,1)S(1)} %get-tuple-element.163), channel_id=1, source_target_pairs={{0,128},{64,192},{128,0},{192,64},{1,129},{65,193},{129,1},{193,65... | collective-permute-start | bytes 860168 | tf_op jit(solution)/shard_map/ppermute | solution.py:475
  12.4 13.8 %collective-permute-start.12 = (bf16[112,1280]{1,0:T(8,128)(2,1)S(1)}, bf16[112,1280]{1,0:T(8,128)(2,1)S(1)}, u32[]{:S(2)}, u32[]{:S(2)}) collective-permute-start(bf16[112,1280]{1,0:T(8,128)(2,1)S(1)} %get-tuple-element.166), channel_id=1, source_target_pairs={{0,64},{64,128},{128,192},{192,0},{1,65},{65,129},{129,193},{193,1... | collective-permute-start | bytes 860168 | tf_op jit(solution)/shard_map/ppermute | solution.py:475
  13.0 13.8 %collective-permute-start.13 = (bf16[112,1280]{1,0:T(8,128)(2,1)S(1)}, bf16[112,1280]{1,0:T(8,128)(2,1)S(1)}, u32[]{:S(2)}, u32[]{:S(2)}) collective-permute-start(bf16[112,1280]{1,0:T(8,128)(2,1)S(1)} %get-tuple-element.167), channel_id=1, source_target_pairs={{0,192},{64,0},{128,64},{192,128},{1,193},{65,1},{129,65},{193,129... | collective-permute-start | bytes 860168 | tf_op jit(solution)/shard_map/ppermute | solution.py:475
  18.9 36.3 %copy-start = (f32[112,2432]{1,0:T(8,128)}, f32[112,2432]{1,0:T(8,128)S(1)}, u32[]{:S(2)}) copy-start(f32[112,2432]{1,0:T(8,128)S(1)} %get-tuple-element.162.own.after) | copy-start | bytes 3268612
  22.4 18.1 %collective-permute-start.14 = (s16[64,2560]{1,0:T(8,128)(2,1)S(1)}, s16[64,2560]{1,0:T(8,128)(2,1)S(1)}, u32[]{:S(2)}, u32[]{:S(2)}) collective-permute-start(s16[64,2560]{1,0:T(8,128)(2,1)S(1)} %get-tuple-element.170), channel_id=1, source_target_pairs={{0,192},{64,0},{128,64},{192,128},{1,193},{65,1},{129,65},{193,129... | collective-permute-start | bytes 983048 | tf_op jit(solution)/shard_map/ppermute | solution.py:496
  30.6 24.7 %collective-permute-start.20 = (bf16[512,640]{1,0:T(8,128)(2,1)S(1)}, bf16[512,640]{1,0:T(8,128)(2,1)S(1)}, u32[]{:S(2)}, u32[]{:S(2)}) collective-permute-start(bf16[512,640]{1,0:T(8,128)(2,1)S(1)} %get-tuple-element.177), channel_id=1, source_target_pairs={{0,32},{32,0},{1,33},{33,1},{2,34},{34,2},{3,35},{35,3},{4,36},{36... | collective-permute-start | bytes 1966088 | tf_op jit(solution)/shard_map/ppermute | solution.py:511
  30.6 10.0 %collective-permute-start.15 = (s16[48,2560]{1,0:T(8,128)(2,1)S(1)}, s16[48,2560]{1,0:T(8,128)(2,1)S(1)}, u32[]{:S(2)}, u32[]{:S(2)}) collective-permute-start(s16[48,2560]{1,0:T(8,128)(2,1)S(1)} %get-tuple-element.171), channel_id=1, source_target_pairs={{0,64},{64,128},{128,192},{192,0},{1,65},{65,129},{129,193},{193,1... | collective-permute-start | bytes 737288 | tf_op jit(solution)/shard_map/ppermute | solution.py:496
  31.6 23.6 %collective-permute-start.18 = (s16[64,2560]{1,0:T(8,128)(2,1)S(1)}, s16[64,2560]{1,0:T(8,128)(2,1)S(1)}, u32[]{:S(2)}, u32[]{:S(2)}) collective-permute-start(s16[64,2560]{1,0:T(8,128)(2,1)S(1)} %get-tuple-element.174), channel_id=1, source_target_pairs={{0,64},{64,128},{128,192},{192,0},{1,65},{65,129},{129,193},{193,1... | collective-permute-start | bytes 983048 | tf_op jit(solution)/shard_map/ppermute | solution.py:507
  40.9 14.3 %collective-permute-start.16 = (s16[64,2560]{1,0:T(8,128)(2,1)S(1)}, s16[64,2560]{1,0:T(8,128)(2,1)S(1)}, u32[]{:S(2)}, u32[]{:S(2)}) collective-permute-start(s16[64,2560]{1,0:T(8,128)(2,1)S(1)} %get-tuple-element.172), channel_id=1, source_target_pairs={{0,192},{64,0},{128,64},{192,128},{1,193},{65,1},{129,65},{193,129... | collective-permute-start | bytes 983048 | tf_op jit(solution)/shard_map/ppermute | solution.py:509
  42.1 13.1 %collective-permute-start.17 = (s16[48,2560]{1,0:T(8,128)(2,1)S(1)}, s16[48,2560]{1,0:T(8,128)(2,1)S(1)}, u32[]{:S(2)}, u32[]{:S(2)}) collective-permute-start(s16[48,2560]{1,0:T(8,128)(2,1)S(1)} %get-tuple-element.173), channel_id=1, source_target_pairs={{0,192},{64,0},{128,64},{192,128},{1,193},{65,1},{129,65},{193,129... | collective-permute-start | bytes 737288 | tf_op jit(solution)/shard_map/ppermute | solution.py:507
  42.3 12.9 %collective-permute-start.19 = (s16[48,2560]{1,0:T(8,128)(2,1)S(1)}, s16[48,2560]{1,0:T(8,128)(2,1)S(1)}, u32[]{:S(2)}, u32[]{:S(2)}) collective-permute-start(s16[48,2560]{1,0:T(8,128)(2,1)S(1)} %get-tuple-element.175), channel_id=1, source_target_pairs={{0,64},{64,128},{128,192},{192,0},{1,65},{65,129},{129,193},{193,1... | collective-permute-start | bytes 737288 | tf_op jit(solution)/shard_map/ppermute | solution.py:509
  55.2 10.3 %copy-start.10 = (s32[128]{0:T(128)S(1)}, s32[128]{0:T(128)}, u32[]{:S(2)}) copy-start(s32[128]{0:T(128)} %param.13) | copy-start | bytes 1540
  56.9 15.1 %all-to-all-start.3 = ((f32[8,8,128]{2,1,0:T(8,128)}), f32[8,8,128]{2,1,0:T(8,128)S(1)}, u32[]{:S(2)}, u32[]{:S(2)}) async-start(f32[8,8,128]{2,1,0:T(8,128)} %get-tuple-element.178), calls=%async_computation.5 | async-start | bytes 65536 | tf_op jit(solution)/shard_map/all_to_all | solution.py:520
  90.4 7.0 %collective-permute-start.23 = (bf16[32,2432]{1,0:T(8,128)(2,1)S(1)}, bf16[32,2432]{1,0:T(8,128)(2,1)S(1)}, u32[]{:S(2)}, u32[]{:S(2)}) collective-permute-start(bf16[32,2432]{1,0:T(8,128)(2,1)S(1)} %shard_map.81), channel_id=1, source_target_pairs={{0,192},{64,0},{128,64},{192,128},{1,193},{65,1},{129,65},{193,129... | collective-permute-start | bytes 466952 | tf_op jit(solution)/shard_map/ppermute | solution.py:545
  91.5 8.4 %collective-permute-start.22 = (bf16[32,2432]{1,0:T(8,128)(2,1)S(1)}, bf16[32,2432]{1,0:T(8,128)(2,1)S(1)}, u32[]{:S(2)}, u32[]{:S(2)}) collective-permute-start(bf16[32,2432]{1,0:T(8,128)(2,1)S(1)} %shard_map.81), channel_id=1, source_target_pairs={{0,128},{64,192},{128,0},{192,64},{1,129},{65,193},{129,1},{193,65... | collective-permute-start | bytes 466952 | tf_op jit(solution)/shard_map/ppermute | solution.py:545
  93.1 9.1 %collective-permute-start.21 = (bf16[32,2432]{1,0:T(8,128)(2,1)S(1)}, bf16[32,2432]{1,0:T(8,128)(2,1)S(1)}, u32[]{:S(2)}, u32[]{:S(2)}) collective-permute-start(bf16[32,2432]{1,0:T(8,128)(2,1)S(1)} %shard_map.81), channel_id=1, source_target_pairs={{0,64},{64,128},{128,192},{192,0},{1,65},{65,129},{129,193},{193,1... | collective-permute-start | bytes 466952 | tf_op jit(solution)/shard_map/ppermute | solution.py:545
  102.2 2.1 %collective-permute-start.24 = (bf16[128,2432]{1,0:T(8,128)(2,1)S(1)}, bf16[128,2432]{1,0:T(8,128)(2,1)S(1)}, u32[]{:S(2)}, u32[]{:S(2)}) collective-permute-start(bf16[128,2432]{1,0:T(8,128)(2,1)S(1)} %pad_maximum_fusion.1.mine), channel_id=1, source_target_pairs={{0,32},{32,0},{1,33},{33,1},{2,34},{34,2},{3,35},{35,3},{4,36},{36... | collective-permute-start | bytes 1867784 | tf_op jit(solution)/shard_map/ppermute | solution.py:547
  106.1 8.1 %collective-permute-start = (bf16[64,640]{1,0:T(8,128)(2,1)S(1)}, bf16[64,640]{1,0:T(8,128)(2,1)S(1)}, u32[]{:S(2)}, u32[]{:S(2)}) collective-permute-start(bf16[64,640]{1,0:T(8,128)(2,1)S(1)} %get-tuple-element.85), channel_id=1, source_target_pairs={{0,8},{8,16},{16,24},{24,0},{1,9},{9,17},{17,25},{25,1},{2,10},{10... | collective-permute-start | bytes 245768 | tf_op jit(solution)/shard_map/cond/branch_0_fun/ppermute | solution.py:557
  106.7 7.5 %collective-permute-start.1 = (bf16[64,640]{1,0:T(8,128)(2,1)S(1)}, bf16[64,640]{1,0:T(8,128)(2,1)S(1)}, u32[]{:S(2)}, u32[]{:S(2)}) collective-permute-start(bf16[64,640]{1,0:T(8,128)(2,1)S(1)} %get-tuple-element.86), channel_id=1, source_target_pairs={{0,16},{8,24},{16,0},{24,8},{1,17},{9,25},{17,1},{25,9},{2,18},{10... | collective-permute-start | bytes 245768 | tf_op jit(solution)/shard_map/cond/branch_0_fun/ppermute | solution.py:557
  108.6 5.6 %collective-permute-start.2 = (bf16[64,640]{1,0:T(8,128)(2,1)S(1)}, bf16[64,640]{1,0:T(8,128)(2,1)S(1)}, u32[]{:S(2)}, u32[]{:S(2)}) collective-permute-start(bf16[64,640]{1,0:T(8,128)(2,1)S(1)} %get-tuple-element.87), channel_id=1, source_target_pairs={{0,24},{8,0},{16,8},{24,16},{1,25},{9,1},{17,9},{25,17},{2,26},{10... | collective-permute-start | bytes 245768 | tf_op jit(solution)/shard_map/cond/branch_0_fun/ppermute | solution.py:557
  109.6 11.2 %copy-start.4 = (bf16[512,640]{1,0:T(8,128)(2,1)S(1)}, bf16[512,640]{1,0:T(8,128)(2,1)}, u32[]{:S(2)}) copy-start(bf16[512,640]{1,0:T(8,128)(2,1)} %get-tuple-element.81.hid_theirs) | copy-start | bytes 1966084 | tf_op jit(solution)/shard_map/cond
  109.6 11.2 %copy-start.7 = (bf16[512,640]{1,0:T(8,128)(2,1)S(1)}, bf16[512,640]{1,0:T(8,128)(2,1)}, u32[]{:S(2)}) copy-start(bf16[512,640]{1,0:T(8,128)(2,1)} %get-tuple-element.80.hid_mine) | copy-start | bytes 1966084 | tf_op jit(solution)/shard_map/cond
  116.1 13.7 %all-to-all-start = ((s16[8,16,768]{2,1,0:T(8,128)(2,1)}), s16[8,16,768]{2,1,0:T(8,128)(2,1)S(1)}, u32[]{:S(2)}, u32[]{:S(2)}) async-start(s16[8,16,768]{2,1,0:T(8,128)(2,1)} %bitcast), calls=%async_computation | async-start | bytes 393216 | tf_op jit(solution)/shard_map/cond/branch_0_fun/all_to_all | solution.py:568
  (5 other events, 33.4 us)

commit v9 on v6

--- a/solution.py
+++ b/solution.py
@@ -9,7 +9,7 @@
 from jax.sharding import Mesh, PartitionSpec as P
 
 ROUNDS = 24
-LEVELS = 6
+LEVELS = 8
 CAP = 16
 CAP_SMALL = 32
 ORDER = (2, 0, 3, 1)
@@ -68,23 +68,23 @@
 def bisect(entropy, counted, start_high):
     columns = jnp.transpose(entropy)
     quota = jnp.floor((counted + 0.5) * 0.2)
-    lane = lax.broadcasted_iota(jnp.int32, (1, 128), 1)
     leaves = 1 << LEVELS
-    low = jnp.zeros((1, 128), f32)
-    high = jnp.full((1, 128), start_high, f32)
+    lane = lax.broadcasted_iota(jnp.int32, (1, leaves), 1)
+    low = jnp.zeros((1, leaves), f32)
+    high = jnp.full((1, leaves), start_high, f32)
     for _ in range(ROUNDS // LEVELS):
         for level in range(LEVELS):
             middle = (low + high) * 0.5
             bit = ((lane >> (LEVELS - 1 - level)) & 1) == 1
             low, high = jnp.where(bit, middle, low), jnp.where(bit, high, middle)
-        above = jnp.zeros((128, 128), f32)
+        above = jnp.zeros((128, leaves), f32)
         for i in range(8):
             above = above + jnp.where(columns[:, i : i + 1] > low, 1.0, 0.0)
         above = jnp.sum(above, axis=0, keepdims=True)
-        more = jnp.where(((above > quota) | (lane == 0)) & (lane < leaves), 1.0, 0.0)
+        more = jnp.where((above > quota) | (lane == 0), 1.0, 0.0)
         here = lane == jnp.sum(more, axis=1, keepdims=True).astype(jnp.int32) - 1
         low, high = (
-            jnp.broadcast_to(jnp.sum(jnp.where(here, v, 0.0), axis=1, keepdims=True), (1, 128))
+            jnp.broadcast_to(jnp.sum(jnp.where(here, v, 0.0), axis=1, keepdims=True), (1, leaves))
             for v in (low, high)
         )
     return high[:, :1]
@@ -329,12 +329,17 @@
     return lax.rem(at[0] - s + NX, NX) * 2 + lax.rem(at[1] + k, 2)
 
 
-def product_kernel(at, mine, theirs, turned, slopes, o0, o1, o2, o3, held):
+def half_kernel(mine, turned, out):
+    out[...] = jnp.dot(mine[...], turned[...], preferred_element_type=f32).astype(bf16)
+
+
+def product_kernel(at, mine, theirs, turned, first, slopes, o0, o1, o2, o3, held):
     half = mine.shape[0]
     cap = half // NX
     slopes[0:half, :] = mine[...]
     slopes[half:, :] = theirs[...]
-    held[...] = jnp.dot(slopes[...], turned[...], preferred_element_type=f32).astype(bf16)
+    held[0:half, :] = first[...]
+    held[half:, :] = jnp.dot(theirs[...], turned[...], preferred_element_type=f32).astype(bf16)
     for step, out in enumerate((o0, o1, o2, o3)):
         source = lax.rem(at[0] - at[5] - step + 2 * NX, NX) * cap
         for k in range(2):
@@ -403,16 +408,16 @@
         )
         spread.append(part.astype(bf16))
     spread = jnp.concatenate(spread, axis=1)
-    total = jnp.zeros(out.shape, f32)
+    total = jnp.zeros((size, r0.shape[1]), f32)
     for r in (r0, r1, r2, r3):
         total = total + jnp.dot(spread, r[...], preferred_element_type=f32)
-    out[...] = total
+    pack(total, out, slice(0, size))
 
 
 def sum_kernel(at, parts, slot_all, out, ranks):
-    total = parts[0:CAP, :]
+    total = unpack(parts, slice(0, CAP))
     for i in range(1, parts.shape[0] // CAP):
-        total = total + parts[i * CAP : (i + 1) * CAP, :]
+        total = total + unpack(parts, slice(i * CAP, (i + 1) * CAP))
     group = out.shape[0]
     per_owner = 128 // group
     owner, place = at[4] // per_owner, lax.rem(at[4], per_owner)
@@ -508,10 +513,16 @@
         pieces = {s: lax.ppermute(piece, "x", ring(nx, s)) for s in (2, 1, 3)}
         mine = jnp.concatenate([piece, pieces[1], pieces[2], pieces[3]], axis=0)
         theirs = lax.ppermute(mine, "c", SWAP)
+        first = call(
+            half_kernel,
+            struct((nx * cap, rows), bf16),
+            [mine, turned],
+            cost_estimate=estimate(nx * cap, voc_cols, rows),
+        )
         return call(
             product_kernel,
             [struct((2 * nx * cap, voc_cols), bf16)] + [struct((2 * cap, rows), bf16)] * nx,
-            [at, mine, theirs, turned],
+            [at, mine, theirs, turned, first],
             [pltpu.VMEM((2 * nx * cap, rows), bf16)],
             smem=1,
         )
@@ -524,7 +535,7 @@
         head_grad, tick = outer(*sides, 0, early, packed_all, packed_all)
         spread, tick = call(
             spread_kernel,
-            [struct((n_voc * CAP // nx, rows), f32), tick_shape],
+            [struct((n_voc * CAP // nx, rows + 128), jnp.int16), tick_shape],
             [at, tick, *parts, packed_all, slot_all],
             smem=1,
         )

time: 135 us -> 132 us (0.978)
  waiting for transfers between devices: 38.7 us -> 35.1 us
    all_to_all x1, waiting for transfers between devices: 8.19 us -> 5.39 us  [finish(): spread = lax.all_to_all(spread, 'z', 0, 0, tiled=True)]
    pallas_call x13 -> x14, Pallas kernels: 19.9 us -> 20.3 us  [call(): pl.pallas_call(kernel, in_specs=specs, out_shape=out, scratch_shapes=list...]
  transfers between devices with their start and end apart: 19 -> 19, of which waited for: 16 -> 16; matrix products, arithmetic and copies ran while one was open for 0% -> 0% of each run, Pallas kernels for 13% -> 14%
where the time goes in v9:
time: 132 us; the launch traced here: 130 us
  waiting for transfers between devices  35.1 us (27%)
  blocking collectives  27.4 us (21%)
  Pallas kernels  27.1 us (21%)
  starting transfers between devices  25.2 us (19%)
  between operations  14.8 us (11%)
    pallas_call x14, Pallas kernels, call(): pl.pallas_call(kernel, in_specs=specs, out_shape=out, scratch_shapes=list...  20.3 us
    all_to_all x1, blocking collectives, shards(): stats = lax.all_to_all(stats, 'z', 0, 0, tiled=True)  14.9 us
    all_to_all x1, blocking collectives, shards(): stats = lax.all_to_all(stats, everyone, 0, 0, tiled=True)  12.5 us
    ppermute x3, waiting for transfers between devices, backward(): pieces = {s: lax.ppermute(piece, 'x', ring(nx, s)) for s in (2, 1, 3)}  9.02 us
    pallas_call x2, Pallas kernels, outer(): pl.pallas_call(outer_kernel, grid=(count,), in_specs=in_specs, out_specs=...  6.87 us
    ppermute x3, starting transfers between devices, shards(): came = {s: lax.ppermute(leave[s - 1], 'x', ring(nx, s)) for s in (2, 1, 3)}  6.35 us
    all_to_all x1, waiting for transfers between devices, finish(): spread = lax.all_to_all(spread, 'z', 0, 0, tiled=True)  5.39 us
    ppermute x3, waiting for transfers between devices, shards(): came = {s: lax.ppermute(leave[s - 1], 'x', ring(nx, s)) for s in (2, 1, 3)}  4.76 us
  transfers between devices with their start and end apart: 19, of which 16 were waited for; matrix products, arithmetic and copies ran while one was open for 0% of the time, Pallas kernels for 14%

profile of v9, /device:TPU:32, one launch (start us, length us, event | category | flops | bytes accessed | tf_op | source)
XLA Modules:
  0.0 129.8 jit_solution(2278352554773928392)
XLA Ops:
  8.8 3.1 %collective-permute-start.11 = (bf16[128,1280]{1,0:T(8,128)(2,1)S(1)}, bf16[128,1280]{1,0:T(8,128)(2,1)S(1)}, u32[]{:S(2)}, u32[]{:S(2)}) collective-permute-start(bf16[128,1280]{1,0:T(8,128)(2,1)S(1)} %get-tuple-element.156), channel_id=1, source_target_pairs={{0,128},{64,192},{128,0},{192,64},{1,129},{65,193},{129,1},{193,65... | collective-permute-start | bytes 983048 | tf_op jit(solution)/shard_map/ppermute | solution.py:445
  12.5 2.6 %collective-permute-start.13 = (bf16[128,1280]{1,0:T(8,128)(2,1)S(1)}, bf16[128,1280]{1,0:T(8,128)(2,1)S(1)}, u32[]{:S(2)}, u32[]{:S(2)}) collective-permute-start(bf16[128,1280]{1,0:T(8,128)(2,1)S(1)} %get-tuple-element.160), channel_id=1, source_target_pairs={{0,192},{64,0},{128,64},{192,128},{1,193},{65,1},{129,65},{193,129... | collective-permute-start | bytes 983048 | tf_op jit(solution)/shard_map/ppermute | solution.py:445
  15.1 3.3 %shard_map.72 = (f32[128,2432]{1,0:T(8,128)S(1)}, bf16[640,2432]{1,0:T(8,128)(2,1)S(1)}) custom-call(s32[6]{0:T(128)S(1)} %stack.27.at, bf16[128,1280]{1,0:T(8,128)(2,1)S(1)} %get-tuple-element.154.block.b0, bf16[640,2432]{1,0:T(8,128)(2,1)} %head.1, bf16[640,2432]{1,0:T(8,128)(2,1)S(1)} %collective-permute-done.10.other), custom_call_target="tpu_custom_call" | custom-call | flops 796917760 | bytes 6225920 | tf_op jit(solution)/shard_map/pallas_call | solution.py:97
  18.5 2.5 %collective-permute-done.11.block.b2 = bf16[128,1280]{1,0:T(8,128)(2,1)S(1)} collective-permute-done((bf16[128,1280]{1,0:T(8,128)(2,1)S(1)}, bf16[128,1280]{1,0:T(8,128)(2,1)S(1)}, u32[]{:S(2)}, u32[]{:S(2)}) %collective-permute-start.11) | collective-permute-done | bytes 327712 | tf_op jit(solution)/shard_map/ppermute | solution.py:445
  20.9 2.0 %shard_map.73 = (s16[64,2560]{1,0:T(8,128)(2,1)S(1)}, s16[64,2560]{1,0:T(8,128)(2,1)S(1)}, f32[8,128]{1,0:T(8,128)S(1)}) custom-call(s32[6]{0:T(128)S(1)} %stack.27.at, bf16[128,1280]{1,0:T(8,128)(2,1)S(1)} %collective-permute-done.11.block.b2, bf16[640,2432]{1,0:T(8,128)(2,1)S(1)} %get-tuple-element.157.head, ...), custom_call_target="tpu_custom_call" | custom-call | flops 796917760 | bytes 6225920 | tf_op jit(solution)/shard_map/pallas_call | solution.py:97
  22.9 2.8 %collective-permute-start.14 = (s16[64,2560]{1,0:T(8,128)(2,1)S(1)}, s16[64,2560]{1,0:T(8,128)(2,1)S(1)}, u32[]{:S(2)}, u32[]{:S(2)}) collective-permute-start(s16[64,2560]{1,0:T(8,128)(2,1)S(1)} %get-tuple-element.163), channel_id=1, source_target_pairs={{0,192},{64,0},{128,64},{192,128},{1,193},{65,1},{129,65},{193,129... | collective-permute-start | bytes 983048 | tf_op jit(solution)/shard_map/ppermute | solution.py:464
  28.0 3.0 %shard_map.74 = (f32[64,2432]{1,0:T(8,128)S(1)}, f32[64,2432]{1,0:T(8,128)S(1)}, s16[64,2560]{1,0:T(8,128)(2,1)S(1)}, s16[64,2560]{1,0:T(8,128)(2,1)S(1)}, bf16[...) custom-call(s32[6]{0:T(128)S(1)} %stack.27.at, f32[8,128]{1,0:T(8,128)S(1)} %get-tuple-element.158.tick, ...), custom_call_target="tpu_custom_call" | custom-call | flops 1593835520 | bytes 6225920 | tf_op jit(solution)/shard_map/pallas_call | solution.py:97
  31.1 2.4 %collective-permute-start.17 = (s16[64,2560]{1,0:T(8,128)(2,1)S(1)}, s16[64,2560]{1,0:T(8,128)(2,1)S(1)}, u32[]{:S(2)}, u32[]{:S(2)}) collective-permute-start(s16[64,2560]{1,0:T(8,128)(2,1)S(1)} %get-tuple-element.166), channel_id=1, source_target_pairs={{0,192},{64,0},{128,64},{192,128},{1,193},{65,1},{129,65},{193,129... | collective-permute-start | bytes 983048 | tf_op jit(solution)/shard_map/ppermute | solution.py:475
  36.0 2.0 %collective-permute-start.16 = (s16[64,2560]{1,0:T(8,128)(2,1)S(1)}, s16[64,2560]{1,0:T(8,128)(2,1)S(1)}, u32[]{:S(2)}, u32[]{:S(2)}) collective-permute-start(s16[64,2560]{1,0:T(8,128)(2,1)S(1)} %get-tuple-element.165), channel_id=1, source_target_pairs={{0,192},{64,0},{128,64},{192,128},{1,193},{65,1},{129,65},{193,129... | collective-permute-start | bytes 983048 | tf_op jit(solution)/shard_map/ppermute | solution.py:477
  39.1 2.9 %collective-permute-done.17.q1_high = s16[64,2560]{1,0:T(8,128)(2,1)S(1)} collective-permute-done((s16[64,2560]{1,0:T(8,128)(2,1)S(1)}, s16[64,2560]{1,0:T(8,128)(2,1)S(1)}, u32[]{:S(2)}, u32[]{:S(2)}) %collective-permute-start.17) | collective-permute-done | bytes 327712 | tf_op jit(solution)/shard_map/ppermute | solution.py:475
  42.1 3.2 %collective-permute-done.18.q3_low = s16[64,2560]{1,0:T(8,128)(2,1)S(1)} collective-permute-done((s16[64,2560]{1,0:T(8,128)(2,1)S(1)}, s16[64,2560]{1,0:T(8,128)(2,1)S(1)}, u32[]{:S(2)}, u32[]{:S(2)}) %collective-permute-start.18) | collective-permute-done | bytes 327712 | tf_op jit(solution)/shard_map/ppermute | solution.py:475
  45.3 3.4 %collective-permute-done.16.q1_low = s16[64,2560]{1,0:T(8,128)(2,1)S(1)} collective-permute-done((s16[64,2560]{1,0:T(8,128)(2,1)S(1)}, s16[64,2560]{1,0:T(8,128)(2,1)S(1)}, u32[]{:S(2)}, u32[]{:S(2)}) %collective-permute-start.16) | collective-permute-done | bytes 327712 | tf_op jit(solution)/shard_map/ppermute | solution.py:477
  48.7 2.8 %collective-permute-done.19.q3_high = s16[64,2560]{1,0:T(8,128)(2,1)S(1)} collective-permute-done((s16[64,2560]{1,0:T(8,128)(2,1)S(1)}, s16[64,2560]{1,0:T(8,128)(2,1)S(1)}, u32[]{:S(2)}, u32[]{:S(2)}) %collective-permute-start.19) | collective-permute-done | bytes 327712 | tf_op jit(solution)/shard_map/ppermute | solution.py:477
  52.4 14.9 %all_to_all.42.parts = f32[8,8,128]{2,1,0:T(8,128)S(1)} all-to-all(f32[8,8,128]{2,1,0:T(8,128)S(1)} %get-tuple-element.171), channel_id=1, replica_groups=mesh['x'=4,'c'=2,'y'=4,'z'=8] {'z'}, dimensions={0} | all-to-all | bytes 65536 | tf_op jit(solution)/shard_map/all_to_all | solution.py:488
  67.4 12.5 %all_to_all.43.parts = f32[32,8,128]{2,1,0:T(8,128)S(1)} all-to-all(f32[32,8,128]{2,1,0:T(8,128)S(1)} %shard_map.78), channel_id=1, replica_groups=mesh['x'=4,'c'=2,'y'=4,'z'=8] {'x','c','y'}, dimensions={0} | all-to-all | bytes 262144 | tf_op jit(solution)/shard_map/all_to_all | solution.py:495
  79.9 2.0 %shard_map.79 = (f32[8,128]{1,0:T(8,128)S(1)}, f32[8,128]{1,0:T(8,128)S(1)}, f32[8,128]{1,0:T(8,128)S(1)}, f32[8,128]{1,0:T(8,128)S(1)}, s32[1,1]{1,0:T(1,128)}) custom-call(f32[32,8,128]{2,1,0:T(8,128)S(1)} %all_to_all.43.parts), custom_call_target="tpu_custom_call" | custom-call | tf_op jit(solution)/shard_map/pallas_call | solution.py:97
  85.7 4.2 %collective-permute-done.23 = bf16[32,2432]{1,0:T(8,128)(2,1)S(1)} collective-permute-done((bf16[32,2432]{1,0:T(8,128)(2,1)S(1)}, bf16[32,2432]{1,0:T(8,128)(2,1)S(1)}, u32[]{:S(2)}, u32[]{:S(2)}) %collective-permute-start.23) | collective-permute-done | bytes 155680 | tf_op jit(solution)/shard_map/ppermute | solution.py:513
  89.9 2.6 %collective-permute-done.22 = bf16[32,2432]{1,0:T(8,128)(2,1)S(1)} collective-permute-done((bf16[32,2432]{1,0:T(8,128)(2,1)S(1)}, bf16[32,2432]{1,0:T(8,128)(2,1)S(1)}, u32[]{:S(2)}, u32[]{:S(2)}) %collective-permute-start.22) | collective-permute-done | bytes 155680 | tf_op jit(solution)/shard_map/ppermute | solution.py:513
  92.6 2.2 %collective-permute-done.21 = bf16[32,2432]{1,0:T(8,128)(2,1)S(1)} collective-permute-done((bf16[32,2432]{1,0:T(8,128)(2,1)S(1)}, bf16[32,2432]{1,0:T(8,128)(2,1)S(1)}, u32[]{:S(2)}, u32[]{:S(2)}) %collective-permute-start.21) | collective-permute-done | bytes 155680 | tf_op jit(solution)/shard_map/ppermute | solution.py:513
  98.3 24.7 %conditional.1 = (f32[32,640]{1,0:T(8,128)}, f32[640,2432]{1,0:T(8,128)}) conditional(s32[]{:T(128)} %bitcast.17, (s32[6]{0:T(128)S(1)}, f32[8,128]{1,0:T(8,128)S(1)}, bf16[512,640]{1,0:T(8,128)(2,1)S(1)}, bf16[512,640]{1,0:T(8,128)(2,1)S(1)}, bf16[256,2432]{1,0:T(8,128)(2,1)S(1)}, /*index=5*/bf16[64,640]{1,0:T(8,128)(2,1)S(1)}, ...), branch_computations={%region_0.0_spmd, %region_1.0_spmd, %region_2.17_spmd} | conditional | flops 9566442496 | bytes 125846592 | solution.py:564
  101.8 3.8 %branch_0_fun.4 = (f32[640,2432]{1,0:T(8,128)}, f32[8,128]{1,0:T(8,128)S(1)}) custom-call(s32[6]{0:T(128)S(1)} %get-tuple-element.74.at, f32[8,128]{1,0:T(8,128)S(1)} %get-tuple-element.75.packed_all.above.after, bf16[512,640]{1,0:T(8,128)(2,1)S(1)} %get-tuple-element.76.hid_mine, bf16[512,640]{1,0:T(8,128)(2,1)S(1)} %get-tuple-element.77.hid_theirs, ...), custom_call_target="tpu_custom_call" | custom-call | flops 478150656 | bytes 1245184 | tf_op jit(solution)/shard_map/cond/branch_0_fun/pallas_call | solution.py:380
  108.3 4.7 %all-to-all-start = ((s16[8,16,768]{2,1,0:T(8,128)(2,1)}), s16[8,16,768]{2,1,0:T(8,128)(2,1)S(1)}, u32[]{:S(2)}, u32[]{:S(2)}) async-start(s16[8,16,768]{2,1,0:T(8,128)(2,1)} %bitcast), calls=%async_computation | async-start | bytes 393216 | tf_op jit(solution)/shard_map/cond/branch_0_fun/all_to_all | solution.py:542
  113.1 3.1 %branch_0_fun.7 = (f32[640,2432]{1,0:T(8,128)}, f32[8,128]{1,0:T(8,128)}) custom-call(s32[6]{0:T(128)S(1)} %get-tuple-element.74.at, f32[8,128]{1,0:T(8,128)S(1)} %get-tuple-element.75.packed_all.above.after, bf16[512,640]{1,0:T(8,128)(2,1)} %copy-done.2, bf16[512,640]{1,0:T(8,128)(2,1)S(1)} %get-tuple-element.77.hid_theirs, ...), custom_call_target="tpu_custom_call", output_to_operand_aliasing={{0}: (5, {})} | custom-call | flops 318767104 | bytes 1245184 | tf_op jit(solution)/shard_map/cond/branch_0_fun/pallas_call | solution.py:380
  116.1 5.4 %all-to-all-done = s16[8,16,768]{2,1,0:T(8,128)(2,1)S(1)} async-done(((s16[8,16,768]{2,1,0:T(8,128)(2,1)}), s16[8,16,768]{2,1,0:T(8,128)(2,1)S(1)}, u32[]{:S(2)}, u32[]{:S(2)}) %all-to-all-start) | async-done | bytes 196640 | tf_op jit(solution)/shard_map/cond/branch_0_fun/all_to_all | solution.py:542
  (43 shorter events, 23.6 us)
Async XLA Ops:
  7.2 8.0 %collective-permute-start.10 = (bf16[640,2432]{1,0:T(8,128)(2,1)}, bf16[640,2432]{1,0:T(8,128)(2,1)S(1)}, u32[]{:S(2)}, u32[]{:S(2)}) collective-permute-start(bf16[640,2432]{1,0:T(8,128)(2,1)} %head.1), channel_id=1, source_target_pairs={{0,32},{32,0},{1,33},{33,1},{2,34},{34,2},{3,35},{35,3},{4,36},{36... | collective-permute-start | bytes 9338888 | tf_op jit(solution)/shard_map/ppermute | solution.py:441
  8.8 12.1 %collective-permute-start.11 = (bf16[128,1280]{1,0:T(8,128)(2,1)S(1)}, bf16[128,1280]{1,0:T(8,128)(2,1)S(1)}, u32[]{:S(2)}, u32[]{:S(2)}) collective-permute-start(bf16[128,1280]{1,0:T(8,128)(2,1)S(1)} %get-tuple-element.156), channel_id=1, source_target_pairs={{0,128},{64,192},{128,0},{192,64},{1,129},{65,193},{129,1},{193,65... | collective-permute-start | bytes 983048 | tf_op jit(solution)/shard_map/ppermute | solution.py:445
  11.9 15.6 %collective-permute-start.12 = (bf16[128,1280]{1,0:T(8,128)(2,1)S(1)}, bf16[128,1280]{1,0:T(8,128)(2,1)S(1)}, u32[]{:S(2)}, u32[]{:S(2)}) collective-permute-start(bf16[128,1280]{1,0:T(8,128)(2,1)S(1)} %get-tuple-element.159), channel_id=1, source_target_pairs={{0,64},{64,128},{128,192},{192,0},{1,65},{65,129},{129,193},{193,1... | collective-permute-start | bytes 983048 | tf_op jit(solution)/shard_map/ppermute | solution.py:445
  12.5 15.5 %collective-permute-start.13 = (bf16[128,1280]{1,0:T(8,128)(2,1)S(1)}, bf16[128,1280]{1,0:T(8,128)(2,1)S(1)}, u32[]{:S(2)}, u32[]{:S(2)}) collective-permute-start(bf16[128,1280]{1,0:T(8,128)(2,1)S(1)} %get-tuple-element.160), channel_id=1, source_target_pairs={{0,192},{64,0},{128,64},{192,128},{1,193},{65,1},{129,65},{193,129... | collective-permute-start | bytes 983048 | tf_op jit(solution)/shard_map/ppermute | solution.py:445
  22.9 12.2 %collective-permute-start.14 = (s16[64,2560]{1,0:T(8,128)(2,1)S(1)}, s16[64,2560]{1,0:T(8,128)(2,1)S(1)}, u32[]{:S(2)}, u32[]{:S(2)}) collective-permute-start(s16[64,2560]{1,0:T(8,128)(2,1)S(1)} %get-tuple-element.163), channel_id=1, source_target_pairs={{0,192},{64,0},{128,64},{192,128},{1,193},{65,1},{129,65},{193,129... | collective-permute-start | bytes 983048 | tf_op jit(solution)/shard_map/ppermute | solution.py:464
  25.7 9.9 %collective-permute-start.15 = (s16[64,2560]{1,0:T(8,128)(2,1)S(1)}, s16[64,2560]{1,0:T(8,128)(2,1)S(1)}, u32[]{:S(2)}, u32[]{:S(2)}) collective-permute-start(s16[64,2560]{1,0:T(8,128)(2,1)S(1)} %get-tuple-element.164), channel_id=1, source_target_pairs={{0,64},{64,128},{128,192},{192,0},{1,65},{65,129},{129,193},{193,1... | collective-permute-start | bytes 983048 | tf_op jit(solution)/shard_map/ppermute | solution.py:464
  31.0 20.5 %collective-permute-start.20 = (bf16[512,640]{1,0:T(8,128)(2,1)S(1)}, bf16[512,640]{1,0:T(8,128)(2,1)S(1)}, u32[]{:S(2)}, u32[]{:S(2)}) collective-permute-start(bf16[512,640]{1,0:T(8,128)(2,1)S(1)} %get-tuple-element.170), channel_id=1, source_target_pairs={{0,32},{32,0},{1,33},{33,1},{2,34},{34,2},{3,35},{35,3},{4,36},{36... | collective-permute-start | bytes 1966088 | tf_op jit(solution)/shard_map/ppermute | solution.py:479
  31.1 11.0 %collective-permute-start.17 = (s16[64,2560]{1,0:T(8,128)(2,1)S(1)}, s16[64,2560]{1,0:T(8,128)(2,1)S(1)}, u32[]{:S(2)}, u32[]{:S(2)}) collective-permute-start(s16[64,2560]{1,0:T(8,128)(2,1)S(1)} %get-tuple-element.166), channel_id=1, source_target_pairs={{0,192},{64,0},{128,64},{192,128},{1,193},{65,1},{129,65},{193,129... | collective-permute-start | bytes 983048 | tf_op jit(solution)/shard_map/ppermute | solution.py:475
  33.5 11.8 %collective-permute-start.18 = (s16[64,2560]{1,0:T(8,128)(2,1)S(1)}, s16[64,2560]{1,0:T(8,128)(2,1)S(1)}, u32[]{:S(2)}, u32[]{:S(2)}) collective-permute-start(s16[64,2560]{1,0:T(8,128)(2,1)S(1)} %get-tuple-element.167), channel_id=1, source_target_pairs={{0,64},{64,128},{128,192},{192,0},{1,65},{65,129},{129,193},{193,1... | collective-permute-start | bytes 983048 | tf_op jit(solution)/shard_map/ppermute | solution.py:475
  36.0 12.7 %collective-permute-start.16 = (s16[64,2560]{1,0:T(8,128)(2,1)S(1)}, s16[64,2560]{1,0:T(8,128)(2,1)S(1)}, u32[]{:S(2)}, u32[]{:S(2)}) collective-permute-start(s16[64,2560]{1,0:T(8,128)(2,1)S(1)} %get-tuple-element.165), channel_id=1, source_target_pairs={{0,192},{64,0},{128,64},{192,128},{1,193},{65,1},{129,65},{193,129... | collective-permute-start | bytes 983048 | tf_op jit(solution)/shard_map/ppermute | solution.py:477
  37.9 13.6 %collective-permute-start.19 = (s16[64,2560]{1,0:T(8,128)(2,1)S(1)}, s16[64,2560]{1,0:T(8,128)(2,1)S(1)}, u32[]{:S(2)}, u32[]{:S(2)}) collective-permute-start(s16[64,2560]{1,0:T(8,128)(2,1)S(1)} %get-tuple-element.168), channel_id=1, source_target_pairs={{0,64},{64,128},{128,192},{192,0},{1,65},{65,129},{129,193},{193,1... | collective-permute-start | bytes 983048 | tf_op jit(solution)/shard_map/ppermute | solution.py:477
  51.5 15.8 %copy-start.5 = (s32[128]{0:T(128)S(1)}, s32[128]{0:T(128)}, u32[]{:S(2)}) copy-start(s32[128]{0:T(128)} %param.13) | copy-start | bytes 1540
  51.5 15.8 %copy-start.6 = (f32[128]{0:T(128)S(1)}, f32[128]{0:T(128)}, u32[]{:S(2)}) copy-start(f32[128]{0:T(128)} %param.14) | copy-start | bytes 1540
  51.5 30.3 %copy-start.4 = (s32[128]{0:T(128)S(1)}, s32[128]{0:T(128)}, u32[]{:S(2)}) copy-start(s32[128]{0:T(128)} %param.12) | copy-start | bytes 1540
  83.0 6.9 %collective-permute-start.23 = (bf16[32,2432]{1,0:T(8,128)(2,1)S(1)}, bf16[32,2432]{1,0:T(8,128)(2,1)S(1)}, u32[]{:S(2)}, u32[]{:S(2)}) collective-permute-start(bf16[32,2432]{1,0:T(8,128)(2,1)S(1)} %shard_map.80), channel_id=1, source_target_pairs={{0,192},{64,0},{128,64},{192,128},{1,193},{65,1},{129,65},{193,129... | collective-permute-start | bytes 466952 | tf_op jit(solution)/shard_map/ppermute | solution.py:513
  84.2 8.4 %collective-permute-start.22 = (bf16[32,2432]{1,0:T(8,128)(2,1)S(1)}, bf16[32,2432]{1,0:T(8,128)(2,1)S(1)}, u32[]{:S(2)}, u32[]{:S(2)}) collective-permute-start(bf16[32,2432]{1,0:T(8,128)(2,1)S(1)} %shard_map.80), channel_id=1, source_target_pairs={{0,128},{64,192},{128,0},{192,64},{1,129},{65,193},{129,1},{193,65... | collective-permute-start | bytes 466952 | tf_op jit(solution)/shard_map/ppermute | solution.py:513
  85.7 9.1 %collective-permute-start.21 = (bf16[32,2432]{1,0:T(8,128)(2,1)S(1)}, bf16[32,2432]{1,0:T(8,128)(2,1)S(1)}, u32[]{:S(2)}, u32[]{:S(2)}) collective-permute-start(bf16[32,2432]{1,0:T(8,128)(2,1)S(1)} %shard_map.80), channel_id=1, source_target_pairs={{0,64},{64,128},{128,192},{192,0},{1,65},{65,129},{129,193},{193,1... | collective-permute-start | bytes 466952 | tf_op jit(solution)/shard_map/ppermute | solution.py:513
  94.8 2.1 %collective-permute-start.24 = (bf16[128,2432]{1,0:T(8,128)(2,1)S(1)}, bf16[128,2432]{1,0:T(8,128)(2,1)S(1)}, u32[]{:S(2)}, u32[]{:S(2)}) collective-permute-start(bf16[128,2432]{1,0:T(8,128)(2,1)S(1)} %pad_maximum_fusion.1.mine), channel_id=1, source_target_pairs={{0,32},{32,0},{1,33},{33,1},{2,34},{34,2},{3,35},{35,3},{4,36},{36... | collective-permute-start | bytes 1867784 | tf_op jit(solution)/shard_map/ppermute | solution.py:515
  98.3 10.0 %copy-start.2 = (bf16[512,640]{1,0:T(8,128)(2,1)}, bf16[512,640]{1,0:T(8,128)(2,1)S(1)}, u32[]{:S(2)}) copy-start(bf16[512,640]{1,0:T(8,128)(2,1)S(1)} %get-tuple-element.76.hid_mine) | copy-start | bytes 1966084 | tf_op jit(solution)/shard_map/cond
  98.3 7.5 %collective-permute-start = (bf16[64,640]{1,0:T(8,128)(2,1)S(1)}, bf16[64,640]{1,0:T(8,128)(2,1)S(1)}, u32[]{:S(2)}, u32[]{:S(2)}) collective-permute-start(bf16[64,640]{1,0:T(8,128)(2,1)S(1)} %get-tuple-element.81), channel_id=1, source_target_pairs={{0,8},{8,16},{16,24},{24,0},{1,9},{9,17},{17,25},{25,1},{2,10},{10... | collective-permute-start | bytes 245768 | tf_op jit(solution)/shard_map/cond/branch_0_fun/ppermute | solution.py:531
  98.9 6.9 %collective-permute-start.1 = (bf16[64,640]{1,0:T(8,128)(2,1)S(1)}, bf16[64,640]{1,0:T(8,128)(2,1)S(1)}, u32[]{:S(2)}, u32[]{:S(2)}) collective-permute-start(bf16[64,640]{1,0:T(8,128)(2,1)S(1)} %get-tuple-element.82), channel_id=1, source_target_pairs={{0,16},{8,24},{16,0},{24,8},{1,17},{9,25},{17,1},{25,9},{2,18},{10... | collective-permute-start | bytes 245768 | tf_op jit(solution)/shard_map/cond/branch_0_fun/ppermute | solution.py:531
  100.8 5.6 %collective-permute-start.2 = (bf16[64,640]{1,0:T(8,128)(2,1)S(1)}, bf16[64,640]{1,0:T(8,128)(2,1)S(1)}, u32[]{:S(2)}, u32[]{:S(2)}) collective-permute-start(bf16[64,640]{1,0:T(8,128)(2,1)S(1)} %get-tuple-element.83), channel_id=1, source_target_pairs={{0,24},{8,0},{16,8},{24,16},{1,25},{9,1},{17,9},{25,17},{2,26},{10... | collective-permute-start | bytes 245768 | tf_op jit(solution)/shard_map/cond/branch_0_fun/ppermute | solution.py:531
  108.3 13.2 %all-to-all-start = ((s16[8,16,768]{2,1,0:T(8,128)(2,1)}), s16[8,16,768]{2,1,0:T(8,128)(2,1)S(1)}, u32[]{:S(2)}, u32[]{:S(2)}) async-start(s16[8,16,768]{2,1,0:T(8,128)(2,1)} %bitcast), calls=%async_computation | async-start | bytes 393216 | tf_op jit(solution)/shard_map/cond/branch_0_fun/all_to_all | solution.py:542
